TPU v7x, 512 devices: a whole 4x8x8 slice. The times are simulated.
512 devices in a mesh: row: 64 (over y, z), col: 8 (over x, core).
Axes of the slice: x: 4, y: 8, z: 8, core: 2. Of those that a mesh axis runs over, the one named last changes fastest.
Arguments:
- vectors: bfloat16 [65536, 512], P(('row', 'col')), may hold values from -6 to 6
- onsite: float32 [65536], P(('row', 'col')), may hold values from 2.5 to 8
- tile_values: bfloat16 [64, 8, 24, 128, 128], P('row', 'col'), may hold values from -0.21875 to 0.21875
- tile_rows: int32 [64, 8, 24], P('row', 'col'), may hold values from 0 to 7
- tile_cols: int32 [64, 8, 24], P('row', 'col'), may hold values from 0 to 63
- tile_count: int32 [64, 8], P('row', 'col'), may hold values from 1 to 24, as said below
Outputs:
- states: float32 [65536, 512], P(('row', 'col'))
- upper: float32 [512, 512], replicated
Inputs may be any that keep to these rules, and one draw needn't show every extreme that they name: `tile_count`: some device has all 24 slots live in every draw.
All inputs are finite; a program needn't handle non-finite values.
Results may differ from a plain program's by a relative error of at most 0.0003.
Values may be sent and summed in bfloat16 or wider, within the bound.
No kernel may reach another device: no remote copies, remote signals or barrier semaphores. Data moves between devices by JAX's collectives and lax.ppermute only.
A program may use at most 128 MiB of HBM per device.

v0:
```python
import math

import jax
import jax.numpy as jnp
from jax import lax
from jax.sharding import PartitionSpec as P


def matmul_full(left, right):
    return jnp.dot(left, right, precision=lax.Precision.HIGHEST)


def factor_lower(block):
    size = block.shape[0]
    if size == 1:
        root = jnp.sqrt(block)
        return (root, 1.0 / root)
    half = size // 2
    first_lower, first_inverse = factor_lower(block[:half, :half])
    below = matmul_full(block[half:, :half], first_inverse.T)
    rest = block[half:, half:] - matmul_full(below, below.T)
    second_lower, second_inverse = factor_lower(rest)
    corner = -matmul_full(second_inverse, matmul_full(below, first_inverse))
    zeros_top = jnp.zeros((half, size - half), jnp.float32)
    lower = jnp.block([[first_lower, zeros_top], [below, second_lower]])
    inverse = jnp.block([[first_inverse, zeros_top], [corner, second_inverse]])
    return (lower, inverse)


def per_device(vectors, onsite, tile_values, tile_rows, tile_cols, tile_count):
    own_rows = vectors.shape[0]
    kstates = vectors.shape[1]
    width = tile_values.shape[-1]
    slots = tile_values.shape[2]
    ncol = lax.axis_size("col")
    group_rows = own_rows * ncol
    rblocks = group_rows // width
    gathered = lax.all_gather(vectors, "row", axis=0, tiled=True)
    blocks = gathered.reshape(-1, width, kstates)
    tiles = tile_values[0, 0]
    rows_here = tile_rows[0, 0]
    cols_here = tile_cols[0, 0]
    count = tile_count[0, 0]
    group = math.gcd(slots, 16)

    def one_group(step, acc):
        start = step * group
        piece = lax.dynamic_slice_in_dim(tiles, start, group, 0)
        cidx = lax.dynamic_slice_in_dim(cols_here, start, group, 0)
        ridx = lax.dynamic_slice_in_dim(rows_here, start, group, 0)
        picked = jnp.take(blocks, cidx, axis=0)
        prod = jnp.einsum("tij,tjk->tik", piece, picked, preferred_element_type=jnp.float32)
        live = (start + jnp.arange(group) < count).astype(jnp.float32)
        return acc.at[ridx].add(prod * live[:, None, None])

    acc = jnp.zeros((rblocks, width, kstates), jnp.float32)
    acc = lax.fori_loop(0, (count + group - 1) // group, one_group, acc)
    partial_value = acc.reshape(group_rows, kstates)
    offset = lax.axis_index("col") * own_rows
    local = onsite[:, None] * vectors.astype(jnp.float32)
    mine = lax.dynamic_slice_in_dim(partial_value, offset, own_rows, 0) + local
    partial_value = lax.dynamic_update_slice_in_dim(partial_value, mine, offset, 0)
    applied = lax.psum_scatter(partial_value, "col", scatter_dimension=0, tiled=True)
    correlation = jnp.dot(applied.T, applied, precision=lax.Precision.HIGHEST)
    gram = lax.psum(correlation, ("row", "col"))
    lower, lower_inverse = factor_lower(gram)
    upper = lower.T
    inverse = lower_inverse.T
    states = jnp.dot(applied, inverse, precision=lax.Precision.HIGHEST)
    return (states, upper)


def solution(mesh):
    return jax.shard_map(
        per_device,
        mesh=mesh,
        in_specs=(
            P(("row", "col"), None),
            P(("row", "col")),
            P("row", "col", None, None, None),
            P("row", "col", None),
            P("row", "col", None),
            P("row", "col"),
        ),
        out_specs=(P(("row", "col"), None), P()),
        check_vma=False,
    )
```

profile of v0, /device:TPU:1, one launch (start us, length us, event | category | flops | bytes accessed | tf_op | source)
XLA Modules:
  0.0 1384.5 jit_solution(7257845683408481022)
XLA Ops:
  8.6 107.3 %all-gather.2.cloned.1.call-done = bf16[8192,512]{1,0:T(8,128)(2,1)} async-done(((bf16[128,512]{1,0:T(8,128)(2,1)}), bf16[8192,512]{1,0:T(8,128)(2,1)}) %all-gather.2.cloned.1.call-update) | async-done | bytes 8388624 | tf_op jit(solution)/shard_map/all_gather | solution.py:38
  115.9 1.6 broadcast_in_dim.21
  117.5 10.4 while.10
  117.5 0.8 compare_and_fusion.2
  118.3 4.0 gather_fusion
  122.3 1.4 convolution_multiply_fusion.2
  123.8 4.1 scatter_fusion
  128.0 1.8 add_dynamic-update-slice_fusion
  129.8 56.3 %reduce-scatter.2.cloned.1.call-done = f32[128,512]{1,0:T(8,128)} async-done(((f32[1024,512]{1,0:T(8,128)}), f32[128,512]{1,0:T(8,128)}) %reduce-scatter.2.cloned.1.call-update) | async-done | bytes 262160 | tf_op jit(solution)/shard_map/reduce_scatter | solution.py:63
  186.1 3.0 fusion.5141
  189.2 275.9 %all-reduce.512.cloned.1.call-done = f32[512,512]{1,0:T(8,128)} async-done(((f32[512,512]{1,0:T(8,128)}), f32[512,512]{1,0:T(8,128)}) %all-reduce.512.cloned.1.call-update) | async-done | bytes 1048592 | tf_op jit(solution)/shard_map/psum | solution.py:65
  465.0 1.5 fusion.4885
  468.8 0.8 fusion.4433
  469.6 0.8 convolution_subtract_fusion.254
  473.5 0.8 fusion.2897
  474.4 0.8 convolution_subtract_fusion.126
  482.0 0.8 fusion.1935
  482.8 0.8 convolution_subtract_fusion.62
  497.3 0.8 fusion.1195
  498.1 0.8 convolution_subtract_fusion.30
  525.9 0.9 fusion.709
  526.8 0.9 convolution_subtract_fusion.14
  731.9 0.7 fusion.4939
  738.7 0.7 fusion.4993
  807.5 0.7 fusion.4988
  972.5 0.7 fusion.4976
  1034.5 0.7 fusion.4928
  1120.6 0.9 fusion.4965
  1342.0 0.8 fusion.5396
  1368.4 4.1 fusion.49
  1372.6 1.3 copy.268
  1375.9 1.7 fusion.40
  (1917 shorter events, 357.3 us)
Async XLA Ops:
  7.2 110.3 %copy-start.5 = (s32[1,1,24]{2,1,0:T(1,128)S(1)}, s32[1,1,24]{2,1,0:T(1,128)}, u32[]{:S(2)}) copy-start(s32[1,1,24]{2,1,0:T(1,128)} %param.11) | copy-start | bytes 292
  7.2 110.3 %copy-start.3 = (s32[1,1,24]{2,1,0:T(1,128)S(1)}, s32[1,1,24]{2,1,0:T(1,128)}, u32[]{:S(2)}) copy-start(s32[1,1,24]{2,1,0:T(1,128)} %param.12) | copy-start | bytes 292
  7.2 108.7 %all-gather.2.cloned.1.call-start = ((), (), s32[]{:S(2)}) async-start(), calls=%async_computation.1 | async-start | bytes 8519680 | tf_op jit(solution)/shard_map/all_gather | solution.py:38
  7.9 178.2 %reduce-scatter.2.cloned.1.call-start = ((), (), s32[]{:S(2)}) async-start(), calls=%async_computation.2 | async-start | bytes 2359296 | tf_op jit(solution)/shard_map/reduce_scatter | solution.py:63
  117.5 10.5 copy-start.2
  117.5 10.5 copy-start.4
  129.7 335.3 %all-reduce.512.cloned.1.call-start = ((), (), s32[]{:S(2)}) async-start(), calls=%async_computation.3 | async-start | bytes 2097152 | tf_op jit(solution)/shard_map/psum | solution.py:65
  465.0 116.0 %copy-start.1 = (f32[512,512]{1,0:T(8,128)S(1)}, f32[512,512]{1,0:T(8,128)}, u32[]{:S(2)}) copy-start(f32[512,512]{1,0:T(8,128)} %all-reduce.512.cloned.1.call-done) | copy-start | bytes 3145732
  1373.9 2.0 copy-start
Sparse Core Ops, SparseCore 0:
  11.0 104.8 all-gather.1
  129.9 56.2 reduce-scatter.1
  191.8 273.2 all-reduce.511
where the time goes:
time: 1400 us; the launch traced here: 1380 us
  between operations  549 us (39%)
  waiting for transfers between devices  440 us (31%)
  local copies, waits for them, and re-layouts  178 us (13%)
  matrix products  165 us (12%)
  other arithmetic  52.4 us (4%)
    psum x1, waiting for transfers between devices, per_device(): gram = lax.psum(correlation, ('row', 'col'))  276 us
    slice x256, local copies, waits for them, and re-layouts, factor_lower(): first_lower, first_inverse = factor_lower(block[:half, :half])  170 us
    dot_general x1020, matrix products, matmul_full(): return jnp.dot(left, right, precision=lax.Precision.HIGHEST)  159 us
    all_gather x1, waiting for transfers between devices, per_device(): gathered = lax.all_gather(vectors, 'row', axis=0, tiled=True)  107 us
    reduce_scatter x1, waiting for transfers between devices, per_device(): lax.psum_scatter(partial_value, 'col', scatter_dimension=0, tiled=True)  56.3 us
  transfers between devices with their start and end apart: 3, of which 3 were waited for; matrix products, arithmetic and copies ran while one was open for 0% of the time, Pallas kernels for 0%

commit v1 on v0

v1 whole, which is shorter than its diff:
```python
import functools

import jax
import jax.numpy as jnp
from jax import lax
from jax.experimental import pallas as pl
from jax.experimental.pallas import tpu as pltpu
from jax.sharding import Mesh, PartitionSpec as P

FULL = lax.Precision.HIGHEST
STRIP = 8


def dot_full(left, right, left_dim, right_dim):
    dims = (((left_dim,), (right_dim,)), ((), ()))
    return lax.dot_general(left, right, dims, precision=FULL, preferred_element_type=jnp.float32)


def tile_products(kcore_ref, rows_ref, cols_ref, count_ref, tiles_ref, blocks_ref, keep_ref, send_ref, held, sems):
    slots = tiles_ref.shape[0]
    count = count_ref[0]
    kcore = kcore_ref[0]

    def fetch(t):
        return pltpu.make_async_copy(blocks_ref.at[cols_ref[t]], held.at[t], sems.at[t])

    for t in range(slots):
        @pl.when(t < count)
        def _():
            fetch(t).start()

    keep_ref[...] = jnp.zeros_like(keep_ref)
    send_ref[...] = jnp.zeros_like(send_ref)

    @pl.loop(0, count)
    def _(t):
        fetch(t).wait()
        row = rows_ref[t]
        prod = jnp.dot(tiles_ref[t], held[t], preferred_element_type=jnp.float32)
        own = lax.rem(row, 2) == kcore

        @pl.when(own)
        def _():
            keep_ref[row // 2] += prod

        @pl.when(jnp.logical_not(own))
        def _():
            send_ref[row // 2] += prod


def gram_blocks(parts_ref, local_ref, applied_ref, gram_ref):
    width = gram_ref.shape[1]
    applied = local_ref[...]
    for i in range(parts_ref.shape[0]):
        applied = applied + parts_ref[i]
    applied_ref[...] = applied
    nblocks = applied.shape[1] // width
    at = 0
    for j in range(nblocks):
        row = dot_full(applied[:, j * width:(j + 1) * width], applied[:, j * width:], 0, 0)
        for k in range(nblocks - j):
            gram_ref[at] = row[:, k * width:(k + 1) * width]
            at += 1


def factor_diagonal(a_ref, inverse_ref, u_ref, base, n):
    sub = lax.broadcasted_iota(jnp.int32, (STRIP, n), 0)
    lane = lax.broadcasted_iota(jnp.int32, (STRIP, n), 1)
    strips = n // STRIP

    def spread(rows, k):
        return jnp.broadcast_to(rows[k:k + 1, :], (STRIP, n))

    rows_a = [a_ref[STRIP * i:STRIP * (i + 1), :] for i in range(strips)]
    rows_e = [jnp.where(lane == sub + STRIP * i, 1.0, 0.0) for i in range(strips)]
    for s in range(strips):
        first = STRIP * s
        here = slice(first, first + STRIP)
        cols = [jnp.broadcast_to(rows_a[s][:, first + k:first + k + 1], (STRIP, n)) for k in range(STRIP)]
        down_a, down_e = rows_a[s], rows_e[s]
        full_a, full_e = rows_a[s], rows_e[s]
        pivots = None
        for k in range(STRIP):
            pivot = spread(cols[k], k)
            recip = 1.0 / pivot
            ratio = cols[k] * recip
            at = sub == k
            both = jnp.where(at, -recip, ratio)
            below = jnp.where(sub > k, ratio, 0.0)
            for b in range(k + 1, STRIP):
                cols[b] = jnp.where(at, 0.0, cols[b]) - both * spread(cols[b], k)
            row_a, row_e = spread(full_a, k), spread(full_e, k)
            down_a = down_a - below * spread(down_a, k)
            down_e = down_e - below * spread(down_e, k)
            full_a = jnp.where(at, 0.0, full_a) - both * row_a
            full_e = jnp.where(at, 0.0, full_e) - both * row_e
            pivots = pivot if pivots is None else jnp.where(sub >= k, pivot, pivots)
        scale = lax.rsqrt(pivots)
        u_ref[base + first:base + first + STRIP, base:base + n] = jnp.where(lane >= sub + first, down_a * scale, 0.0)
        inverse_ref[here, :] = down_e * scale
        spread_a = [spread(full_a, k) for k in range(STRIP)]
        spread_e = [spread(full_e, k) for k in range(STRIP)]
        for i in range(s + 1, strips):
            next_a, next_e = rows_a[i], rows_e[i]
            for k in range(STRIP):
                c = jnp.broadcast_to(rows_a[i][:, first + k:first + k + 1], (STRIP, n))
                next_a = next_a - c * spread_a[k]
                next_e = next_e - c * spread_e[k]
            rows_a[i], rows_e[i] = next_a, next_e


def factor_and_solve(gram_ref, applied_ref, states_ref, u_ref, work, inverse):
    n = gram_ref.shape[1]
    size = u_ref.shape[0]
    nblocks = size // n
    at = 0
    for j in range(nblocks):
        for k in range(j, nblocks):
            work[n * j:n * (j + 1), n * k:n * (k + 1)] = gram_ref[at]
            at += 1
    states_ref[...] = applied_ref[...]
    u_ref[...] = jnp.zeros_like(u_ref)
    for j in range(nblocks):
        lo, hi = n * j, n * (j + 1)
        factor_diagonal(work.at[lo:hi, lo:hi], inverse, u_ref, lo, n)
        inv = inverse[...]
        solved = dot_full(states_ref[:, lo:hi], inv, 1, 1)
        states_ref[:, lo:hi] = solved
        if hi < size:
            panel = dot_full(inv, work[lo:hi, hi:], 1, 0)
            u_ref[lo:hi, hi:] = panel
            for k in range(j + 1, nblocks):
                a, b = n * k, n * (k + 1)
                work[a:b, a:] -= dot_full(panel[:, a - hi:b - hi], panel[:, a - hi:], 0, 0)
            states_ref[:, hi:] -= dot_full(solved, panel, 1, 0)


def call(body, outs, in_spaces, scratch=(), mib=40):
    return pl.pallas_call(
        body,
        out_shape=outs,
        in_specs=[pl.BlockSpec(memory_space=space) for space in in_spaces],
        out_specs=[pl.BlockSpec(memory_space=pltpu.VMEM) for _ in outs],
        scratch_shapes=list(scratch),
        compiler_params=pltpu.CompilerParams(vmem_limit_bytes=mib * 2**20),
    )


def per_device(vectors, onsite, tile_values, tile_rows, tile_cols, tile_count):
    own_rows, kstates = vectors.shape
    width = tile_values.shape[-1]
    slots = tile_values.shape[2]
    f32 = jnp.float32
    vm, sm, anywhere = pltpu.VMEM, pltpu.SMEM, pl.ANY
    halves = lax.axis_size("x")
    kcore = lax.axis_index("k").astype(jnp.int32).reshape(1)

    gathered = lax.all_gather(vectors, ("y", "z"), axis=0, tiled=True).reshape(-1, width, kstates)
    local = onsite[:, None] * vectors.astype(f32)

    part = jax.ShapeDtypeStruct((halves, width, kstates), f32)
    keep, send = call(
        tile_products,
        [part, part],
        [sm, sm, sm, sm, vm, anywhere],
        [vm((slots, width, kstates), jnp.bfloat16), pltpu.SemaphoreType.DMA((slots,))],
    )(kcore, tile_rows.reshape(slots), tile_cols.reshape(slots), tile_count.reshape(1), tile_values[0, 0], gathered)
    other = lax.ppermute(send, "k", [(0, 1), (1, 0)])
    parts = lax.all_to_all(keep + other, "x", 0, 0, tiled=True)

    nblocks = kstates // width
    upper_blocks = nblocks * (nblocks + 1) // 2
    applied, gram = call(
        gram_blocks,
        [jax.ShapeDtypeStruct((own_rows, kstates), f32), jax.ShapeDtypeStruct((upper_blocks, width, width), f32)],
        [vm, vm],
    )(parts, local)

    ncol = lax.axis_size(("x", "k"))
    nrow = lax.axis_size(("y", "z"))
    piece = lax.all_to_all(gram.reshape(ncol, -1, width), ("x", "k"), 0, 0, tiled=True).sum(0)
    shape = piece.shape
    piece = lax.all_to_all(piece.reshape(nrow, -1), ("y", "z"), 0, 0, tiled=True).sum(0, keepdims=True)
    piece = lax.all_to_all(jnp.tile(piece, (nrow, 1)), ("y", "z"), 0, 0, tiled=True).reshape(shape)
    gram = lax.all_to_all(jnp.tile(piece[None], (ncol, 1, 1)), ("x", "k"), 0, 0, tiled=True)
    gram = gram.reshape(upper_blocks, width, width)

    states, upper = call(
        factor_and_solve,
        [jax.ShapeDtypeStruct((own_rows, kstates), f32), jax.ShapeDtypeStruct((kstates, kstates), f32)],
        [vm, vm],
        [vm((kstates, kstates), f32), vm((width, width), f32)],
    )(gram, applied)
    return (states, upper)


def solution(mesh):
    fine = Mesh(mesh.devices.reshape(8, 8, 4, 2), ("y", "z", "x", "k"))
    row, col = ("y", "z"), ("x", "k")
    return jax.shard_map(
        per_device,
        mesh=fine,
        in_specs=(
            P(row + col, None),
            P(row + col),
            P(row, col, None, None, None),
            P(row, col, None),
            P(row, col, None),
            P(row, col),
        ),
        out_specs=(P(row + col, None), P()),
        check_vma=False,
    )
```

time: 1400 us -> 254 us (0.18); the launches traced: 1380 us -> 254 us
  between operations: 549 us -> 14.8 us
  waiting for transfers between devices: 440 us -> 125 us
  local copies, waits for them, and re-layouts: 178 us -> 6.16 us
  matrix products: 165 us -> 0 us
  blocking collectives: 0 us -> 67.6 us
  other arithmetic: 52.4 us -> 1.63 us
  Pallas kernels: 0 us -> 26.6 us
    psum x1 -> x0, waiting for transfers between devices: 276 us -> none  [per_device(): gram = lax.psum(correlation, ('row', 'col'))]
    slice x256 -> x0, local copies, waits for them, and re-layouts: 170 us -> none  [factor_lower(): first_lower, first_inverse = factor_lower(block[:half, :half])]
    dot_general x1023 -> x0, matrix products: 165 us -> none  [the longest x1020 159 us: matmul_full(): return jnp.dot(left, right, precision=lax.Precision.HIGHEST)]
    all_to_all x0 -> x4, blocking collectives: none -> 67.6 us  [the longest x1 21.2 us: per_device(): lax.all_to_all(piece.reshape(nrow, -1), ('y', 'z'), 0, 0, tiled=True)]
    reduce_scatter x1 -> x0, waiting for transfers between devices: 56.3 us -> none  [per_device(): lax.psum_scatter(partial_value, 'col', scatter_dimension=0, tiled=True)]
    concatenate x509 -> x0, other arithmetic: 41.6 us -> none  [the longest x255 21.1 us: factor_lower(): inverse = jnp.block([[first_inverse, zeros_top], [corner, second_inverse]])]
    pallas_call x0 -> x3, Pallas kernels: none -> 26.6 us  [the longest x1 21.9 us: per_device(): call(factor_and_solve, [jax.ShapeDtypeStruct((own_rows, kstates), f32), j...]
    all_to_all x0 -> x1, waiting for transfers between devices: none -> 14.7 us  [per_device(): parts = lax.all_to_all(keep + other, 'x', 0, 0, tiled=True)]
where the time goes in v1:
time: 254 us
  waiting for transfers between devices  125 us (49%)
  blocking collectives  67.6 us (27%)
  Pallas kernels  26.6 us (10%)
  between operations  14.8 us (6%)
  starting transfers between devices  11.9 us (5%)
  local copies, waits for them, and re-layouts  6.16 us (2%)
    all_gather x1, waiting for transfers between devices, per_device(): lax.all_gather(vectors, ('y', 'z'), axis=0, tiled=True)  107 us
    pallas_call x1, Pallas kernels, per_device(): call(factor_and_solve, [jax.ShapeDtypeStruct((own_rows, kstates), f32), j...  21.9 us
    all_to_all x1, blocking collectives, per_device(): lax.all_to_all(piece.reshape(nrow, -1), ('y', 'z'), 0, 0, tiled=True)  21.2 us
    all_to_all x1, blocking collectives, per_device(): lax.all_to_all(jnp.tile(piece[None], (ncol, 1, 1)), ('x', 'k'), 0, 0, til...  16.7 us
    all_to_all x1, blocking collectives, per_device(): lax.all_to_all(jnp.tile(piece, (nrow, 1)), ('y', 'z'), 0, 0, tiled=True)  15.1 us
    all_to_all x1, waiting for transfers between devices, per_device(): parts = lax.all_to_all(keep + other, 'x', 0, 0, tiled=True)  14.7 us
    all_to_all x1, blocking collectives, per_device(): lax.all_to_all(gram.reshape(ncol, -1, width), ('x', 'k'), 0, 0, tiled=True)  14.6 us
    all_to_all x1, starting transfers between devices, per_device(): parts = lax.all_to_all(keep + other, 'x', 0, 0, tiled=True)  7.79 us
  transfers between devices with their start and end apart: 3, of which 3 were waited for; matrix products, arithmetic and copies ran while one was open for 0% of the time, Pallas kernels for 0%

profile of v1, /device:TPU:1, one launch (start us, length us, event | category | flops | bytes accessed | tf_op | source)
XLA Modules:
  0.0 253.7 jit_solution(4876075903526154565)
XLA Ops:
  7.2 0.0 copy-start.4
  7.2 0.0 copy-start.5
  7.2 0.0 all-gather.2.cloned.1.call-start
  7.2 0.7 all-gather.2.cloned.1.call-update
  8.6 107.3 %all-gather.2.cloned.1.call-done = bf16[8192,512]{1,0:T(8,128)(2,1)} async-done(((bf16[128,512]{1,0:T(8,128)(2,1)}), bf16[8192,512]{1,0:T(8,128)(2,1)}) %all-gather.2.cloned.1.call-update) | async-done | bytes 8388624 | tf_op jit(solution)/shard_map/all_gather | solution.py:158
  115.9 0.0 copy-start
  115.9 3.4 %copy-done = bf16[8192,512]{1,0:T(8,128)(2,1)S(1)} copy-done((bf16[8192,512]{1,0:T(8,128)(2,1)S(1)}, bf16[8192,512]{1,0:T(8,128)(2,1)}, u32[]{:S(2)}) %copy-start) | copy-done | bytes 8388632
  119.3 0.0 copy-start.1
  119.3 1.1 copy-done.1
  120.4 0.0 copy-start.2
  120.4 0.7 copy-done.2
  121.1 0.7 copy-done.3
  121.7 4.0 %shard_map.77 = (f32[4,128,512]{2,1,0:T(8,128)S(1)}, f32[4,128,512]{2,1,0:T(8,128)S(1)}) custom-call(s32[1]{0:T(128)} %bitcast.kcore_ref, s32[24]{0:T(128)S(1)} %bitcast.13, s32[24]{0:T(128)S(1)} %bitcast.14, s32[1]{0:T(128)} %bitcast.8.count_ref, bf16[24,128,128]{2,1,0:T(8,128)(2,1)S(1)} %bitcast.11, bf16[64,128,512]{2,1,0:T(8,128)(2,1)S(1)} %bitcast.9), custom_call_target="tpu_custom_call" | custom-call | tf_op jit(solution)/shard_map/pallas_call | solution.py:162
  125.7 4.1 %collective-permute-start = (f32[4,128,512]{2,1,0:T(8,128)S(1)}, f32[4,128,512]{2,1,0:T(8,128)S(1)}, u32[]{:S(2)}, u32[]{:S(2)}) collective-permute-start(f32[4,128,512]{2,1,0:T(8,128)S(1)} %get-tuple-element.7), channel_id=1, source_target_pairs={{0,1},{1,0},{2,3},{3,2},{4,5},{5,4},{6,7},{7,6},{8,9},{9,8},{10,11... | collective-permute-start | bytes 3145736 | tf_op jit(solution)/shard_map/ppermute | solution.py:168
  129.8 2.3 collective-permute-done
  132.1 1.2 add.3
  133.2 7.8 %all-to-all-start = ((f32[4,128,512]{2,1,0:T(8,128)}), f32[4,128,512]{2,1,0:T(8,128)S(1)}, u32[]{:S(2)}, u32[]{:S(2)}) async-start(f32[4,128,512]{2,1,0:T(8,128)} %add.3), calls=%async_computation | async-start | bytes 2097152 | tf_op jit(solution)/shard_map/all_to_all | solution.py:169
  141.0 0.0 copy-done.4
  141.0 0.0 copy-done.5
  141.0 0.1 convert_multiply_fusion.local_ref
  141.1 14.7 %all-to-all-done.parts_ref = f32[4,128,512]{2,1,0:T(8,128)S(1)} async-done(((f32[4,128,512]{2,1,0:T(8,128)}), f32[4,128,512]{2,1,0:T(8,128)S(1)}, u32[]{:S(2)}, u32[]{:S(2)}) %all-to-all-start) | async-done | bytes 1048608 | tf_op jit(solution)/shard_map/all_to_all | solution.py:169
  155.8 0.8 shard_map.78
  156.6 14.6 %all_to_all.30 = f32[8,160,128]{2,1,0:T(8,128)S(1)} all-to-all(f32[8,160,128]{2,1,0:T(8,128)S(1)} %bitcast.12), channel_id=1, replica_groups=mesh['y'=8,'z'=8,'x'=4,'k'=2] {'x','k'}, dimensions={0} | all-to-all | bytes 1310720 | tf_op jit(solution)/shard_map/all_to_all | solution.py:181
  171.2 0.1 all_to_all.21
  171.4 21.2 %all_to_all.31 = f32[64,1,320]{2,1,0:T(1,128)S(1)} all-to-all(f32[64,1,320]{2,1,0:T(1,128)S(1)} %all_to_all.21), channel_id=1, replica_groups=mesh['y'=8,'z'=8,'x'=4,'k'=2] {'y','z'}, dimensions={0} | all-to-all | bytes 163840 | tf_op jit(solution)/shard_map/all_to_all | solution.py:183
  192.5 0.1 reduce_sum.19
  192.6 0.1 tile.6
  192.7 15.1 %all_to_all.32 = f32[64,1,320]{2,1,0:T(1,128)S(1)} all-to-all(f32[64,1,320]{2,1,0:T(1,128)S(1)} %tile.6), channel_id=1, replica_groups=mesh['y'=8,'z'=8,'x'=4,'k'=2] {'y','z'}, dimensions={0} | all-to-all | bytes 163840 | tf_op jit(solution)/shard_map/all_to_all | solution.py:184
  207.8 0.2 reduce.1
  208.0 0.1 tile.7
  208.2 16.7 %all_to_all.33 = f32[8,160,128]{2,1,0:T(8,128)S(1)} all-to-all(f32[8,160,128]{2,1,0:T(8,128)S(1)} %tile.16), channel_id=1, replica_groups=mesh['y'=8,'z'=8,'x'=4,'k'=2] {'x','k'}, dimensions={0} | all-to-all | bytes 1310720 | tf_op jit(solution)/shard_map/all_to_all | solution.py:185
  224.9 21.9 %shard_map.79 = (f32[128,512]{1,0:T(8,128)}, f32[512,512]{1,0:T(8,128)}) custom-call(f32[10,128,128]{2,1,0:T(8,128)S(1)} %bitcast.10, f32[128,512]{1,0:T(8,128)S(1)} %get-tuple-element.9.applied_ref), custom_call_target="tpu_custom_call" | custom-call | tf_op jit(solution)/shard_map/pallas_call | solution.py:188
  (3 shorter events, 0.1 us)
Async XLA Ops:
  7.2 133.9 %copy-start.4 = (bf16[128,512]{1,0:T(8,128)(2,1)S(1)}, bf16[128,512]{1,0:T(8,128)(2,1)}, u32[]{:S(2)}) copy-start(bf16[128,512]{1,0:T(8,128)(2,1)} %param.6) | copy-start | bytes 393220
  7.2 133.9 %copy-start.5 = (f32[128]{0:T(128)S(1)}, f32[128]{0:T(128)}, u32[]{:S(2)}) copy-start(f32[128]{0:T(128)} %param.7) | copy-start | bytes 1540
  7.2 108.7 %all-gather.2.cloned.1.call-start = ((), (), s32[]{:S(2)}) async-start(), calls=%async_computation.5 | async-start | bytes 8519680 | tf_op jit(solution)/shard_map/all_gather | solution.py:158
  115.9 3.4 %copy-start = (bf16[8192,512]{1,0:T(8,128)(2,1)S(1)}, bf16[8192,512]{1,0:T(8,128)(2,1)}, u32[]{:S(2)}) copy-start(bf16[8192,512]{1,0:T(8,128)(2,1)} %all-gather.2.cloned.1.call-done) | copy-start | bytes 25165828
  119.3 1.1 copy-start.1
  120.4 0.7 copy-start.2
  121.1 0.7 copy-start.3
  125.7 6.4 %collective-permute-start = (f32[4,128,512]{2,1,0:T(8,128)S(1)}, f32[4,128,512]{2,1,0:T(8,128)S(1)}, u32[]{:S(2)}, u32[]{:S(2)}) collective-permute-start(f32[4,128,512]{2,1,0:T(8,128)S(1)} %get-tuple-element.7), channel_id=1, source_target_pairs={{0,1},{1,0},{2,3},{3,2},{4,5},{5,4},{6,7},{7,6},{8,9},{9,8},{10,11... | collective-permute-start | bytes 3145736 | tf_op jit(solution)/shard_map/ppermute | solution.py:168
  133.2 22.6 %all-to-all-start = ((f32[4,128,512]{2,1,0:T(8,128)}), f32[4,128,512]{2,1,0:T(8,128)S(1)}, u32[]{:S(2)}, u32[]{:S(2)}) async-start(f32[4,128,512]{2,1,0:T(8,128)} %add.3), calls=%async_computation | async-start | bytes 2097152 | tf_op jit(solution)/shard_map/all_to_all | solution.py:169
Sparse Core Ops, SparseCore 0:
  11.0 104.8 all-gather.1

commit v2 on v1

--- a/solution.py
+++ b/solution.py
@@ -9,6 +9,7 @@
 
 FULL = lax.Precision.HIGHEST
 STRIP = 8
+GROUP = 3
 
 
 def dot_full(left, right, left_dim, right_dim):
@@ -16,36 +17,44 @@
     return lax.dot_general(left, right, dims, precision=FULL, preferred_element_type=jnp.float32)
 
 
-def tile_products(kcore_ref, rows_ref, cols_ref, count_ref, tiles_ref, blocks_ref, keep_ref, send_ref, held, sems):
+def tile_products(meta_ref, tiles_ref, *refs):
+    *sources, keep_ref, send_ref, sums, tiles, held, tile_sem, sems, out_sems = refs
     slots = tiles_ref.shape[0]
-    count = count_ref[0]
-    kcore = kcore_ref[0]
-
-    def fetch(t):
-        return pltpu.make_async_copy(blocks_ref.at[cols_ref[t]], held.at[t], sems.at[t])
-
-    for t in range(slots):
-        @pl.when(t < count)
-        def _():
-            fetch(t).start()
-
-    keep_ref[...] = jnp.zeros_like(keep_ref)
-    send_ref[...] = jnp.zeros_like(send_ref)
-
-    @pl.loop(0, count)
+    per_core = keep_ref.shape[0]
+    count = meta_ref[3 * slots]
+    steps = (count + GROUP - 1) // GROUP
+
+    fetch_tiles = pltpu.make_async_copy(tiles_ref, tiles, tile_sem)
+    fetch_tiles.start()
+
+    @pl.loop(0, steps * GROUP)
     def _(t):
-        fetch(t).wait()
-        row = rows_ref[t]
-        prod = jnp.dot(tiles_ref[t], held[t], preferred_element_type=jnp.float32)
-        own = lax.rem(row, 2) == kcore
-
-        @pl.when(own)
-        def _():
-            keep_ref[row // 2] += prod
-
-        @pl.when(jnp.logical_not(own))
-        def _():
-            send_ref[row // 2] += prod
+        for at, source in enumerate(sources):
+            @pl.when(meta_ref[slots + t] == at)
+            def _():
+                pltpu.make_async_copy(source.at[meta_ref[2 * slots + t]], held.at[t], sems.at[t]).start()
+
+    sums[...] = jnp.zeros_like(sums)
+    fetch_tiles.wait()
+
+    @pl.loop(0, steps)
+    def _(step):
+        first = step * GROUP
+        prods = []
+        for t in range(GROUP):
+            pltpu.make_async_copy(sources[0].at[0], held.at[first + t], sems.at[first + t]).wait()
+            tile = tiles[first + t]
+            tile = jnp.where(first + t < count, tile, jnp.zeros_like(tile))
+            prods.append(jnp.dot(tile, held[first + t], preferred_element_type=jnp.float32))
+        for t in range(GROUP):
+            sums[meta_ref[first + t]] += prods[t]
+
+    put_keep = pltpu.make_async_copy(sums.at[:per_core], keep_ref, out_sems.at[0])
+    put_send = pltpu.make_async_copy(sums.at[per_core:], send_ref, out_sems.at[1])
+    put_send.start()
+    put_keep.start()
+    put_send.wait()
+    put_keep.wait()
 
 
 def gram_blocks(parts_ref, local_ref, applied_ref, gram_ref):
@@ -135,15 +144,52 @@
             states_ref[:, hi:] -= dot_full(solved, panel, 1, 0)
 
 
-def call(body, outs, in_spaces, scratch=(), mib=40):
+def call(body, outs, in_spaces, scratch=(), out_space=pltpu.VMEM, mib=40):
     return pl.pallas_call(
         body,
         out_shape=outs,
         in_specs=[pl.BlockSpec(memory_space=space) for space in in_spaces],
-        out_specs=[pl.BlockSpec(memory_space=pltpu.VMEM) for _ in outs],
+        out_specs=[pl.BlockSpec(memory_space=out_space) for _ in outs],
         scratch_shapes=list(scratch),
         compiler_params=pltpu.CompilerParams(vmem_limit_bytes=mib * 2**20),
     )
+
+
+def move(value, by_core):
+    ny, nz, nk = (lax.axis_size(axis) for axis in ("y", "z", "k"))
+    pairs = []
+    for y in range(ny):
+        for z in range(nz):
+            for k in range(nk):
+                to_y, to_z = by_core[k](y, z)
+                pairs.append(((y * nz + z) * nk + k, ((to_y % ny) * nz + to_z % nz) * nk + k))
+    return lax.ppermute(value, ("y", "z", "k"), pairs)
+
+
+def gather_states(vectors):
+    held = vectors[None]
+    for bit in (4, 2, 1):
+        other = move(held, [lambda y, z: (y, z ^ bit), lambda y, z: (y ^ bit, z)])
+        held = jnp.concatenate([held, other])
+    up = [lambda y, z: (y + 1, z), lambda y, z: (y, z + 1)]
+    down = [lambda y, z: (y - 1, z), lambda y, z: (y, z - 1)]
+    half = held.shape[0] // 2
+    above, below = [held], [held]
+    for _ in range(3):
+        above.append(move(above[-1], up))
+        below.append(move(below[-1], down))
+    last_above = move(above[-1][:half], up)
+    last_below = move(below[-1][half:], down)
+    return above + [last_above] + below[:0:-1] + [last_below]
+
+
+def where_blocks(cols, y, z, k):
+    from_y, from_z = cols // 8, cols % 8
+    near = jnp.where(k == 0, from_z ^ z, from_y ^ y)
+    far = jnp.where(k == 0, y - from_y, z - from_z) % 8
+    place = near // 4 + near // 2 % 2 * 2 + near % 2 * 4
+    source = jnp.where((far == 4) & (place >= 4), 8, far)
+    return source, jnp.where(far == 4, place % 4, place)
 
 
 def per_device(vectors, onsite, tile_values, tile_rows, tile_cols, tile_count):
@@ -153,18 +199,30 @@
     f32 = jnp.float32
     vm, sm, anywhere = pltpu.VMEM, pltpu.SMEM, pl.ANY
     halves = lax.axis_size("x")
-    kcore = lax.axis_index("k").astype(jnp.int32).reshape(1)
-
-    gathered = lax.all_gather(vectors, ("y", "z"), axis=0, tiled=True).reshape(-1, width, kstates)
+    y, z, k = (lax.axis_index(axis) for axis in ("y", "z", "k"))
+
+    rows = tile_rows.reshape(slots)
+    source, place = where_blocks(tile_cols.reshape(slots), y, z, k)
+    meta = jnp.concatenate([(rows + k) % 2 * halves + rows // 2, source, place, tile_count.reshape(1)])
     local = onsite[:, None] * vectors.astype(f32)
+    buffers = gather_states(vectors)
 
     part = jax.ShapeDtypeStruct((halves, width, kstates), f32)
     keep, send = call(
         tile_products,
         [part, part],
-        [sm, sm, sm, sm, vm, anywhere],
-        [vm((slots, width, kstates), jnp.bfloat16), pltpu.SemaphoreType.DMA((slots,))],
-    )(kcore, tile_rows.reshape(slots), tile_cols.reshape(slots), tile_count.reshape(1), tile_values[0, 0], gathered)
+        [sm, anywhere] + [anywhere] * len(buffers),
+        [
+            vm((2 * halves, width, kstates), f32),
+            vm((slots, width, width), jnp.bfloat16),
+            vm((slots, width, kstates), jnp.bfloat16),
+            pltpu.SemaphoreType.DMA,
+            pltpu.SemaphoreType.DMA((slots,)),
+            pltpu.SemaphoreType.DMA((2,)),
+        ],
+        anywhere,
+        20,
+    )(meta, tile_values[0, 0], *buffers)
     other = lax.ppermute(send, "k", [(0, 1), (1, 0)])
     parts = lax.all_to_all(keep + other, "x", 0, 0, tiled=True)
 

time: 254 us -> 241 us (0.949)
  waiting for transfers between devices: 125 us -> 70.3 us
  starting transfers between devices: 11.9 us -> 62.9 us
  between operations: 14.8 us -> 1.53 us
  blocking collectives: 67.6 us -> 71.4 us
    all_gather x1 -> x0, waiting for transfers between devices: 107 us -> none  [per_device(): lax.all_gather(vectors, ('y', 'z'), axis=0, tiled=True)]
    ppermute x0 -> x11, waiting for transfers between devices: none -> 53.6 us  [move(): return lax.ppermute(value, ('y', 'z', 'k'), pairs)]
    ppermute x0 -> x11, starting transfers between devices: none -> 50.8 us  [move(): return lax.ppermute(value, ('y', 'z', 'k'), pairs)]
    all_to_all x1, blocking collectives: 21.2 us -> 24.7 us  [per_device(): lax.all_to_all(piece.reshape(nrow, -1), ('y', 'z'), 0, 0, tiled=True)]
    unnamed x12 -> x18, local copies, waits for them, and re-layouts: 5.83 us -> 3.74 us
  transfers between devices with their start and end apart: 3 -> 13, of which waited for: 3 -> 12; matrix products, arithmetic and copies ran while one was open for 0% -> 0% of each run, Pallas kernels for 0% -> 0%
where the time goes in v2:
time: 241 us; the launch traced here: 240 us
  blocking collectives  71.4 us (30%)
  waiting for transfers between devices  70.3 us (29%)
  starting transfers between devices  62.9 us (26%)
  Pallas kernels  27.3 us (11%)
  local copies, waits for them, and re-layouts  4.13 us (2%)
  other arithmetic  2.84 us (1%)
    ppermute x11, waiting for transfers between devices, move(): return lax.ppermute(value, ('y', 'z', 'k'), pairs)  53.6 us
    ppermute x11, starting transfers between devices, move(): return lax.ppermute(value, ('y', 'z', 'k'), pairs)  50.8 us
    all_to_all x1, blocking collectives, per_device(): lax.all_to_all(piece.reshape(nrow, -1), ('y', 'z'), 0, 0, tiled=True)  24.7 us
    pallas_call x1, Pallas kernels, per_device(): call(factor_and_solve, [jax.ShapeDtypeStruct((own_rows, kstates), f32), j...  21.9 us
    all_to_all x1, blocking collectives, per_device(): lax.all_to_all(jnp.tile(piece[None], (ncol, 1, 1)), ('x', 'k'), 0, 0, til...  16.7 us
    all_to_all x1, blocking collectives, per_device(): lax.all_to_all(jnp.tile(piece, (nrow, 1)), ('y', 'z'), 0, 0, tiled=True)  15.1 us
    all_to_all x1, blocking collectives, per_device(): lax.all_to_all(gram.reshape(ncol, -1, width), ('x', 'k'), 0, 0, tiled=True)  14.9 us
    all_to_all x1, waiting for transfers between devices, per_device(): parts = lax.all_to_all(keep + other, 'x', 0, 0, tiled=True)  14.4 us
  transfers between devices with their start and end apart: 13, of which 12 were waited for; matrix products, arithmetic and copies ran while one was open for 0% of the time, Pallas kernels for 0%

profile of v2, /device:TPU:1, one launch (start us, length us, event | category | flops | bytes accessed | tf_op | source)
XLA Modules:
  0.0 240.4 jit_solution(8218257022183531841)
XLA Ops:
  0.6 8.4 %collective-permute-start = (bf16[1,128,512]{2,1,0:T(8,128)(2,1)}, bf16[1,128,512]{2,1,0:T(8,128)(2,1)S(1)}, u32[]{:S(2)}, u32[]{:S(2)}) collective-permute-start(bf16[1,128,512]{2,1,0:T(8,128)(2,1)} %bitcast.41), channel_id=1, source_target_pairs={{0,32},{1,257},{8,40},{9,265},{16,48},{17,273},{24,56},{25,281},{3... | collective-permute-start | bytes 393224 | tf_op jit(solution)/shard_map/ppermute | solution.py:166
  9.1 2.7 %collective-permute-done = bf16[1,128,512]{2,1,0:T(8,128)(2,1)S(1)} collective-permute-done((bf16[1,128,512]{2,1,0:T(8,128)(2,1)}, bf16[1,128,512]{2,1,0:T(8,128)(2,1)S(1)}, u32[]{:S(2)}, u32[]{:S(2)}) %collective-permute-start) | collective-permute-done | bytes 131104 | tf_op jit(solution)/shard_map/ppermute | solution.py:166
  12.6 5.4 %collective-permute-start.1 = (bf16[2,128,512]{2,1,0:T(8,128)(2,1)S(1)}, bf16[2,128,512]{2,1,0:T(8,128)(2,1)S(1)}, u32[]{:S(2)}, u32[]{:S(2)}) collective-permute-start(bf16[2,128,512]{2,1,0:T(8,128)(2,1)S(1)} %pad_maximum_fusion.2), channel_id=1, source_target_pairs={{0,16},{1,129},{8,24},{9,137},{16,0},{17,145},{24,8},{25,153},{32,... | collective-permute-start | bytes 786440 | tf_op jit(solution)/shard_map/ppermute | solution.py:166
  18.0 6.3 %collective-permute-done.1 = bf16[2,128,512]{2,1,0:T(8,128)(2,1)S(1)} collective-permute-done((bf16[2,128,512]{2,1,0:T(8,128)(2,1)S(1)}, bf16[2,128,512]{2,1,0:T(8,128)(2,1)S(1)}, u32[]{:S(2)}, u32[]{:S(2)}) %collective-permute-start.1) | collective-permute-done | bytes 262176 | tf_op jit(solution)/shard_map/ppermute | solution.py:166
  24.4 1.9 collective-permute-start.2
  26.3 8.0 %collective-permute-done.2 = bf16[4,128,512]{2,1,0:T(8,128)(2,1)S(1)} collective-permute-done((bf16[4,128,512]{2,1,0:T(8,128)(2,1)S(1)}, bf16[4,128,512]{2,1,0:T(8,128)(2,1)S(1)}, u32[]{:S(2)}, u32[]{:S(2)}) %collective-permute-start.2) | collective-permute-done | bytes 524320 | tf_op jit(solution)/shard_map/ppermute | solution.py:166
  34.4 11.5 %collective-permute-start.7 = (bf16[8,128,512]{2,1,0:T(8,128)(2,1)S(1)}, bf16[8,128,512]{2,1,0:T(8,128)(2,1)S(1)}, u32[]{:S(2)}, u32[]{:S(2)}) collective-permute-start(bf16[8,128,512]{2,1,0:T(8,128)(2,1)S(1)} %pad_maximum_fusion.refs_0_), channel_id=1, source_target_pairs={{0,448},{1,57},{8,456},{9,1},{16,464},{17,9},{24,472},{25,17},{32,... | collective-permute-start | bytes 3145736 | tf_op jit(solution)/shard_map/ppermute | solution.py:166
  45.9 1.9 collective-permute-start.3
  47.8 9.8 %collective-permute-done.7.refs_7_ = bf16[8,128,512]{2,1,0:T(8,128)(2,1)S(1)} collective-permute-done((bf16[8,128,512]{2,1,0:T(8,128)(2,1)S(1)}, bf16[8,128,512]{2,1,0:T(8,128)(2,1)S(1)}, u32[]{:S(2)}, u32[]{:S(2)}) %collective-permute-start.7) | collective-permute-done | bytes 1048608 | tf_op jit(solution)/shard_map/ppermute | solution.py:166
  57.6 5.3 %collective-permute-start.8 = (bf16[8,128,512]{2,1,0:T(8,128)(2,1)S(1)}, bf16[8,128,512]{2,1,0:T(8,128)(2,1)}, u32[]{:S(2)}, u32[]{:S(2)}) collective-permute-start(bf16[8,128,512]{2,1,0:T(8,128)(2,1)S(1)} %collective-permute-done.7.refs_7_), channel_id=1, source_target_pairs={{0,448},{1,57},{8,456},{9,1},{16,464},{17,9},{24,472},{25,17},{32,... | collective-permute-start | bytes 3145736 | tf_op jit(solution)/shard_map/ppermute | solution.py:166
  63.9 1.9 collective-permute-start.4
  66.8 7.9 %collective-permute-done.8.refs_6_ = bf16[8,128,512]{2,1,0:T(8,128)(2,1)} collective-permute-done((bf16[8,128,512]{2,1,0:T(8,128)(2,1)S(1)}, bf16[8,128,512]{2,1,0:T(8,128)(2,1)}, u32[]{:S(2)}, u32[]{:S(2)}) %collective-permute-start.8) | collective-permute-done | bytes 1048608 | tf_op jit(solution)/shard_map/ppermute | solution.py:166
  74.6 5.4 %collective-permute-start.9 = (bf16[8,128,512]{2,1,0:T(8,128)(2,1)}, bf16[8,128,512]{2,1,0:T(8,128)(2,1)S(1)}, u32[]{:S(2)}, u32[]{:S(2)}) collective-permute-start(bf16[8,128,512]{2,1,0:T(8,128)(2,1)} %collective-permute-done.8.refs_6_), channel_id=1, source_target_pairs={{0,448},{1,57},{8,456},{9,1},{16,464},{17,9},{24,472},{25,17},{32,... | collective-permute-start | bytes 3145736 | tf_op jit(solution)/shard_map/ppermute | solution.py:166
  80.0 1.0 collective-permute-done.4.refs_2_
  81.0 1.9 collective-permute-start.5
  83.6 8.5 %collective-permute-done.9.refs_5_ = bf16[8,128,512]{2,1,0:T(8,128)(2,1)S(1)} collective-permute-done((bf16[8,128,512]{2,1,0:T(8,128)(2,1)}, bf16[8,128,512]{2,1,0:T(8,128)(2,1)S(1)}, u32[]{:S(2)}, u32[]{:S(2)}) %collective-permute-start.9) | collective-permute-done | bytes 1048608 | tf_op jit(solution)/shard_map/ppermute | solution.py:166
  92.1 5.2 %collective-permute-start.10 = (bf16[4,128,512]{2,1,0:T(8,128)(2,1)S(1)}, bf16[4,128,512]{2,1,0:T(8,128)(2,1)S(1)}, u32[]{:S(2)}, u32[]{:S(2)}) collective-permute-start(bf16[4,128,512]{2,1,0:T(8,128)(2,1)S(1)} %slice.9), channel_id=1, source_target_pairs={{0,448},{1,57},{8,456},{9,1},{16,464},{17,9},{24,472},{25,17},{32,... | collective-permute-start | bytes 1572872 | tf_op jit(solution)/shard_map/ppermute | solution.py:166
  98.3 1.9 collective-permute-start.6
  101.0 2.4 %collective-permute-done.10.refs_8_ = bf16[4,128,512]{2,1,0:T(8,128)(2,1)S(1)} collective-permute-done((bf16[4,128,512]{2,1,0:T(8,128)(2,1)S(1)}, bf16[4,128,512]{2,1,0:T(8,128)(2,1)S(1)}, u32[]{:S(2)}, u32[]{:S(2)}) %collective-permute-start.10) | collective-permute-done | bytes 524320 | tf_op jit(solution)/shard_map/ppermute | solution.py:166
  103.4 6.3 %collective-permute-done.6.refs_4_ = bf16[4,128,512]{2,1,0:T(8,128)(2,1)S(1)} collective-permute-done((bf16[4,128,512]{2,1,0:T(8,128)(2,1)S(1)}, bf16[4,128,512]{2,1,0:T(8,128)(2,1)S(1)}, u32[]{:S(2)}, u32[]{:S(2)}) %collective-permute-start.6) | collective-permute-done | bytes 524320 | tf_op jit(solution)/shard_map/ppermute | solution.py:166
  109.7 1.1 copy-done.4
  110.9 4.6 %shard_map.77 = (f32[4,128,512]{2,1,0:T(8,128)S(1)}, f32[4,128,512]{2,1,0:T(8,128)S(1)}) custom-call(s32[73]{0:T(128)S(1)} %pad_add_fusion.meta_ref, bf16[24,128,128]{2,1,0:T(8,128)(2,1)S(1)} %bitcast.39, bf16[8,128,512]{2,1,0:T(8,128)(2,1)S(1)} %pad_maximum_fusion.refs_0_, bf16[8,128,512]{2,1,0:T(8,128)(2,1)S(1)} %copy-done.3, ...), custom_call_target="tpu_custom_call" | custom-call | tf_op jit(solution)/shard_map/pallas_call | solution.py:211
  115.5 5.5 %collective-permute-start.11 = (f32[4,128,512]{2,1,0:T(8,128)S(1)}, f32[4,128,512]{2,1,0:T(8,128)S(1)}, u32[]{:S(2)}, u32[]{:S(2)}) collective-permute-start(f32[4,128,512]{2,1,0:T(8,128)S(1)} %get-tuple-element.7), channel_id=1, source_target_pairs={{0,1},{1,0},{2,3},{3,2},{4,5},{5,4},{6,7},{7,6},{8,9},{9,8},{10,11... | collective-permute-start | bytes 3145736 | tf_op jit(solution)/shard_map/ppermute | solution.py:226
  121.0 2.3 collective-permute-done.11
  123.2 1.2 add.59
  124.4 6.7 %all-to-all-start = ((f32[4,128,512]{2,1,0:T(8,128)}), f32[4,128,512]{2,1,0:T(8,128)S(1)}, u32[]{:S(2)}, u32[]{:S(2)}) async-start(f32[4,128,512]{2,1,0:T(8,128)} %add.59), calls=%async_computation | async-start | bytes 2097152 | tf_op jit(solution)/shard_map/all_to_all | solution.py:227
  131.2 14.4 %all-to-all-done.parts_ref = f32[4,128,512]{2,1,0:T(8,128)S(1)} async-done(((f32[4,128,512]{2,1,0:T(8,128)}), f32[4,128,512]{2,1,0:T(8,128)S(1)}, u32[]{:S(2)}, u32[]{:S(2)}) %all-to-all-start) | async-done | bytes 1048608 | tf_op jit(solution)/shard_map/all_to_all | solution.py:227
  146.4 14.9 %all_to_all.30 = f32[8,160,128]{2,1,0:T(8,128)S(1)} all-to-all(f32[8,160,128]{2,1,0:T(8,128)S(1)} %bitcast.40), channel_id=1, replica_groups=mesh['y'=8,'z'=8,'x'=4,'k'=2] {'x','k'}, dimensions={0} | all-to-all | bytes 1310720 | tf_op jit(solution)/shard_map/all_to_all | solution.py:239
  161.4 24.7 %all_to_all.31 = f32[64,1,320]{2,1,0:T(1,128)S(1)} all-to-all(f32[64,1,320]{2,1,0:T(1,128)S(1)} %all_to_all.21), channel_id=1, replica_groups=mesh['y'=8,'z'=8,'x'=4,'k'=2] {'y','z'}, dimensions={0} | all-to-all | bytes 163840 | tf_op jit(solution)/shard_map/all_to_all | solution.py:241
  186.3 15.1 %all_to_all.32 = f32[64,1,320]{2,1,0:T(1,128)S(1)} all-to-all(f32[64,1,320]{2,1,0:T(1,128)S(1)} %tile.6), channel_id=1, replica_groups=mesh['y'=8,'z'=8,'x'=4,'k'=2] {'y','z'}, dimensions={0} | all-to-all | bytes 163840 | tf_op jit(solution)/shard_map/all_to_all | solution.py:242
  201.8 16.7 %all_to_all.33 = f32[8,160,128]{2,1,0:T(8,128)S(1)} all-to-all(f32[8,160,128]{2,1,0:T(8,128)S(1)} %tile.16), channel_id=1, replica_groups=mesh['y'=8,'z'=8,'x'=4,'k'=2] {'x','k'}, dimensions={0} | all-to-all | bytes 1310720 | tf_op jit(solution)/shard_map/all_to_all | solution.py:243
  218.5 21.9 %shard_map.79 = (f32[128,512]{1,0:T(8,128)}, f32[512,512]{1,0:T(8,128)}) custom-call(f32[10,128,128]{2,1,0:T(8,128)S(1)} %bitcast.38, f32[128,512]{1,0:T(8,128)S(1)} %get-tuple-element.9.applied_ref), custom_call_target="tpu_custom_call" | custom-call | tf_op jit(solution)/shard_map/pallas_call | solution.py:246
  (36 shorter events, 6.4 us)
Async XLA Ops:
  0.6 23.7 %copy-start.5 = (bf16[128,512]{1,0:T(8,128)(2,1)S(1)}, bf16[128,512]{1,0:T(8,128)(2,1)}, u32[]{:S(2)}) copy-start(bf16[128,512]{1,0:T(8,128)(2,1)} %param.6) | copy-start | bytes 393220
  0.6 11.1 %collective-permute-start = (bf16[1,128,512]{2,1,0:T(8,128)(2,1)}, bf16[1,128,512]{2,1,0:T(8,128)(2,1)S(1)}, u32[]{:S(2)}, u32[]{:S(2)}) collective-permute-start(bf16[1,128,512]{2,1,0:T(8,128)(2,1)} %bitcast.41), channel_id=1, source_target_pairs={{0,32},{1,257},{8,40},{9,265},{16,48},{17,273},{24,56},{25,281},{3... | collective-permute-start | bytes 393224 | tf_op jit(solution)/shard_map/ppermute | solution.py:166
  12.6 11.7 %collective-permute-start.1 = (bf16[2,128,512]{2,1,0:T(8,128)(2,1)S(1)}, bf16[2,128,512]{2,1,0:T(8,128)(2,1)S(1)}, u32[]{:S(2)}, u32[]{:S(2)}) collective-permute-start(bf16[2,128,512]{2,1,0:T(8,128)(2,1)S(1)} %pad_maximum_fusion.2), channel_id=1, source_target_pairs={{0,16},{1,129},{8,24},{9,137},{16,0},{17,145},{24,8},{25,153},{32,... | collective-permute-start | bytes 786440 | tf_op jit(solution)/shard_map/ppermute | solution.py:166
  24.4 9.9 %collective-permute-start.2 = (bf16[4,128,512]{2,1,0:T(8,128)(2,1)S(1)}, bf16[4,128,512]{2,1,0:T(8,128)(2,1)S(1)}, u32[]{:S(2)}, u32[]{:S(2)}) collective-permute-start(bf16[4,128,512]{2,1,0:T(8,128)(2,1)S(1)} %pad_maximum_fusion.1), channel_id=1, source_target_pairs={{0,8},{1,65},{8,0},{9,73},{16,24},{17,81},{24,16},{25,89},{32,40},... | collective-permute-start | bytes 1572872 | tf_op jit(solution)/shard_map/ppermute | solution.py:166
  34.3 65.9 %copy-start.7 = (s32[1,1,24]{2,1,0:T(1,128)S(1)}, s32[1,1,24]{2,1,0:T(1,128)}, u32[]{:S(2)}) copy-start(s32[1,1,24]{2,1,0:T(1,128)} %param.10) | copy-start | bytes 292
  34.4 23.2 %collective-permute-start.7 = (bf16[8,128,512]{2,1,0:T(8,128)(2,1)S(1)}, bf16[8,128,512]{2,1,0:T(8,128)(2,1)S(1)}, u32[]{:S(2)}, u32[]{:S(2)}) collective-permute-start(bf16[8,128,512]{2,1,0:T(8,128)(2,1)S(1)} %pad_maximum_fusion.refs_0_), channel_id=1, source_target_pairs={{0,448},{1,57},{8,456},{9,1},{16,464},{17,9},{24,472},{25,17},{32,... | collective-permute-start | bytes 3145736 | tf_op jit(solution)/shard_map/ppermute | solution.py:166
  45.9 18.0 %collective-permute-start.3 = (bf16[8,128,512]{2,1,0:T(8,128)(2,1)S(1)}, bf16[8,128,512]{2,1,0:T(8,128)(2,1)S(1)}, u32[]{:S(2)}, u32[]{:S(2)}) collective-permute-start(bf16[8,128,512]{2,1,0:T(8,128)(2,1)S(1)} %pad_maximum_fusion.refs_0_), channel_id=1, source_target_pairs={{0,64},{1,9},{8,72},{9,17},{16,80},{17,25},{24,88},{25,33},{32,96}... | collective-permute-start | bytes 3145736 | tf_op jit(solution)/shard_map/ppermute | solution.py:166
  57.6 17.0 %collective-permute-start.8 = (bf16[8,128,512]{2,1,0:T(8,128)(2,1)S(1)}, bf16[8,128,512]{2,1,0:T(8,128)(2,1)}, u32[]{:S(2)}, u32[]{:S(2)}) collective-permute-start(bf16[8,128,512]{2,1,0:T(8,128)(2,1)S(1)} %collective-permute-done.7.refs_7_), channel_id=1, source_target_pairs={{0,448},{1,57},{8,456},{9,1},{16,464},{17,9},{24,472},{25,17},{32,... | collective-permute-start | bytes 3145736 | tf_op jit(solution)/shard_map/ppermute | solution.py:166
  62.9 1.0 copy-start
  63.9 17.1 %collective-permute-start.4 = (bf16[8,128,512]{2,1,0:T(8,128)(2,1)S(1)}, bf16[8,128,512]{2,1,0:T(8,128)(2,1)}, u32[]{:S(2)}, u32[]{:S(2)}) collective-permute-start(bf16[8,128,512]{2,1,0:T(8,128)(2,1)S(1)} %collective-permute-done.3.refs_1_), channel_id=1, source_target_pairs={{0,64},{1,9},{8,72},{9,17},{16,80},{17,25},{24,88},{25,33},{32,96}... | collective-permute-start | bytes 3145736 | tf_op jit(solution)/shard_map/ppermute | solution.py:166
  65.8 1.0 copy-start.2
  74.6 17.5 %collective-permute-start.9 = (bf16[8,128,512]{2,1,0:T(8,128)(2,1)}, bf16[8,128,512]{2,1,0:T(8,128)(2,1)S(1)}, u32[]{:S(2)}, u32[]{:S(2)}) collective-permute-start(bf16[8,128,512]{2,1,0:T(8,128)(2,1)} %collective-permute-done.8.refs_6_), channel_id=1, source_target_pairs={{0,448},{1,57},{8,456},{9,1},{16,464},{17,9},{24,472},{25,17},{32,... | collective-permute-start | bytes 3145736 | tf_op jit(solution)/shard_map/ppermute | solution.py:166
  81.0 17.2 %collective-permute-start.5 = (bf16[8,128,512]{2,1,0:T(8,128)(2,1)}, bf16[8,128,512]{2,1,0:T(8,128)(2,1)S(1)}, u32[]{:S(2)}, u32[]{:S(2)}) collective-permute-start(bf16[8,128,512]{2,1,0:T(8,128)(2,1)} %collective-permute-done.4.refs_2_), channel_id=1, source_target_pairs={{0,64},{1,9},{8,72},{9,17},{16,80},{17,25},{24,88},{25,33},{32,96}... | collective-permute-start | bytes 3145736 | tf_op jit(solution)/shard_map/ppermute | solution.py:166
  83.6 26.1 %copy-start.1 = (bf16[8,128,512]{2,1,0:T(8,128)(2,1)S(1)}, bf16[8,128,512]{2,1,0:T(8,128)(2,1)}, u32[]{:S(2)}) copy-start(bf16[8,128,512]{2,1,0:T(8,128)(2,1)} %copy-done) | copy-start | bytes 3145732
  83.6 26.1 %copy-start.3 = (bf16[8,128,512]{2,1,0:T(8,128)(2,1)S(1)}, bf16[8,128,512]{2,1,0:T(8,128)(2,1)}, u32[]{:S(2)}) copy-start(bf16[8,128,512]{2,1,0:T(8,128)(2,1)} %copy-done.2) | copy-start | bytes 3145732
  92.1 11.3 %collective-permute-start.10 = (bf16[4,128,512]{2,1,0:T(8,128)(2,1)S(1)}, bf16[4,128,512]{2,1,0:T(8,128)(2,1)S(1)}, u32[]{:S(2)}, u32[]{:S(2)}) collective-permute-start(bf16[4,128,512]{2,1,0:T(8,128)(2,1)S(1)} %slice.9), channel_id=1, source_target_pairs={{0,448},{1,57},{8,456},{9,1},{16,464},{17,9},{24,472},{25,17},{32,... | collective-permute-start | bytes 1572872 | tf_op jit(solution)/shard_map/ppermute | solution.py:166
  98.3 11.4 %collective-permute-start.6 = (bf16[4,128,512]{2,1,0:T(8,128)(2,1)S(1)}, bf16[4,128,512]{2,1,0:T(8,128)(2,1)S(1)}, u32[]{:S(2)}, u32[]{:S(2)}) collective-permute-start(bf16[4,128,512]{2,1,0:T(8,128)(2,1)S(1)} %slice.8), channel_id=1, source_target_pairs={{0,64},{1,9},{8,72},{9,17},{16,80},{17,25},{24,88},{25,33},{32,96}... | collective-permute-start | bytes 1572872 | tf_op jit(solution)/shard_map/ppermute | solution.py:166
  100.3 0.7 copy-start.8
  109.7 1.1 copy-start.4
  115.5 7.7 %collective-permute-start.11 = (f32[4,128,512]{2,1,0:T(8,128)S(1)}, f32[4,128,512]{2,1,0:T(8,128)S(1)}, u32[]{:S(2)}, u32[]{:S(2)}) collective-permute-start(f32[4,128,512]{2,1,0:T(8,128)S(1)} %get-tuple-element.7), channel_id=1, source_target_pairs={{0,1},{1,0},{2,3},{3,2},{4,5},{5,4},{6,7},{7,6},{8,9},{9,8},{10,11... | collective-permute-start | bytes 3145736 | tf_op jit(solution)/shard_map/ppermute | solution.py:226
  124.4 6.7 %copy-start.6 = (f32[128]{0:T(128)S(1)}, f32[128]{0:T(128)}, u32[]{:S(2)}) copy-start(f32[128]{0:T(128)} %param.7) | copy-start | bytes 1540
  124.4 21.2 %all-to-all-start = ((f32[4,128,512]{2,1,0:T(8,128)}), f32[4,128,512]{2,1,0:T(8,128)S(1)}, u32[]{:S(2)}, u32[]{:S(2)}) async-start(f32[4,128,512]{2,1,0:T(8,128)} %add.59), calls=%async_computation | async-start | bytes 2097152 | tf_op jit(solution)/shard_map/all_to_all | solution.py:227

commit v3 on v2

--- a/solution.py
+++ b/solution.py
@@ -155,41 +155,51 @@
     )
 
 
-def move(value, by_core):
-    ny, nz, nk = (lax.axis_size(axis) for axis in ("y", "z", "k"))
+def line_places(ny, nz, nk):
+    lines = []
+    for fixed in range(ny):
+        for k in range(nk):
+            line = []
+            for along in range(nz):
+                y, z = (fixed, along) if k == 0 else (along, fixed)
+                line.append((y * nz + z) * nk + k)
+            lines.append(line)
+    return lines
+
+
+def ring_pairs(ny, nz, nk, step):
     pairs = []
     for y in range(ny):
         for z in range(nz):
             for k in range(nk):
-                to_y, to_z = by_core[k](y, z)
-                pairs.append(((y * nz + z) * nk + k, ((to_y % ny) * nz + to_z % nz) * nk + k))
-    return lax.ppermute(value, ("y", "z", "k"), pairs)
+                to_y, to_z = ((y + step) % ny, z) if k == 0 else (y, (z + step) % nz)
+                pairs.append(((y * nz + z) * nk + k, (to_y * nz + to_z) * nk + k))
+    return pairs
 
 
 def gather_states(vectors):
-    held = vectors[None]
-    for bit in (4, 2, 1):
-        other = move(held, [lambda y, z: (y, z ^ bit), lambda y, z: (y ^ bit, z)])
-        held = jnp.concatenate([held, other])
-    up = [lambda y, z: (y + 1, z), lambda y, z: (y, z + 1)]
-    down = [lambda y, z: (y - 1, z), lambda y, z: (y, z - 1)]
-    half = held.shape[0] // 2
-    above, below = [held], [held]
-    for _ in range(3):
-        above.append(move(above[-1], up))
-        below.append(move(below[-1], down))
-    last_above = move(above[-1][:half], up)
-    last_below = move(below[-1][half:], down)
-    return above + [last_above] + below[:0:-1] + [last_below]
+    axes = ("y", "z", "k")
+    sizes = tuple(lax.axis_size(axis) for axis in axes)
+    copies = jnp.broadcast_to(vectors[None], (sizes[1],) + vectors.shape)
+    line = lax.all_to_all(copies, axes, 0, 0, axis_index_groups=line_places(*sizes), tiled=True)
+    half = line.shape[0] // 2
+    up, down = ring_pairs(*sizes, 1), ring_pairs(*sizes, -1)
+    halves = [line[:half], line[half:]]
+    above, below = [[h] for h in halves], [[h] for h in halves]
+    for step in range(4):
+        for at in (0, 1):
+            if step < 3 or at == 0:
+                above[at].append(lax.ppermute(above[at][-1], axes, up))
+            if step < 3 or at == 1:
+                below[at].append(lax.ppermute(below[at][-1], axes, down))
+    return above[0] + below[0][:0:-1] + above[1] + below[1][:0:-1]
 
 
 def where_blocks(cols, y, z, k):
     from_y, from_z = cols // 8, cols % 8
-    near = jnp.where(k == 0, from_z ^ z, from_y ^ y)
+    near = jnp.where(k == 0, from_z, from_y)
     far = jnp.where(k == 0, y - from_y, z - from_z) % 8
-    place = near // 4 + near // 2 % 2 * 2 + near % 2 * 4
-    source = jnp.where((far == 4) & (place >= 4), 8, far)
-    return source, jnp.where(far == 4, place % 4, place)
+    return near // 4 * 8 + far, near % 4
 
 
 def per_device(vectors, onsite, tile_values, tile_rows, tile_cols, tile_count):
@@ -221,7 +231,7 @@
             pltpu.SemaphoreType.DMA((2,)),
         ],
         anywhere,
-        20,
+        57,
     )(meta, tile_values[0, 0], *buffers)
     other = lax.ppermute(send, "k", [(0, 1), (1, 0)])
     parts = lax.all_to_all(keep + other, "x", 0, 0, tiled=True)

time: 241 us -> 215 us (0.89)
  waiting for transfers between devices: 70.3 us -> 25.6 us
  blocking collectives: 71.4 us -> 88 us
    ppermute x11 -> x14, waiting for transfers between devices: 53.6 us -> 8.42 us  [the longest x7 7.11 us: gather_states(): above[at].append(lax.ppermute(above[at][-1], axes, up))]
    all_to_all x0 -> x1, blocking collectives: none -> 25.2 us  [gather_states(): lax.all_to_all(copies, axes, 0, 0, axis_index_groups=line_places(*sizes),...]
    all_to_all x1, blocking collectives: 24.7 us -> 16.5 us  [per_device(): lax.all_to_all(piece.reshape(nrow, -1), ('y', 'z'), 0, 0, tiled=True)]
    ppermute x1, starting transfers between devices: 5.47 us -> 9.93 us  [per_device(): other = lax.ppermute(send, 'k', [(0, 1), (1, 0)])]
    all_to_all x1, starting transfers between devices: 6.69 us -> 3.65 us  [per_device(): parts = lax.all_to_all(keep + other, 'x', 0, 0, tiled=True)]
    ppermute x11 -> x14, starting transfers between devices: 50.8 us -> 51.6 us  [the longest x7 38.1 us: gather_states(): below[at].append(lax.ppermute(below[at][-1], axes, down))]
  transfers between devices with their start and end apart: 13 -> 16, of which waited for: 12 -> 5; matrix products, arithmetic and copies ran while one was open for 0% -> 0% of each run, Pallas kernels for 0% -> 0%
where the time goes in v3:
time: 215 us; the launch traced here: 214 us
  blocking collectives  88 us (41%)
  starting transfers between devices  65.1 us (30%)
  Pallas kernels  27.1 us (13%)
  waiting for transfers between devices  25.6 us (12%)
  other arithmetic  3.49 us (2%)
  local copies, waits for them, and re-layouts  2.81 us (1%)
    ppermute x7, starting transfers between devices, gather_states(): below[at].append(lax.ppermute(below[at][-1], axes, down))  38.1 us
    all_to_all x1, blocking collectives, gather_states(): lax.all_to_all(copies, axes, 0, 0, axis_index_groups=line_places(*sizes),...  25.2 us
    pallas_call x1, Pallas kernels, per_device(): call(factor_and_solve, [jax.ShapeDtypeStruct((own_rows, kstates), f32), j...  21.9 us
    all_to_all x1, blocking collectives, per_device(): lax.all_to_all(jnp.tile(piece[None], (ncol, 1, 1)), ('x', 'k'), 0, 0, til...  16.7 us
    all_to_all x1, blocking collectives, per_device(): lax.all_to_all(piece.reshape(nrow, -1), ('y', 'z'), 0, 0, tiled=True)  16.5 us
    all_to_all x1, blocking collectives, per_device(): lax.all_to_all(jnp.tile(piece, (nrow, 1)), ('y', 'z'), 0, 0, tiled=True)  15.1 us
    all_to_all x1, waiting for transfers between devices, per_device(): parts = lax.all_to_all(keep + other, 'x', 0, 0, tiled=True)  14.7 us
    all_to_all x1, blocking collectives, per_device(): lax.all_to_all(gram.reshape(ncol, -1, width), ('x', 'k'), 0, 0, tiled=True)  14.5 us
  transfers between devices with their start and end apart: 16, of which 5 were waited for; matrix products, arithmetic and copies ran while one was open for 0% of the time, Pallas kernels for 0%

profile of v3, /device:TPU:1, one launch (start us, length us, event | category | flops | bytes accessed | tf_op | source)
XLA Modules:
  0.0 213.9 jit_solution(18351344922538987241)
XLA Ops:
  0.6 1.0 broadcast_in_dim.2
  1.6 25.2 %all_to_all.35 = bf16[8,128,512]{2,1,0:T(8,128)(2,1)S(1)} all-to-all(bf16[8,128,512]{2,1,0:T(8,128)(2,1)S(1)} %broadcast_in_dim.2), channel_id=1, replica_groups={{0,8,16,24,32,40,48,56},{1,65,129,193,257,321,385,449},{64,72,80,88,96,..., dimensions={0} | all-to-all | bytes 2097152 | tf_op jit(solution)/shard_map/all_to_all | solution.py:184
  26.9 10.7 %collective-permute-start.10 = (bf16[4,128,512]{2,1,0:T(8,128)(2,1)S(1)}, bf16[4,128,512]{2,1,0:T(8,128)(2,1)S(1)}, u32[]{:S(2)}, u32[]{:S(2)}) collective-permute-start(bf16[4,128,512]{2,1,0:T(8,128)(2,1)S(1)} %get-tuple-element.12.refs_8_), channel_id=1, source_target_pairs={{0,448},{1,57},{8,456},{9,1},{16,464},{17,9},{24,472},{25,17},{32,... | collective-permute-start | bytes 1572872 | tf_op jit(solution)/shard_map/ppermute | solution.py:194
  37.6 1.9 collective-permute-start
  39.5 4.6 %collective-permute-start.4 = (bf16[4,128,512]{2,1,0:T(8,128)(2,1)S(1)}, bf16[4,128,512]{2,1,0:T(8,128)(2,1)S(1)}, u32[]{:S(2)}, u32[]{:S(2)}) collective-permute-start(bf16[4,128,512]{2,1,0:T(8,128)(2,1)S(1)} %get-tuple-element.13.refs_0_), channel_id=1, source_target_pairs={{0,448},{1,57},{8,456},{9,1},{16,464},{17,9},{24,472},{25,17},{32,... | collective-permute-start | bytes 1572872 | tf_op jit(solution)/shard_map/ppermute | solution.py:194
  44.1 1.9 collective-permute-start.7
  46.1 4.6 %collective-permute-start.11 = (bf16[4,128,512]{2,1,0:T(8,128)(2,1)S(1)}, bf16[4,128,512]{2,1,0:T(8,128)(2,1)}, u32[]{:S(2)}, u32[]{:S(2)}) collective-permute-start(bf16[4,128,512]{2,1,0:T(8,128)(2,1)S(1)} %collective-permute-done.10.refs_15_), channel_id=1, source_target_pairs={{0,448},{1,57},{8,456},{9,1},{16,464},{17,9},{24,472},{25,17},{32,... | collective-permute-start | bytes 1572872 | tf_op jit(solution)/shard_map/ppermute | solution.py:194
  50.7 1.9 collective-permute-start.1
  52.6 4.6 %collective-permute-start.5 = (bf16[4,128,512]{2,1,0:T(8,128)(2,1)S(1)}, bf16[4,128,512]{2,1,0:T(8,128)(2,1)}, u32[]{:S(2)}, u32[]{:S(2)}) collective-permute-start(bf16[4,128,512]{2,1,0:T(8,128)(2,1)S(1)} %collective-permute-done.4.refs_7_), channel_id=1, source_target_pairs={{0,448},{1,57},{8,456},{9,1},{16,464},{17,9},{24,472},{25,17},{32,... | collective-permute-start | bytes 1572872 | tf_op jit(solution)/shard_map/ppermute | solution.py:194
  57.2 1.9 collective-permute-start.8
  59.2 4.6 %collective-permute-start.12 = (bf16[4,128,512]{2,1,0:T(8,128)(2,1)}, bf16[4,128,512]{2,1,0:T(8,128)(2,1)}, u32[]{:S(2)}, u32[]{:S(2)}) collective-permute-start(bf16[4,128,512]{2,1,0:T(8,128)(2,1)} %collective-permute-done.11.refs_14_), channel_id=1, source_target_pairs={{0,448},{1,57},{8,456},{9,1},{16,464},{17,9},{24,472},{25,17},{32,... | collective-permute-start | bytes 1572872 | tf_op jit(solution)/shard_map/ppermute | solution.py:194
  63.7 1.9 collective-permute-start.2
  66.4 4.6 %collective-permute-start.6 = (bf16[4,128,512]{2,1,0:T(8,128)(2,1)}, bf16[4,128,512]{2,1,0:T(8,128)(2,1)S(1)}, u32[]{:S(2)}, u32[]{:S(2)}) collective-permute-start(bf16[4,128,512]{2,1,0:T(8,128)(2,1)} %collective-permute-done.5.refs_6_), channel_id=1, source_target_pairs={{0,448},{1,57},{8,456},{9,1},{16,464},{17,9},{24,472},{25,17},{32,... | collective-permute-start | bytes 1572872 | tf_op jit(solution)/shard_map/ppermute | solution.py:194
  70.9 1.9 collective-permute-start.9
  72.9 4.6 %collective-permute-start.13 = (bf16[4,128,512]{2,1,0:T(8,128)(2,1)}, bf16[4,128,512]{2,1,0:T(8,128)(2,1)S(1)}, u32[]{:S(2)}, u32[]{:S(2)}) collective-permute-start(bf16[4,128,512]{2,1,0:T(8,128)(2,1)} %collective-permute-done.12.refs_13_), channel_id=1, source_target_pairs={{0,448},{1,57},{8,456},{9,1},{16,464},{17,9},{24,472},{25,17},{32,... | collective-permute-start | bytes 1572872 | tf_op jit(solution)/shard_map/ppermute | solution.py:194
  77.5 1.9 collective-permute-start.3
  80.7 1.9 collective-permute-done.9.refs_11_
  82.6 1.3 collective-permute-done.13.refs_12_
  83.9 5.2 %collective-permute-done.3.refs_4_ = bf16[4,128,512]{2,1,0:T(8,128)(2,1)S(1)} collective-permute-done((bf16[4,128,512]{2,1,0:T(8,128)(2,1)}, bf16[4,128,512]{2,1,0:T(8,128)(2,1)S(1)}, u32[]{:S(2)}, u32[]{:S(2)}) %collective-permute-start.3) | collective-permute-done | bytes 524320 | tf_op jit(solution)/shard_map/ppermute | solution.py:192
  89.2 0.7 copy-done.9
  89.9 4.5 %shard_map.77 = (f32[4,128,512]{2,1,0:T(8,128)}, f32[4,128,512]{2,1,0:T(8,128)}) custom-call(s32[73]{0:T(128)} %pad_add_fusion.meta_ref, bf16[24,128,128]{2,1,0:T(8,128)(2,1)} %bitcast.38, bf16[4,128,512]{2,1,0:T(8,128)(2,1)} %copy-done.1, bf16[4,128,512]{2,1,0:T(8,128)(2,1)} %copy-done.3, bf16[4,128,512]{2,1,0:T(8,128)(2,1)} %collective-permute-done.1.refs_2_, ...), custom_call_target="tpu_custom_call" | custom-call | tf_op jit(solution)/shard_map/pallas_call | solution.py:221
  94.4 9.9 %collective-permute-start.14 = (f32[4,128,512]{2,1,0:T(8,128)}, f32[4,128,512]{2,1,0:T(8,128)S(1)}, u32[]{:S(2)}, u32[]{:S(2)}) collective-permute-start(f32[4,128,512]{2,1,0:T(8,128)} %get-tuple-element.7), channel_id=1, source_target_pairs={{0,1},{1,0},{2,3},{3,2},{4,5},{5,4},{6,7},{7,6},{8,9},{9,8},{10,11... | collective-permute-start | bytes 3145736 | tf_op jit(solution)/shard_map/ppermute | solution.py:236
  104.3 2.5 %collective-permute-done.14 = f32[4,128,512]{2,1,0:T(8,128)S(1)} collective-permute-done((f32[4,128,512]{2,1,0:T(8,128)}, f32[4,128,512]{2,1,0:T(8,128)S(1)}, u32[]{:S(2)}, u32[]{:S(2)}) %collective-permute-start.14) | collective-permute-done | bytes 1048608 | tf_op jit(solution)/shard_map/ppermute | solution.py:236
  106.8 2.4 %add.44 = f32[4,128,512]{2,1,0:T(8,128)} add(f32[4,128,512]{2,1,0:T(8,128)} %get-tuple-element.6, f32[4,128,512]{2,1,0:T(8,128)S(1)} %collective-permute-done.14) | non-fusion elementwise | flops 262144 | bytes 3145728 | tf_op jit(solution)/shard_map/add | solution.py:237
  109.2 3.6 %all-to-all-start.1 = ((f32[4,128,512]{2,1,0:T(8,128)}), f32[4,128,512]{2,1,0:T(8,128)S(1)}, u32[]{:S(2)}, u32[]{:S(2)}) async-start(f32[4,128,512]{2,1,0:T(8,128)} %add.44), calls=%async_computation.1 | async-start | bytes 2097152 | tf_op jit(solution)/shard_map/all_to_all | solution.py:237
  113.0 14.7 %all-to-all-done.1.parts_ref = f32[4,128,512]{2,1,0:T(8,128)S(1)} async-done(((f32[4,128,512]{2,1,0:T(8,128)}), f32[4,128,512]{2,1,0:T(8,128)S(1)}, u32[]{:S(2)}, u32[]{:S(2)}) %all-to-all-start.1) | async-done | bytes 1048608 | tf_op jit(solution)/shard_map/all_to_all | solution.py:237
  127.7 0.8 shard_map.78
  128.5 14.5 %all_to_all.36 = f32[8,160,128]{2,1,0:T(8,128)S(1)} all-to-all(f32[8,160,128]{2,1,0:T(8,128)S(1)} %bitcast.37), channel_id=1, replica_groups=mesh['y'=8,'z'=8,'x'=4,'k'=2] {'x','k'}, dimensions={0} | all-to-all | bytes 1310720 | tf_op jit(solution)/shard_map/all_to_all | solution.py:249
  143.2 16.5 %all_to_all.37 = f32[64,1,320]{2,1,0:T(1,128)S(1)} all-to-all(f32[64,1,320]{2,1,0:T(1,128)S(1)} %all_to_all.25), channel_id=1, replica_groups=mesh['y'=8,'z'=8,'x'=4,'k'=2] {'y','z'}, dimensions={0} | all-to-all | bytes 163840 | tf_op jit(solution)/shard_map/all_to_all | solution.py:251
  159.8 15.1 %all_to_all.38 = f32[64,1,320]{2,1,0:T(1,128)S(1)} all-to-all(f32[64,1,320]{2,1,0:T(1,128)S(1)} %tile.6), channel_id=1, replica_groups=mesh['y'=8,'z'=8,'x'=4,'k'=2] {'y','z'}, dimensions={0} | all-to-all | bytes 163840 | tf_op jit(solution)/shard_map/all_to_all | solution.py:252
  175.3 16.7 %all_to_all.39 = f32[8,160,128]{2,1,0:T(8,128)S(1)} all-to-all(f32[8,160,128]{2,1,0:T(8,128)S(1)} %tile.16), channel_id=1, replica_groups=mesh['y'=8,'z'=8,'x'=4,'k'=2] {'x','k'}, dimensions={0} | all-to-all | bytes 1310720 | tf_op jit(solution)/shard_map/all_to_all | solution.py:253
  192.0 21.9 %shard_map.79 = (f32[128,512]{1,0:T(8,128)}, f32[512,512]{1,0:T(8,128)}) custom-call(f32[10,128,128]{2,1,0:T(8,128)S(1)} %bitcast.36, f32[128,512]{1,0:T(8,128)S(1)} %get-tuple-element.9.applied_ref), custom_call_target="tpu_custom_call" | custom-call | tf_op jit(solution)/shard_map/pallas_call | solution.py:256
  (50 shorter events, 2.2 us)
Async XLA Ops:
  26.9 62.2 %copy-start = (bf16[4,128,512]{2,1,0:T(8,128)(2,1)}, bf16[4,128,512]{2,1,0:T(8,128)(2,1)S(1)}, u32[]{:S(2)}) copy-start(bf16[4,128,512]{2,1,0:T(8,128)(2,1)S(1)} %get-tuple-element.12.refs_8_) | copy-start | bytes 1572868
  26.9 62.2 %copy-start.1 = (bf16[4,128,512]{2,1,0:T(8,128)(2,1)}, bf16[4,128,512]{2,1,0:T(8,128)(2,1)S(1)}, u32[]{:S(2)}) copy-start(bf16[4,128,512]{2,1,0:T(8,128)(2,1)S(1)} %get-tuple-element.13.refs_0_) | copy-start | bytes 1572868
  26.9 19.1 %collective-permute-start.10 = (bf16[4,128,512]{2,1,0:T(8,128)(2,1)S(1)}, bf16[4,128,512]{2,1,0:T(8,128)(2,1)S(1)}, u32[]{:S(2)}, u32[]{:S(2)}) collective-permute-start(bf16[4,128,512]{2,1,0:T(8,128)(2,1)S(1)} %get-tuple-element.12.refs_8_), channel_id=1, source_target_pairs={{0,448},{1,57},{8,456},{9,1},{16,464},{17,9},{24,472},{25,17},{32,... | collective-permute-start | bytes 1572872 | tf_op jit(solution)/shard_map/ppermute | solution.py:194
  37.6 13.0 %collective-permute-start = (bf16[4,128,512]{2,1,0:T(8,128)(2,1)S(1)}, bf16[4,128,512]{2,1,0:T(8,128)(2,1)S(1)}, u32[]{:S(2)}, u32[]{:S(2)}) collective-permute-start(bf16[4,128,512]{2,1,0:T(8,128)(2,1)S(1)} %get-tuple-element.13.refs_0_), channel_id=1, source_target_pairs={{0,64},{1,9},{8,72},{9,17},{16,80},{17,25},{24,88},{25,33},{32,96}... | collective-permute-start | bytes 1572872 | tf_op jit(solution)/shard_map/ppermute | solution.py:192
  39.5 13.1 %collective-permute-start.4 = (bf16[4,128,512]{2,1,0:T(8,128)(2,1)S(1)}, bf16[4,128,512]{2,1,0:T(8,128)(2,1)S(1)}, u32[]{:S(2)}, u32[]{:S(2)}) collective-permute-start(bf16[4,128,512]{2,1,0:T(8,128)(2,1)S(1)} %get-tuple-element.13.refs_0_), channel_id=1, source_target_pairs={{0,448},{1,57},{8,456},{9,1},{16,464},{17,9},{24,472},{25,17},{32,... | collective-permute-start | bytes 1572872 | tf_op jit(solution)/shard_map/ppermute | solution.py:194
  44.1 13.1 %collective-permute-start.7 = (bf16[4,128,512]{2,1,0:T(8,128)(2,1)S(1)}, bf16[4,128,512]{2,1,0:T(8,128)(2,1)S(1)}, u32[]{:S(2)}, u32[]{:S(2)}) collective-permute-start(bf16[4,128,512]{2,1,0:T(8,128)(2,1)S(1)} %get-tuple-element.12.refs_8_), channel_id=1, source_target_pairs={{0,64},{1,9},{8,72},{9,17},{16,80},{17,25},{24,88},{25,33},{32,96}... | collective-permute-start | bytes 1572872 | tf_op jit(solution)/shard_map/ppermute | solution.py:192
  46.0 43.1 %copy-start.2 = (bf16[4,128,512]{2,1,0:T(8,128)(2,1)}, bf16[4,128,512]{2,1,0:T(8,128)(2,1)S(1)}, u32[]{:S(2)}) copy-start(bf16[4,128,512]{2,1,0:T(8,128)(2,1)S(1)} %collective-permute-done.10.refs_15_) | copy-start | bytes 1572868
  46.1 13.1 %collective-permute-start.11 = (bf16[4,128,512]{2,1,0:T(8,128)(2,1)S(1)}, bf16[4,128,512]{2,1,0:T(8,128)(2,1)}, u32[]{:S(2)}, u32[]{:S(2)}) collective-permute-start(bf16[4,128,512]{2,1,0:T(8,128)(2,1)S(1)} %collective-permute-done.10.refs_15_), channel_id=1, source_target_pairs={{0,448},{1,57},{8,456},{9,1},{16,464},{17,9},{24,472},{25,17},{32,... | collective-permute-start | bytes 1572872 | tf_op jit(solution)/shard_map/ppermute | solution.py:194
  50.7 38.5 %copy-start.3 = (bf16[4,128,512]{2,1,0:T(8,128)(2,1)}, bf16[4,128,512]{2,1,0:T(8,128)(2,1)S(1)}, u32[]{:S(2)}) copy-start(bf16[4,128,512]{2,1,0:T(8,128)(2,1)S(1)} %collective-permute-done.refs_1_) | copy-start | bytes 1572868
  50.7 13.1 %collective-permute-start.1 = (bf16[4,128,512]{2,1,0:T(8,128)(2,1)S(1)}, bf16[4,128,512]{2,1,0:T(8,128)(2,1)}, u32[]{:S(2)}, u32[]{:S(2)}) collective-permute-start(bf16[4,128,512]{2,1,0:T(8,128)(2,1)S(1)} %collective-permute-done.refs_1_), channel_id=1, source_target_pairs={{0,64},{1,9},{8,72},{9,17},{16,80},{17,25},{24,88},{25,33},{32,96}... | collective-permute-start | bytes 1572872 | tf_op jit(solution)/shard_map/ppermute | solution.py:192
  52.6 36.5 %copy-start.4 = (bf16[4,128,512]{2,1,0:T(8,128)(2,1)}, bf16[4,128,512]{2,1,0:T(8,128)(2,1)S(1)}, u32[]{:S(2)}) copy-start(bf16[4,128,512]{2,1,0:T(8,128)(2,1)S(1)} %collective-permute-done.4.refs_7_) | copy-start | bytes 1572868
  52.6 13.7 %collective-permute-start.5 = (bf16[4,128,512]{2,1,0:T(8,128)(2,1)S(1)}, bf16[4,128,512]{2,1,0:T(8,128)(2,1)}, u32[]{:S(2)}, u32[]{:S(2)}) collective-permute-start(bf16[4,128,512]{2,1,0:T(8,128)(2,1)S(1)} %collective-permute-done.4.refs_7_), channel_id=1, source_target_pairs={{0,448},{1,57},{8,456},{9,1},{16,464},{17,9},{24,472},{25,17},{32,... | collective-permute-start | bytes 1572872 | tf_op jit(solution)/shard_map/ppermute | solution.py:194
  57.2 31.9 %copy-start.5 = (bf16[4,128,512]{2,1,0:T(8,128)(2,1)}, bf16[4,128,512]{2,1,0:T(8,128)(2,1)S(1)}, u32[]{:S(2)}) copy-start(bf16[4,128,512]{2,1,0:T(8,128)(2,1)S(1)} %collective-permute-done.7.refs_9_) | copy-start | bytes 1572868
  57.2 13.7 %collective-permute-start.8 = (bf16[4,128,512]{2,1,0:T(8,128)(2,1)S(1)}, bf16[4,128,512]{2,1,0:T(8,128)(2,1)}, u32[]{:S(2)}, u32[]{:S(2)}) collective-permute-start(bf16[4,128,512]{2,1,0:T(8,128)(2,1)S(1)} %collective-permute-done.7.refs_9_), channel_id=1, source_target_pairs={{0,64},{1,9},{8,72},{9,17},{16,80},{17,25},{24,88},{25,33},{32,96}... | collective-permute-start | bytes 1572872 | tf_op jit(solution)/shard_map/ppermute | solution.py:192
  59.2 13.7 %collective-permute-start.12 = (bf16[4,128,512]{2,1,0:T(8,128)(2,1)}, bf16[4,128,512]{2,1,0:T(8,128)(2,1)}, u32[]{:S(2)}, u32[]{:S(2)}) collective-permute-start(bf16[4,128,512]{2,1,0:T(8,128)(2,1)} %collective-permute-done.11.refs_14_), channel_id=1, source_target_pairs={{0,448},{1,57},{8,456},{9,1},{16,464},{17,9},{24,472},{25,17},{32,... | collective-permute-start | bytes 1572872 | tf_op jit(solution)/shard_map/ppermute | solution.py:194
  63.7 13.7 %collective-permute-start.2 = (bf16[4,128,512]{2,1,0:T(8,128)(2,1)}, bf16[4,128,512]{2,1,0:T(8,128)(2,1)}, u32[]{:S(2)}, u32[]{:S(2)}) collective-permute-start(bf16[4,128,512]{2,1,0:T(8,128)(2,1)} %collective-permute-done.1.refs_2_), channel_id=1, source_target_pairs={{0,64},{1,9},{8,72},{9,17},{16,80},{17,25},{24,88},{25,33},{32,96}... | collective-permute-start | bytes 1572872 | tf_op jit(solution)/shard_map/ppermute | solution.py:192
  66.3 13.1 %copy-start.11 = (s32[1,1,24]{2,1,0:T(1,128)S(1)}, s32[1,1,24]{2,1,0:T(1,128)}, u32[]{:S(2)}) copy-start(s32[1,1,24]{2,1,0:T(1,128)} %param.10) | copy-start | bytes 292
  66.4 14.4 %collective-permute-start.6 = (bf16[4,128,512]{2,1,0:T(8,128)(2,1)}, bf16[4,128,512]{2,1,0:T(8,128)(2,1)S(1)}, u32[]{:S(2)}, u32[]{:S(2)}) collective-permute-start(bf16[4,128,512]{2,1,0:T(8,128)(2,1)} %collective-permute-done.5.refs_6_), channel_id=1, source_target_pairs={{0,448},{1,57},{8,456},{9,1},{16,464},{17,9},{24,472},{25,17},{32,... | collective-permute-start | bytes 1572872 | tf_op jit(solution)/shard_map/ppermute | solution.py:194
  70.9 11.6 %collective-permute-start.9 = (bf16[4,128,512]{2,1,0:T(8,128)(2,1)}, bf16[4,128,512]{2,1,0:T(8,128)(2,1)S(1)}, u32[]{:S(2)}, u32[]{:S(2)}) collective-permute-start(bf16[4,128,512]{2,1,0:T(8,128)(2,1)} %collective-permute-done.8.refs_10_), channel_id=1, source_target_pairs={{0,64},{1,9},{8,72},{9,17},{16,80},{17,25},{24,88},{25,33},{32,96}... | collective-permute-start | bytes 1572872 | tf_op jit(solution)/shard_map/ppermute | solution.py:192
  72.9 11.0 %collective-permute-start.13 = (bf16[4,128,512]{2,1,0:T(8,128)(2,1)}, bf16[4,128,512]{2,1,0:T(8,128)(2,1)S(1)}, u32[]{:S(2)}, u32[]{:S(2)}) collective-permute-start(bf16[4,128,512]{2,1,0:T(8,128)(2,1)} %collective-permute-done.12.refs_13_), channel_id=1, source_target_pairs={{0,448},{1,57},{8,456},{9,1},{16,464},{17,9},{24,472},{25,17},{32,... | collective-permute-start | bytes 1572872 | tf_op jit(solution)/shard_map/ppermute | solution.py:194
  77.5 11.6 %collective-permute-start.3 = (bf16[4,128,512]{2,1,0:T(8,128)(2,1)}, bf16[4,128,512]{2,1,0:T(8,128)(2,1)S(1)}, u32[]{:S(2)}, u32[]{:S(2)}) collective-permute-start(bf16[4,128,512]{2,1,0:T(8,128)(2,1)} %collective-permute-done.2.refs_3_), channel_id=1, source_target_pairs={{0,64},{1,9},{8,72},{9,17},{16,80},{17,25},{24,88},{25,33},{32,96}... | collective-permute-start | bytes 1572872 | tf_op jit(solution)/shard_map/ppermute | solution.py:192
  79.4 0.7 copy-start.13
  80.7 8.4 %copy-start.6 = (bf16[4,128,512]{2,1,0:T(8,128)(2,1)}, bf16[4,128,512]{2,1,0:T(8,128)(2,1)S(1)}, u32[]{:S(2)}) copy-start(bf16[4,128,512]{2,1,0:T(8,128)(2,1)S(1)} %collective-permute-done.6.refs_5_) | copy-start | bytes 1572868
  82.6 6.6 %copy-start.7 = (bf16[4,128,512]{2,1,0:T(8,128)(2,1)}, bf16[4,128,512]{2,1,0:T(8,128)(2,1)S(1)}, u32[]{:S(2)}) copy-start(bf16[4,128,512]{2,1,0:T(8,128)(2,1)S(1)} %collective-permute-done.9.refs_11_) | copy-start | bytes 1572868
  83.9 5.3 %copy-start.8 = (bf16[4,128,512]{2,1,0:T(8,128)(2,1)}, bf16[4,128,512]{2,1,0:T(8,128)(2,1)S(1)}, u32[]{:S(2)}) copy-start(bf16[4,128,512]{2,1,0:T(8,128)(2,1)S(1)} %collective-permute-done.13.refs_12_) | copy-start | bytes 1572868
  89.1 0.8 copy-start.9
  94.4 12.4 %collective-permute-start.14 = (f32[4,128,512]{2,1,0:T(8,128)}, f32[4,128,512]{2,1,0:T(8,128)S(1)}, u32[]{:S(2)}, u32[]{:S(2)}) collective-permute-start(f32[4,128,512]{2,1,0:T(8,128)} %get-tuple-element.7), channel_id=1, source_target_pairs={{0,1},{1,0},{2,3},{3,2},{4,5},{5,4},{6,7},{7,6},{8,9},{9,8},{10,11... | collective-permute-start | bytes 3145736 | tf_op jit(solution)/shard_map/ppermute | solution.py:236
  109.2 3.7 %copy-start.10 = (bf16[128,512]{1,0:T(8,128)(2,1)S(1)}, bf16[128,512]{1,0:T(8,128)(2,1)}, u32[]{:S(2)}) copy-start(bf16[128,512]{1,0:T(8,128)(2,1)} %param.6) | copy-start | bytes 393220
  109.2 3.7 %copy-start.12 = (f32[128]{0:T(128)S(1)}, f32[128]{0:T(128)}, u32[]{:S(2)}) copy-start(f32[128]{0:T(128)} %param.7) | copy-start | bytes 1540
  109.2 18.5 %all-to-all-start.1 = ((f32[4,128,512]{2,1,0:T(8,128)}), f32[4,128,512]{2,1,0:T(8,128)S(1)}, u32[]{:S(2)}, u32[]{:S(2)}) async-start(f32[4,128,512]{2,1,0:T(8,128)} %add.44), calls=%async_computation.1 | async-start | bytes 2097152 | tf_op jit(solution)/shard_map/all_to_all | solution.py:237

commit v4 on v3

--- a/solution.py
+++ b/solution.py
@@ -57,19 +57,26 @@
     put_keep.wait()
 
 
-def gram_blocks(parts_ref, local_ref, applied_ref, gram_ref):
-    width = gram_ref.shape[1]
+def upper_pairs(nblocks):
+    pairs = [(j, k) for j in range(nblocks) for k in range(j, nblocks)]
+    return pairs[:len(pairs) // 2], pairs[len(pairs) // 2:]
+
+
+def gram_blocks(core_ref, parts_ref, local_ref, applied_ref, own_ref, other_ref):
+    n = own_ref.shape[1]
     applied = local_ref[...]
     for i in range(parts_ref.shape[0]):
         applied = applied + parts_ref[i]
     applied_ref[...] = applied
-    nblocks = applied.shape[1] // width
-    at = 0
-    for j in range(nblocks):
-        row = dot_full(applied[:, j * width:(j + 1) * width], applied[:, j * width:], 0, 0)
-        for k in range(nblocks - j):
-            gram_ref[at] = row[:, k * width:(k + 1) * width]
-            at += 1
+    nblocks = applied.shape[1] // n
+    rows = [dot_full(applied[:, j * n:(j + 1) * n], applied[:, j * n:], 0, 0) for j in range(nblocks)]
+    for core in (0, 1):
+        @pl.when(core_ref[0] == core)
+        def _():
+            for half, pairs in enumerate(upper_pairs(nblocks)):
+                target = own_ref if half == core else other_ref
+                for at, (j, k) in enumerate(pairs):
+                    target[at] = rows[j][:, (k - j) * n:(k - j + 1) * n]
 
 
 def factor_diagonal(a_ref, inverse_ref, u_ref, base, n):
@@ -118,15 +125,17 @@
             rows_a[i], rows_e[i] = next_a, next_e
 
 
-def factor_and_solve(gram_ref, applied_ref, states_ref, u_ref, work, inverse):
-    n = gram_ref.shape[1]
+def factor_and_solve(core_ref, own_ref, other_ref, applied_ref, states_ref, u_ref, work, inverse):
+    n = own_ref.shape[1]
     size = u_ref.shape[0]
     nblocks = size // n
-    at = 0
-    for j in range(nblocks):
-        for k in range(j, nblocks):
-            work[n * j:n * (j + 1), n * k:n * (k + 1)] = gram_ref[at]
-            at += 1
+    for core in (0, 1):
+        @pl.when(core_ref[0] == core)
+        def _():
+            for half, pairs in enumerate(upper_pairs(nblocks)):
+                source = own_ref if half == core else other_ref
+                for at, (j, k) in enumerate(pairs):
+                    work[n * j:n * (j + 1), n * k:n * (k + 1)] = source[at]
     states_ref[...] = applied_ref[...]
     u_ref[...] = jnp.zeros_like(u_ref)
     for j in range(nblocks):
@@ -200,6 +209,44 @@
     near = jnp.where(k == 0, from_z, from_y)
     far = jnp.where(k == 0, y - from_y, z - from_z) % 8
     return near // 4 * 8 + far, near % 4
+
+
+def sum_groups(ny, nz, nx, nk):
+    def device(y, z, x, k):
+        return ((y * nz + z) * nx + x) * nk + k
+
+    four, same = [], []
+    for y in range(ny):
+        for z in range(nz):
+            four.append([device(y, z, x, 0) for x in range(nx)])
+    for x in range(nx):
+        same.append([device(y, z, x, 0) for y in range(ny) for z in range(nz)])
+        for y in range(0, ny, 2):
+            for z in range(0, nz, 2):
+                four.append([device(y + i, z + j, x, 1) for i in (0, 1) for j in (0, 1)])
+    for i in (0, 1):
+        for j in (0, 1):
+            same.append([
+                device(y + i, z + j, x, 1)
+                for x in range(nx) for y in range(0, ny, 2) for z in range(0, nz, 2)
+            ])
+    return four, same
+
+
+def sum_halves(value):
+    axes = ("y", "z", "x", "k")
+    four, same = sum_groups(*(lax.axis_size(axis) for axis in axes))
+
+    def exchange(pieces, groups):
+        return lax.all_to_all(pieces, axes, 0, 0, axis_index_groups=groups, tiled=True)
+
+    def copies(piece, groups):
+        return jnp.broadcast_to(piece[None], (len(groups[0]),) + piece.shape)
+
+    part = exchange(value.reshape(len(four[0]), -1, value.shape[-1]), four).sum(0)
+    piece = exchange(part.reshape(len(same[0]), -1), same).sum(0)
+    part = exchange(copies(piece, same), same).reshape(part.shape)
+    return exchange(copies(part, four), four).reshape(value.shape)
 
 
 def per_device(vectors, onsite, tile_values, tile_rows, tile_cols, tile_count):
@@ -237,28 +284,22 @@
     parts = lax.all_to_all(keep + other, "x", 0, 0, tiled=True)
 
     nblocks = kstates // width
-    upper_blocks = nblocks * (nblocks + 1) // 2
-    applied, gram = call(
+    half = jax.ShapeDtypeStruct((nblocks * (nblocks + 1) // 4, width, width), f32)
+    core = k.astype(jnp.int32).reshape(1)
+    applied, own, other = call(
         gram_blocks,
-        [jax.ShapeDtypeStruct((own_rows, kstates), f32), jax.ShapeDtypeStruct((upper_blocks, width, width), f32)],
-        [vm, vm],
-    )(parts, local)
-
-    ncol = lax.axis_size(("x", "k"))
-    nrow = lax.axis_size(("y", "z"))
-    piece = lax.all_to_all(gram.reshape(ncol, -1, width), ("x", "k"), 0, 0, tiled=True).sum(0)
-    shape = piece.shape
-    piece = lax.all_to_all(piece.reshape(nrow, -1), ("y", "z"), 0, 0, tiled=True).sum(0, keepdims=True)
-    piece = lax.all_to_all(jnp.tile(piece, (nrow, 1)), ("y", "z"), 0, 0, tiled=True).reshape(shape)
-    gram = lax.all_to_all(jnp.tile(piece[None], (ncol, 1, 1)), ("x", "k"), 0, 0, tiled=True)
-    gram = gram.reshape(upper_blocks, width, width)
+        [jax.ShapeDtypeStruct((own_rows, kstates), f32), half, half],
+        [sm, vm, vm],
+    )(core, parts, local)
+    own = sum_halves(own + lax.ppermute(other, "k", [(0, 1), (1, 0)]))
+    other = lax.ppermute(own, "k", [(0, 1), (1, 0)])
 
     states, upper = call(
         factor_and_solve,
         [jax.ShapeDtypeStruct((own_rows, kstates), f32), jax.ShapeDtypeStruct((kstates, kstates), f32)],
-        [vm, vm],
+        [sm, vm, vm, vm],
         [vm((kstates, kstates), f32), vm((width, width), f32)],
-    )(gram, applied)
+    )(core, own, other, applied)
     return (states, upper)
 
 

time: 215 us -> 214 us (level)
  blocking collectives: 88 us -> 81.1 us
  waiting for transfers between devices: 25.6 us -> 27.8 us
    all_to_all x4, blocking collectives: 62.8 us -> 55.9 us  [exchange(): lax.all_to_all(pieces, axes, 0, 0, axis_index_groups=groups, tiled=True)]
    ppermute x0 -> x2, starting transfers between devices: none -> 5.81 us  [the longest x1 3.42 us: per_device(): own = sum_halves(own + lax.ppermute(other, 'k', [(0, 1), (1, 0)]))]
    ppermute x1, starting transfers between devices: 9.93 us -> 5.02 us  [per_device(): other = lax.ppermute(send, 'k', [(0, 1), (1, 0)])]
    ppermute x0 -> x2, waiting for transfers between devices: none -> 2.47 us  [the longest x1 1.23 us: per_device(): own = sum_halves(own + lax.ppermute(other, 'k', [(0, 1), (1, 0)]))]
  transfers between devices with their start and end apart: 16 -> 18, of which waited for: 5 -> 7; matrix products, arithmetic and copies ran while one was open for 0% -> 0% of each run, Pallas kernels for 0% -> 0%
where the time goes in v4:
time: 214 us; the launch traced here: 213 us
  blocking collectives  81.1 us (38%)
  starting transfers between devices  67.1 us (31%)
  Pallas kernels  28.6 us (13%)
  waiting for transfers between devices  27.8 us (13%)
  other arithmetic  3.54 us (2%)
  local copies, waits for them, and re-layouts  2.79 us (1%)
    all_to_all x4, blocking collectives, exchange(): lax.all_to_all(pieces, axes, 0, 0, axis_index_groups=groups, tiled=True)  55.9 us
    ppermute x7, starting transfers between devices, gather_states(): below[at].append(lax.ppermute(below[at][-1], axes, down))  38.1 us
    all_to_all x1, blocking collectives, gather_states(): lax.all_to_all(copies, axes, 0, 0, axis_index_groups=line_places(*sizes),...  25.2 us
    pallas_call x1, Pallas kernels, per_device(): call(factor_and_solve, [jax.ShapeDtypeStruct((own_rows, kstates), f32), j...  22.2 us
    all_to_all x1, waiting for transfers between devices, per_device(): parts = lax.all_to_all(keep + other, 'x', 0, 0, tiled=True)  14.4 us
    ppermute x7, starting transfers between devices, gather_states(): above[at].append(lax.ppermute(above[at][-1], axes, up))  13.4 us
    ppermute x7, waiting for transfers between devices, gather_states(): above[at].append(lax.ppermute(above[at][-1], axes, up))  7.08 us
    pallas_call x1, Pallas kernels, per_device(): call(tile_products, [part, part], [sm, anywhere] + [anywhere] * len(buffe...  5.61 us
  transfers between devices with their start and end apart: 18, of which 7 were waited for; matrix products, arithmetic and copies ran while one was open for 0% of the time, Pallas kernels for 0%

profile of v4, /device:TPU:1, one launch (start us, length us, event | category | flops | bytes accessed | tf_op | source)
XLA Modules:
  0.0 212.6 jit_solution(11855244737707089583)
XLA Ops:
  1.6 25.2 %all_to_all.35 = bf16[8,128,512]{2,1,0:T(8,128)(2,1)S(1)} all-to-all(bf16[8,128,512]{2,1,0:T(8,128)(2,1)S(1)} %broadcast_in_dim.8), channel_id=1, replica_groups={{0,8,16,24,32,40,48,56},{1,65,129,193,257,321,385,449},{64,72,80,88,96,..., dimensions={0} | all-to-all | bytes 2097152 | tf_op jit(solution)/shard_map/all_to_all | solution.py:193
  26.9 10.7 %collective-permute-start.10 = (bf16[4,128,512]{2,1,0:T(8,128)(2,1)S(1)}, bf16[4,128,512]{2,1,0:T(8,128)(2,1)S(1)}, u32[]{:S(2)}, u32[]{:S(2)}) collective-permute-start(bf16[4,128,512]{2,1,0:T(8,128)(2,1)S(1)} %get-tuple-element.14.refs_8_), channel_id=1, source_target_pairs={{0,448},{1,57},{8,456},{9,1},{16,464},{17,9},{24,472},{25,17},{32,... | collective-permute-start | bytes 1572872 | tf_op jit(solution)/shard_map/ppermute | solution.py:203
  37.6 1.9 collective-permute-start
  39.5 4.6 %collective-permute-start.4 = (bf16[4,128,512]{2,1,0:T(8,128)(2,1)S(1)}, bf16[4,128,512]{2,1,0:T(8,128)(2,1)S(1)}, u32[]{:S(2)}, u32[]{:S(2)}) collective-permute-start(bf16[4,128,512]{2,1,0:T(8,128)(2,1)S(1)} %get-tuple-element.15.refs_0_), channel_id=1, source_target_pairs={{0,448},{1,57},{8,456},{9,1},{16,464},{17,9},{24,472},{25,17},{32,... | collective-permute-start | bytes 1572872 | tf_op jit(solution)/shard_map/ppermute | solution.py:203
  44.1 1.9 collective-permute-start.7
  46.1 4.6 %collective-permute-start.11 = (bf16[4,128,512]{2,1,0:T(8,128)(2,1)S(1)}, bf16[4,128,512]{2,1,0:T(8,128)(2,1)}, u32[]{:S(2)}, u32[]{:S(2)}) collective-permute-start(bf16[4,128,512]{2,1,0:T(8,128)(2,1)S(1)} %collective-permute-done.10.refs_15_), channel_id=1, source_target_pairs={{0,448},{1,57},{8,456},{9,1},{16,464},{17,9},{24,472},{25,17},{32,... | collective-permute-start | bytes 1572872 | tf_op jit(solution)/shard_map/ppermute | solution.py:203
  50.7 1.9 collective-permute-start.1
  52.6 4.6 %collective-permute-start.5 = (bf16[4,128,512]{2,1,0:T(8,128)(2,1)S(1)}, bf16[4,128,512]{2,1,0:T(8,128)(2,1)}, u32[]{:S(2)}, u32[]{:S(2)}) collective-permute-start(bf16[4,128,512]{2,1,0:T(8,128)(2,1)S(1)} %collective-permute-done.4.refs_7_), channel_id=1, source_target_pairs={{0,448},{1,57},{8,456},{9,1},{16,464},{17,9},{24,472},{25,17},{32,... | collective-permute-start | bytes 1572872 | tf_op jit(solution)/shard_map/ppermute | solution.py:203
  57.2 1.9 collective-permute-start.8
  59.2 4.6 %collective-permute-start.12 = (bf16[4,128,512]{2,1,0:T(8,128)(2,1)}, bf16[4,128,512]{2,1,0:T(8,128)(2,1)}, u32[]{:S(2)}, u32[]{:S(2)}) collective-permute-start(bf16[4,128,512]{2,1,0:T(8,128)(2,1)} %collective-permute-done.11.refs_14_), channel_id=1, source_target_pairs={{0,448},{1,57},{8,456},{9,1},{16,464},{17,9},{24,472},{25,17},{32,... | collective-permute-start | bytes 1572872 | tf_op jit(solution)/shard_map/ppermute | solution.py:203
  63.7 1.9 collective-permute-start.2
  66.4 4.6 %collective-permute-start.6 = (bf16[4,128,512]{2,1,0:T(8,128)(2,1)}, bf16[4,128,512]{2,1,0:T(8,128)(2,1)S(1)}, u32[]{:S(2)}, u32[]{:S(2)}) collective-permute-start(bf16[4,128,512]{2,1,0:T(8,128)(2,1)} %collective-permute-done.5.refs_6_), channel_id=1, source_target_pairs={{0,448},{1,57},{8,456},{9,1},{16,464},{17,9},{24,472},{25,17},{32,... | collective-permute-start | bytes 1572872 | tf_op jit(solution)/shard_map/ppermute | solution.py:203
  70.9 1.9 collective-permute-start.9
  72.9 4.6 %collective-permute-start.13 = (bf16[4,128,512]{2,1,0:T(8,128)(2,1)}, bf16[4,128,512]{2,1,0:T(8,128)(2,1)S(1)}, u32[]{:S(2)}, u32[]{:S(2)}) collective-permute-start(bf16[4,128,512]{2,1,0:T(8,128)(2,1)} %collective-permute-done.12.refs_13_), channel_id=1, source_target_pairs={{0,448},{1,57},{8,456},{9,1},{16,464},{17,9},{24,472},{25,17},{32,... | collective-permute-start | bytes 1572872 | tf_op jit(solution)/shard_map/ppermute | solution.py:203
  77.5 1.9 collective-permute-start.3
  80.7 1.8 collective-permute-done.9.refs_11_
  82.6 1.3 collective-permute-done.13.refs_12_
  83.9 5.2 %collective-permute-done.3.refs_4_ = bf16[4,128,512]{2,1,0:T(8,128)(2,1)S(1)} collective-permute-done((bf16[4,128,512]{2,1,0:T(8,128)(2,1)}, bf16[4,128,512]{2,1,0:T(8,128)(2,1)S(1)}, u32[]{:S(2)}, u32[]{:S(2)}) %collective-permute-start.3) | collective-permute-done | bytes 524320 | tf_op jit(solution)/shard_map/ppermute | solution.py:201
  89.9 5.6 %shard_map.77 = (f32[4,128,512]{2,1,0:T(8,128)}, f32[4,128,512]{2,1,0:T(8,128)}) custom-call(s32[73]{0:T(128)} %pad_add_fusion.meta_ref, bf16[24,128,128]{2,1,0:T(8,128)(2,1)} %bitcast.40, bf16[4,128,512]{2,1,0:T(8,128)(2,1)} %copy-done.1, bf16[4,128,512]{2,1,0:T(8,128)(2,1)} %copy-done.3, bf16[4,128,512]{2,1,0:T(8,128)(2,1)} %collective-permute-done.1.refs_2_, ...), custom_call_target="tpu_custom_call" | custom-call | tf_op jit(solution)/shard_map/pallas_call | solution.py:268
  95.5 5.0 %collective-permute-start.14 = (f32[4,128,512]{2,1,0:T(8,128)}, f32[4,128,512]{2,1,0:T(8,128)S(1)}, u32[]{:S(2)}, u32[]{:S(2)}) collective-permute-start(f32[4,128,512]{2,1,0:T(8,128)} %get-tuple-element.8), channel_id=1, source_target_pairs={{0,1},{1,0},{2,3},{3,2},{4,5},{5,4},{6,7},{7,6},{8,9},{9,8},{10,11... | collective-permute-start | bytes 3145736 | tf_op jit(solution)/shard_map/ppermute | solution.py:283
  100.6 2.5 %collective-permute-done.14 = f32[4,128,512]{2,1,0:T(8,128)S(1)} collective-permute-done((f32[4,128,512]{2,1,0:T(8,128)}, f32[4,128,512]{2,1,0:T(8,128)S(1)}, u32[]{:S(2)}, u32[]{:S(2)}) %collective-permute-start.14) | collective-permute-done | bytes 1048608 | tf_op jit(solution)/shard_map/ppermute | solution.py:283
  103.0 2.4 %add.47 = f32[4,128,512]{2,1,0:T(8,128)} add(f32[4,128,512]{2,1,0:T(8,128)} %get-tuple-element.7, f32[4,128,512]{2,1,0:T(8,128)S(1)} %collective-permute-done.14) | non-fusion elementwise | flops 262144 | bytes 3145728 | tf_op jit(solution)/shard_map/add | solution.py:284
  105.4 4.7 %all-to-all-start.1 = ((f32[4,128,512]{2,1,0:T(8,128)}), f32[4,128,512]{2,1,0:T(8,128)S(1)}, u32[]{:S(2)}, u32[]{:S(2)}) async-start(f32[4,128,512]{2,1,0:T(8,128)} %add.47), calls=%async_computation.1 | async-start | bytes 2097152 | tf_op jit(solution)/shard_map/all_to_all | solution.py:284
  110.2 14.4 %all-to-all-done.1.parts_ref = f32[4,128,512]{2,1,0:T(8,128)S(1)} async-done(((f32[4,128,512]{2,1,0:T(8,128)}), f32[4,128,512]{2,1,0:T(8,128)S(1)}, u32[]{:S(2)}, u32[]{:S(2)}) %all-to-all-start.1) | async-done | bytes 1048608 | tf_op jit(solution)/shard_map/all_to_all | solution.py:284
  125.5 3.4 %collective-permute-start.15 = (f32[5,128,128]{2,1,0:T(8,128)S(1)}, f32[5,128,128]{2,1,0:T(8,128)S(1)}, u32[]{:S(2)}, u32[]{:S(2)}) collective-permute-start(f32[5,128,128]{2,1,0:T(8,128)S(1)} %get-tuple-element.10), channel_id=1, source_target_pairs={{0,1},{1,0},{2,3},{3,2},{4,5},{5,4},{6,7},{7,6},{8,9},{9,8},{10,11... | collective-permute-start | bytes 983048 | tf_op jit(solution)/shard_map/ppermute | solution.py:294
  128.9 1.2 collective-permute-done.15
  130.2 8.2 %all_to_all.36 = f32[4,160,128]{2,1,0:T(8,128)S(1)} all-to-all(f32[4,160,128]{2,1,0:T(8,128)S(1)} %bitcast.39), channel_id=1, replica_groups={{0,2,4,6},{8,10,12,14},{16,18,20,22},{24,26,28,30},{32,34,36,38},{40,42..., dimensions={0} | all-to-all | bytes 655360 | tf_op jit(solution)/shard_map/all_to_all | solution.py:241
  138.6 21.9 %all_to_all.37 = f32[64,1,320]{2,1,0:T(1,128)S(1)} all-to-all(f32[64,1,320]{2,1,0:T(1,128)S(1)} %all_to_all.25), channel_id=1, replica_groups={{0,8,16,24,32,40,48,56,64,72,80,88,96,104,112,120,128,136,144,152,160,1..., dimensions={0} | all-to-all | bytes 163840 | tf_op jit(solution)/shard_map/all_to_all | solution.py:241
  160.6 18.0 %all_to_all.38 = f32[64,1,320]{2,1,0:T(1,128)S(1)} all-to-all(f32[64,1,320]{2,1,0:T(1,128)S(1)} %broadcast_in_dim.9), channel_id=1, replica_groups={{0,8,16,24,32,40,48,56,64,72,80,88,96,104,112,120,128,136,144,152,160,1..., dimensions={0} | all-to-all | bytes 163840 | tf_op jit(solution)/shard_map/all_to_all | solution.py:241
  179.0 7.8 %all_to_all.39 = f32[4,160,128]{2,1,0:T(8,128)S(1)} all-to-all(f32[4,160,128]{2,1,0:T(8,128)S(1)} %broadcast_in_dim.11), channel_id=1, replica_groups={{0,2,4,6},{8,10,12,14},{16,18,20,22},{24,26,28,30},{32,34,36,38},{40,42..., dimensions={0} | all-to-all | bytes 655360 | tf_op jit(solution)/shard_map/all_to_all | solution.py:241
  186.8 2.4 %collective-permute-start.16 = (f32[5,128,128]{2,1,0:T(8,128)S(1)}, f32[5,128,128]{2,1,0:T(8,128)S(1)}, u32[]{:S(2)}, u32[]{:S(2)}) collective-permute-start(f32[5,128,128]{2,1,0:T(8,128)S(1)} %bitcast.37), channel_id=1, source_target_pairs={{0,1},{1,0},{2,3},{3,2},{4,5},{5,4},{6,7},{7,6},{8,9},{9,8},{10,11... | collective-permute-start | bytes 983048 | tf_op jit(solution)/shard_map/ppermute | solution.py:295
  190.4 22.2 %shard_map.79 = (f32[128,512]{1,0:T(8,128)}, f32[512,512]{1,0:T(8,128)}) custom-call(s32[1]{0:T(128)} %bitcast.core_ref, f32[5,128,128]{2,1,0:T(8,128)S(1)} %bitcast.38, f32[5,128,128]{2,1,0:T(8,128)S(1)} %collective-permute-done.16.other_ref, f32[128,512]{1,0:T(8,128)S(1)} %get-tuple-element.11.applied_ref), custom_call_target="tpu_custom_call" | custom-call | tf_op jit(solution)/shard_map/pallas_call | solution.py:297
  (55 shorter events, 6.0 us)
Async XLA Ops:
  26.9 62.2 %copy-start = (bf16[4,128,512]{2,1,0:T(8,128)(2,1)}, bf16[4,128,512]{2,1,0:T(8,128)(2,1)S(1)}, u32[]{:S(2)}) copy-start(bf16[4,128,512]{2,1,0:T(8,128)(2,1)S(1)} %get-tuple-element.14.refs_8_) | copy-start | bytes 1572868
  26.9 62.2 %copy-start.1 = (bf16[4,128,512]{2,1,0:T(8,128)(2,1)}, bf16[4,128,512]{2,1,0:T(8,128)(2,1)S(1)}, u32[]{:S(2)}) copy-start(bf16[4,128,512]{2,1,0:T(8,128)(2,1)S(1)} %get-tuple-element.15.refs_0_) | copy-start | bytes 1572868
  26.9 19.1 %collective-permute-start.10 = (bf16[4,128,512]{2,1,0:T(8,128)(2,1)S(1)}, bf16[4,128,512]{2,1,0:T(8,128)(2,1)S(1)}, u32[]{:S(2)}, u32[]{:S(2)}) collective-permute-start(bf16[4,128,512]{2,1,0:T(8,128)(2,1)S(1)} %get-tuple-element.14.refs_8_), channel_id=1, source_target_pairs={{0,448},{1,57},{8,456},{9,1},{16,464},{17,9},{24,472},{25,17},{32,... | collective-permute-start | bytes 1572872 | tf_op jit(solution)/shard_map/ppermute | solution.py:203
  37.6 13.0 %collective-permute-start = (bf16[4,128,512]{2,1,0:T(8,128)(2,1)S(1)}, bf16[4,128,512]{2,1,0:T(8,128)(2,1)S(1)}, u32[]{:S(2)}, u32[]{:S(2)}) collective-permute-start(bf16[4,128,512]{2,1,0:T(8,128)(2,1)S(1)} %get-tuple-element.15.refs_0_), channel_id=1, source_target_pairs={{0,64},{1,9},{8,72},{9,17},{16,80},{17,25},{24,88},{25,33},{32,96}... | collective-permute-start | bytes 1572872 | tf_op jit(solution)/shard_map/ppermute | solution.py:201
  39.5 13.1 %collective-permute-start.4 = (bf16[4,128,512]{2,1,0:T(8,128)(2,1)S(1)}, bf16[4,128,512]{2,1,0:T(8,128)(2,1)S(1)}, u32[]{:S(2)}, u32[]{:S(2)}) collective-permute-start(bf16[4,128,512]{2,1,0:T(8,128)(2,1)S(1)} %get-tuple-element.15.refs_0_), channel_id=1, source_target_pairs={{0,448},{1,57},{8,456},{9,1},{16,464},{17,9},{24,472},{25,17},{32,... | collective-permute-start | bytes 1572872 | tf_op jit(solution)/shard_map/ppermute | solution.py:203
  44.1 13.1 %collective-permute-start.7 = (bf16[4,128,512]{2,1,0:T(8,128)(2,1)S(1)}, bf16[4,128,512]{2,1,0:T(8,128)(2,1)S(1)}, u32[]{:S(2)}, u32[]{:S(2)}) collective-permute-start(bf16[4,128,512]{2,1,0:T(8,128)(2,1)S(1)} %get-tuple-element.14.refs_8_), channel_id=1, source_target_pairs={{0,64},{1,9},{8,72},{9,17},{16,80},{17,25},{24,88},{25,33},{32,96}... | collective-permute-start | bytes 1572872 | tf_op jit(solution)/shard_map/ppermute | solution.py:201
  46.0 43.1 %copy-start.2 = (bf16[4,128,512]{2,1,0:T(8,128)(2,1)}, bf16[4,128,512]{2,1,0:T(8,128)(2,1)S(1)}, u32[]{:S(2)}) copy-start(bf16[4,128,512]{2,1,0:T(8,128)(2,1)S(1)} %collective-permute-done.10.refs_15_) | copy-start | bytes 1572868
  46.1 13.1 %collective-permute-start.11 = (bf16[4,128,512]{2,1,0:T(8,128)(2,1)S(1)}, bf16[4,128,512]{2,1,0:T(8,128)(2,1)}, u32[]{:S(2)}, u32[]{:S(2)}) collective-permute-start(bf16[4,128,512]{2,1,0:T(8,128)(2,1)S(1)} %collective-permute-done.10.refs_15_), channel_id=1, source_target_pairs={{0,448},{1,57},{8,456},{9,1},{16,464},{17,9},{24,472},{25,17},{32,... | collective-permute-start | bytes 1572872 | tf_op jit(solution)/shard_map/ppermute | solution.py:203
  50.7 38.5 %copy-start.3 = (bf16[4,128,512]{2,1,0:T(8,128)(2,1)}, bf16[4,128,512]{2,1,0:T(8,128)(2,1)S(1)}, u32[]{:S(2)}) copy-start(bf16[4,128,512]{2,1,0:T(8,128)(2,1)S(1)} %collective-permute-done.refs_1_) | copy-start | bytes 1572868
  50.7 13.1 %collective-permute-start.1 = (bf16[4,128,512]{2,1,0:T(8,128)(2,1)S(1)}, bf16[4,128,512]{2,1,0:T(8,128)(2,1)}, u32[]{:S(2)}, u32[]{:S(2)}) collective-permute-start(bf16[4,128,512]{2,1,0:T(8,128)(2,1)S(1)} %collective-permute-done.refs_1_), channel_id=1, source_target_pairs={{0,64},{1,9},{8,72},{9,17},{16,80},{17,25},{24,88},{25,33},{32,96}... | collective-permute-start | bytes 1572872 | tf_op jit(solution)/shard_map/ppermute | solution.py:201
  52.6 36.5 %copy-start.4 = (bf16[4,128,512]{2,1,0:T(8,128)(2,1)}, bf16[4,128,512]{2,1,0:T(8,128)(2,1)S(1)}, u32[]{:S(2)}) copy-start(bf16[4,128,512]{2,1,0:T(8,128)(2,1)S(1)} %collective-permute-done.4.refs_7_) | copy-start | bytes 1572868
  52.6 13.7 %collective-permute-start.5 = (bf16[4,128,512]{2,1,0:T(8,128)(2,1)S(1)}, bf16[4,128,512]{2,1,0:T(8,128)(2,1)}, u32[]{:S(2)}, u32[]{:S(2)}) collective-permute-start(bf16[4,128,512]{2,1,0:T(8,128)(2,1)S(1)} %collective-permute-done.4.refs_7_), channel_id=1, source_target_pairs={{0,448},{1,57},{8,456},{9,1},{16,464},{17,9},{24,472},{25,17},{32,... | collective-permute-start | bytes 1572872 | tf_op jit(solution)/shard_map/ppermute | solution.py:203
  57.2 31.9 %copy-start.5 = (bf16[4,128,512]{2,1,0:T(8,128)(2,1)}, bf16[4,128,512]{2,1,0:T(8,128)(2,1)S(1)}, u32[]{:S(2)}) copy-start(bf16[4,128,512]{2,1,0:T(8,128)(2,1)S(1)} %collective-permute-done.7.refs_9_) | copy-start | bytes 1572868
  57.2 13.7 %collective-permute-start.8 = (bf16[4,128,512]{2,1,0:T(8,128)(2,1)S(1)}, bf16[4,128,512]{2,1,0:T(8,128)(2,1)}, u32[]{:S(2)}, u32[]{:S(2)}) collective-permute-start(bf16[4,128,512]{2,1,0:T(8,128)(2,1)S(1)} %collective-permute-done.7.refs_9_), channel_id=1, source_target_pairs={{0,64},{1,9},{8,72},{9,17},{16,80},{17,25},{24,88},{25,33},{32,96}... | collective-permute-start | bytes 1572872 | tf_op jit(solution)/shard_map/ppermute | solution.py:201
  59.2 13.7 %collective-permute-start.12 = (bf16[4,128,512]{2,1,0:T(8,128)(2,1)}, bf16[4,128,512]{2,1,0:T(8,128)(2,1)}, u32[]{:S(2)}, u32[]{:S(2)}) collective-permute-start(bf16[4,128,512]{2,1,0:T(8,128)(2,1)} %collective-permute-done.11.refs_14_), channel_id=1, source_target_pairs={{0,448},{1,57},{8,456},{9,1},{16,464},{17,9},{24,472},{25,17},{32,... | collective-permute-start | bytes 1572872 | tf_op jit(solution)/shard_map/ppermute | solution.py:203
  63.7 13.7 %collective-permute-start.2 = (bf16[4,128,512]{2,1,0:T(8,128)(2,1)}, bf16[4,128,512]{2,1,0:T(8,128)(2,1)}, u32[]{:S(2)}, u32[]{:S(2)}) collective-permute-start(bf16[4,128,512]{2,1,0:T(8,128)(2,1)} %collective-permute-done.1.refs_2_), channel_id=1, source_target_pairs={{0,64},{1,9},{8,72},{9,17},{16,80},{17,25},{24,88},{25,33},{32,96}... | collective-permute-start | bytes 1572872 | tf_op jit(solution)/shard_map/ppermute | solution.py:201
  66.3 13.1 %copy-start.11 = (s32[1,1,24]{2,1,0:T(1,128)S(1)}, s32[1,1,24]{2,1,0:T(1,128)}, u32[]{:S(2)}) copy-start(s32[1,1,24]{2,1,0:T(1,128)} %param.10) | copy-start | bytes 292
  66.4 14.4 %collective-permute-start.6 = (bf16[4,128,512]{2,1,0:T(8,128)(2,1)}, bf16[4,128,512]{2,1,0:T(8,128)(2,1)S(1)}, u32[]{:S(2)}, u32[]{:S(2)}) collective-permute-start(bf16[4,128,512]{2,1,0:T(8,128)(2,1)} %collective-permute-done.5.refs_6_), channel_id=1, source_target_pairs={{0,448},{1,57},{8,456},{9,1},{16,464},{17,9},{24,472},{25,17},{32,... | collective-permute-start | bytes 1572872 | tf_op jit(solution)/shard_map/ppermute | solution.py:203
  70.9 11.6 %collective-permute-start.9 = (bf16[4,128,512]{2,1,0:T(8,128)(2,1)}, bf16[4,128,512]{2,1,0:T(8,128)(2,1)S(1)}, u32[]{:S(2)}, u32[]{:S(2)}) collective-permute-start(bf16[4,128,512]{2,1,0:T(8,128)(2,1)} %collective-permute-done.8.refs_10_), channel_id=1, source_target_pairs={{0,64},{1,9},{8,72},{9,17},{16,80},{17,25},{24,88},{25,33},{32,96}... | collective-permute-start | bytes 1572872 | tf_op jit(solution)/shard_map/ppermute | solution.py:201
  72.9 11.0 %collective-permute-start.13 = (bf16[4,128,512]{2,1,0:T(8,128)(2,1)}, bf16[4,128,512]{2,1,0:T(8,128)(2,1)S(1)}, u32[]{:S(2)}, u32[]{:S(2)}) collective-permute-start(bf16[4,128,512]{2,1,0:T(8,128)(2,1)} %collective-permute-done.12.refs_13_), channel_id=1, source_target_pairs={{0,448},{1,57},{8,456},{9,1},{16,464},{17,9},{24,472},{25,17},{32,... | collective-permute-start | bytes 1572872 | tf_op jit(solution)/shard_map/ppermute | solution.py:203
  77.5 11.6 %collective-permute-start.3 = (bf16[4,128,512]{2,1,0:T(8,128)(2,1)}, bf16[4,128,512]{2,1,0:T(8,128)(2,1)S(1)}, u32[]{:S(2)}, u32[]{:S(2)}) collective-permute-start(bf16[4,128,512]{2,1,0:T(8,128)(2,1)} %collective-permute-done.2.refs_3_), channel_id=1, source_target_pairs={{0,64},{1,9},{8,72},{9,17},{16,80},{17,25},{24,88},{25,33},{32,96}... | collective-permute-start | bytes 1572872 | tf_op jit(solution)/shard_map/ppermute | solution.py:201
  79.4 0.7 copy-start.13
  80.7 8.4 %copy-start.6 = (bf16[4,128,512]{2,1,0:T(8,128)(2,1)}, bf16[4,128,512]{2,1,0:T(8,128)(2,1)S(1)}, u32[]{:S(2)}) copy-start(bf16[4,128,512]{2,1,0:T(8,128)(2,1)S(1)} %collective-permute-done.6.refs_5_) | copy-start | bytes 1572868
  82.6 6.6 %copy-start.7 = (bf16[4,128,512]{2,1,0:T(8,128)(2,1)}, bf16[4,128,512]{2,1,0:T(8,128)(2,1)S(1)}, u32[]{:S(2)}) copy-start(bf16[4,128,512]{2,1,0:T(8,128)(2,1)S(1)} %collective-permute-done.9.refs_11_) | copy-start | bytes 1572868
  83.9 5.3 %copy-start.8 = (bf16[4,128,512]{2,1,0:T(8,128)(2,1)}, bf16[4,128,512]{2,1,0:T(8,128)(2,1)S(1)}, u32[]{:S(2)}) copy-start(bf16[4,128,512]{2,1,0:T(8,128)(2,1)S(1)} %collective-permute-done.13.refs_12_) | copy-start | bytes 1572868
  89.1 0.8 copy-start.9
  95.5 7.5 %collective-permute-start.14 = (f32[4,128,512]{2,1,0:T(8,128)}, f32[4,128,512]{2,1,0:T(8,128)S(1)}, u32[]{:S(2)}, u32[]{:S(2)}) collective-permute-start(f32[4,128,512]{2,1,0:T(8,128)} %get-tuple-element.8), channel_id=1, source_target_pairs={{0,1},{1,0},{2,3},{3,2},{4,5},{5,4},{6,7},{7,6},{8,9},{9,8},{10,11... | collective-permute-start | bytes 3145736 | tf_op jit(solution)/shard_map/ppermute | solution.py:283
  105.4 4.7 %copy-start.10 = (bf16[128,512]{1,0:T(8,128)(2,1)S(1)}, bf16[128,512]{1,0:T(8,128)(2,1)}, u32[]{:S(2)}) copy-start(bf16[128,512]{1,0:T(8,128)(2,1)} %param.6) | copy-start | bytes 393220
  105.4 4.7 %copy-start.12 = (f32[128]{0:T(128)S(1)}, f32[128]{0:T(128)}, u32[]{:S(2)}) copy-start(f32[128]{0:T(128)} %param.7) | copy-start | bytes 1540
  105.4 19.2 %all-to-all-start.1 = ((f32[4,128,512]{2,1,0:T(8,128)}), f32[4,128,512]{2,1,0:T(8,128)S(1)}, u32[]{:S(2)}, u32[]{:S(2)}) async-start(f32[4,128,512]{2,1,0:T(8,128)} %add.47), calls=%async_computation.1 | async-start | bytes 2097152 | tf_op jit(solution)/shard_map/all_to_all | solution.py:284
  125.5 4.7 %collective-permute-start.15 = (f32[5,128,128]{2,1,0:T(8,128)S(1)}, f32[5,128,128]{2,1,0:T(8,128)S(1)}, u32[]{:S(2)}, u32[]{:S(2)}) collective-permute-start(f32[5,128,128]{2,1,0:T(8,128)S(1)} %get-tuple-element.10), channel_id=1, source_target_pairs={{0,1},{1,0},{2,3},{3,2},{4,5},{5,4},{6,7},{7,6},{8,9},{9,8},{10,11... | collective-permute-start | bytes 983048 | tf_op jit(solution)/shard_map/ppermute | solution.py:294
  186.8 3.6 %collective-permute-start.16 = (f32[5,128,128]{2,1,0:T(8,128)S(1)}, f32[5,128,128]{2,1,0:T(8,128)S(1)}, u32[]{:S(2)}, u32[]{:S(2)}) collective-permute-start(f32[5,128,128]{2,1,0:T(8,128)S(1)} %bitcast.37), channel_id=1, source_target_pairs={{0,1},{1,0},{2,3},{3,2},{4,5},{5,4},{6,7},{7,6},{8,9},{9,8},{10,11... | collective-permute-start | bytes 983048 | tf_op jit(solution)/shard_map/ppermute | solution.py:295

commit v5 on v4

--- a/solution.py
+++ b/solution.py
@@ -9,7 +9,6 @@
 
 FULL = lax.Precision.HIGHEST
 STRIP = 8
-GROUP = 3
 
 
 def dot_full(left, right, left_dim, right_dim):
@@ -18,43 +17,26 @@
 
 
 def tile_products(meta_ref, tiles_ref, *refs):
-    *sources, keep_ref, send_ref, sums, tiles, held, tile_sem, sems, out_sems = refs
+    *sources, keep_ref, send_ref, sums = refs
     slots = tiles_ref.shape[0]
     per_core = keep_ref.shape[0]
-    count = meta_ref[3 * slots]
-    steps = (count + GROUP - 1) // GROUP
-
-    fetch_tiles = pltpu.make_async_copy(tiles_ref, tiles, tile_sem)
-    fetch_tiles.start()
-
-    @pl.loop(0, steps * GROUP)
+    sums[...] = jnp.zeros_like(sums)
+
+    def add(t, which, first, last):
+        if last - first == 1:
+            block = sources[first][meta_ref[2 * slots + t]]
+            sums[meta_ref[t]] += jnp.dot(tiles_ref[t], block, preferred_element_type=jnp.float32)
+            return
+        middle = (first + last) // 2
+        pl.when(which < middle)(lambda: add(t, which, first, middle))
+        pl.when(which >= middle)(lambda: add(t, which, middle, last))
+
+    @pl.loop(0, meta_ref[3 * slots])
     def _(t):
-        for at, source in enumerate(sources):
-            @pl.when(meta_ref[slots + t] == at)
-            def _():
-                pltpu.make_async_copy(source.at[meta_ref[2 * slots + t]], held.at[t], sems.at[t]).start()
-
-    sums[...] = jnp.zeros_like(sums)
-    fetch_tiles.wait()
-
-    @pl.loop(0, steps)
-    def _(step):
-        first = step * GROUP
-        prods = []
-        for t in range(GROUP):
-            pltpu.make_async_copy(sources[0].at[0], held.at[first + t], sems.at[first + t]).wait()
-            tile = tiles[first + t]
-            tile = jnp.where(first + t < count, tile, jnp.zeros_like(tile))
-            prods.append(jnp.dot(tile, held[first + t], preferred_element_type=jnp.float32))
-        for t in range(GROUP):
-            sums[meta_ref[first + t]] += prods[t]
-
-    put_keep = pltpu.make_async_copy(sums.at[:per_core], keep_ref, out_sems.at[0])
-    put_send = pltpu.make_async_copy(sums.at[per_core:], send_ref, out_sems.at[1])
-    put_send.start()
-    put_keep.start()
-    put_send.wait()
-    put_keep.wait()
+        add(t, meta_ref[slots + t], 0, len(sources))
+
+    keep_ref[...] = sums[:per_core]
+    send_ref[...] = sums[per_core:]
 
 
 def upper_pairs(nblocks):
@@ -99,17 +81,16 @@
         for k in range(STRIP):
             pivot = spread(cols[k], k)
             recip = 1.0 / pivot
-            ratio = cols[k] * recip
             at = sub == k
-            both = jnp.where(at, -recip, ratio)
-            below = jnp.where(sub > k, ratio, 0.0)
+            both = jnp.where(at, -1.0, cols[k])
+            below = jnp.where(sub > k, cols[k], 0.0)
             for b in range(k + 1, STRIP):
-                cols[b] = jnp.where(at, 0.0, cols[b]) - both * spread(cols[b], k)
+                cols[b] = jnp.where(at, 0.0, cols[b]) - (both * spread(cols[b], k)) * recip
             row_a, row_e = spread(full_a, k), spread(full_e, k)
-            down_a = down_a - below * spread(down_a, k)
-            down_e = down_e - below * spread(down_e, k)
-            full_a = jnp.where(at, 0.0, full_a) - both * row_a
-            full_e = jnp.where(at, 0.0, full_e) - both * row_e
+            down_a = down_a - (below * spread(down_a, k)) * recip
+            down_e = down_e - (below * spread(down_e, k)) * recip
+            full_a = jnp.where(at, 0.0, full_a) - (both * row_a) * recip
+            full_e = jnp.where(at, 0.0, full_e) - (both * row_e) * recip
             pivots = pivot if pivots is None else jnp.where(sub >= k, pivot, pivots)
         scale = lax.rsqrt(pivots)
         u_ref[base + first:base + first + STRIP, base:base + n] = jnp.where(lane >= sub + first, down_a * scale, 0.0)
@@ -153,12 +134,12 @@
             states_ref[:, hi:] -= dot_full(solved, panel, 1, 0)
 
 
-def call(body, outs, in_spaces, scratch=(), out_space=pltpu.VMEM, mib=40):
+def call(body, outs, in_spaces, scratch=(), mib=40):
     return pl.pallas_call(
         body,
         out_shape=outs,
         in_specs=[pl.BlockSpec(memory_space=space) for space in in_spaces],
-        out_specs=[pl.BlockSpec(memory_space=out_space) for _ in outs],
+        out_specs=[pl.BlockSpec(memory_space=pltpu.VMEM) for _ in outs],
         scratch_shapes=list(scratch),
         compiler_params=pltpu.CompilerParams(vmem_limit_bytes=mib * 2**20),
     )
@@ -254,7 +235,7 @@
     width = tile_values.shape[-1]
     slots = tile_values.shape[2]
     f32 = jnp.float32
-    vm, sm, anywhere = pltpu.VMEM, pltpu.SMEM, pl.ANY
+    vm, sm = pltpu.VMEM, pltpu.SMEM
     halves = lax.axis_size("x")
     y, z, k = (lax.axis_index(axis) for axis in ("y", "z", "k"))
 
@@ -268,17 +249,9 @@
     keep, send = call(
         tile_products,
         [part, part],
-        [sm, anywhere] + [anywhere] * len(buffers),
-        [
-            vm((2 * halves, width, kstates), f32),
-            vm((slots, width, width), jnp.bfloat16),
-            vm((slots, width, kstates), jnp.bfloat16),
-            pltpu.SemaphoreType.DMA,
-            pltpu.SemaphoreType.DMA((slots,)),
-            pltpu.SemaphoreType.DMA((2,)),
-        ],
-        anywhere,
-        57,
+        [sm, vm] + [vm] * len(buffers),
+        [vm((2 * halves, width, kstates), f32)],
+        24,
     )(meta, tile_values[0, 0], *buffers)
     other = lax.ppermute(send, "k", [(0, 1), (1, 0)])
     parts = lax.all_to_all(keep + other, "x", 0, 0, tiled=True)

time: 214 us -> 209 us (0.977)
  starting transfers between devices: 67.1 us -> 70.8 us
  blocking collectives: 81.1 us -> 77.9 us
  Pallas kernels: 28.6 us -> 26.1 us
    ppermute x1, starting transfers between devices: 5.02 us -> 9.44 us  [per_device(): other = lax.ppermute(send, 'k', [(0, 1), (1, 0)])]
    all_to_all x4, blocking collectives: 55.9 us -> 52.7 us  [exchange(): lax.all_to_all(pieces, axes, 0, 0, axis_index_groups=groups, tiled=True)]
where the time goes in v5:
time: 209 us; the launch traced here: 208 us
  blocking collectives  77.9 us (37%)
  starting transfers between devices  70.8 us (34%)
  waiting for transfers between devices  28.1 us (13%)
  Pallas kernels  26.1 us (12%)
    all_to_all x4, blocking collectives, exchange(): lax.all_to_all(pieces, axes, 0, 0, axis_index_groups=groups, tiled=True)  52.7 us
    ppermute x7, starting transfers between devices, gather_states(): below[at].append(lax.ppermute(below[at][-1], axes, down))  38.2 us
    all_to_all x1, blocking collectives, gather_states(): lax.all_to_all(copies, axes, 0, 0, axis_index_groups=line_places(*sizes),...  25.2 us
    pallas_call x1, Pallas kernels, per_device(): call(factor_and_solve, [jax.ShapeDtypeStruct((own_rows, kstates), f32), j...  21.4 us
    all_to_all x1, waiting for transfers between devices, per_device(): parts = lax.all_to_all(keep + other, 'x', 0, 0, tiled=True)  14.4 us
    ppermute x7, starting transfers between devices, gather_states(): above[at].append(lax.ppermute(above[at][-1], axes, up))  13.4 us
    ppermute x1, starting transfers between devices, per_device(): other = lax.ppermute(send, 'k', [(0, 1), (1, 0)])  9.44 us
    ppermute x7, waiting for transfers between devices, gather_states(): above[at].append(lax.ppermute(above[at][-1], axes, up))  7.63 us
  transfers between devices with their start and end apart: 18, of which 7 were waited for; matrix products, arithmetic and copies ran while one was open for 0% of the time, Pallas kernels for 0%

profile of v5, /device:TPU:1, one launch (start us, length us, event | category | flops | bytes accessed | tf_op | source)
XLA Modules:
  0.0 208.3 jit_solution(13738323150246157303)
XLA Ops:
  1.6 25.2 %all_to_all.35 = bf16[8,128,512]{2,1,0:T(8,128)(2,1)S(1)} all-to-all(bf16[8,128,512]{2,1,0:T(8,128)(2,1)S(1)} %broadcast_in_dim.8), channel_id=1, replica_groups={{0,8,16,24,32,40,48,56},{1,65,129,193,257,321,385,449},{64,72,80,88,96,..., dimensions={0} | all-to-all | bytes 2097152 | tf_op jit(solution)/shard_map/all_to_all | solution.py:174
  26.9 10.8 %collective-permute-start.10 = (bf16[4,128,512]{2,1,0:T(8,128)(2,1)S(1)}, bf16[4,128,512]{2,1,0:T(8,128)(2,1)S(1)}, u32[]{:S(2)}, u32[]{:S(2)}) collective-permute-start(bf16[4,128,512]{2,1,0:T(8,128)(2,1)S(1)} %get-tuple-element.14.refs_8_), channel_id=1, source_target_pairs={{0,448},{1,57},{8,456},{9,1},{16,464},{17,9},{24,472},{25,17},{32,... | collective-permute-start | bytes 1572872 | tf_op jit(solution)/shard_map/ppermute | solution.py:184
  37.7 1.9 collective-permute-start
  39.6 4.6 %collective-permute-start.4 = (bf16[4,128,512]{2,1,0:T(8,128)(2,1)S(1)}, bf16[4,128,512]{2,1,0:T(8,128)(2,1)S(1)}, u32[]{:S(2)}, u32[]{:S(2)}) collective-permute-start(bf16[4,128,512]{2,1,0:T(8,128)(2,1)S(1)} %get-tuple-element.15.refs_0_), channel_id=1, source_target_pairs={{0,448},{1,57},{8,456},{9,1},{16,464},{17,9},{24,472},{25,17},{32,... | collective-permute-start | bytes 1572872 | tf_op jit(solution)/shard_map/ppermute | solution.py:184
  44.2 1.9 collective-permute-start.7
  46.2 4.6 %collective-permute-start.11 = (bf16[4,128,512]{2,1,0:T(8,128)(2,1)S(1)}, bf16[4,128,512]{2,1,0:T(8,128)(2,1)}, u32[]{:S(2)}, u32[]{:S(2)}) collective-permute-start(bf16[4,128,512]{2,1,0:T(8,128)(2,1)S(1)} %collective-permute-done.10.refs_15_), channel_id=1, source_target_pairs={{0,448},{1,57},{8,456},{9,1},{16,464},{17,9},{24,472},{25,17},{32,... | collective-permute-start | bytes 1572872 | tf_op jit(solution)/shard_map/ppermute | solution.py:184
  50.8 1.9 collective-permute-start.1
  52.7 4.6 %collective-permute-start.5 = (bf16[4,128,512]{2,1,0:T(8,128)(2,1)S(1)}, bf16[4,128,512]{2,1,0:T(8,128)(2,1)}, u32[]{:S(2)}, u32[]{:S(2)}) collective-permute-start(bf16[4,128,512]{2,1,0:T(8,128)(2,1)S(1)} %collective-permute-done.4.refs_7_), channel_id=1, source_target_pairs={{0,448},{1,57},{8,456},{9,1},{16,464},{17,9},{24,472},{25,17},{32,... | collective-permute-start | bytes 1572872 | tf_op jit(solution)/shard_map/ppermute | solution.py:184
  57.3 1.9 collective-permute-start.8
  59.2 4.6 %collective-permute-start.12 = (bf16[4,128,512]{2,1,0:T(8,128)(2,1)}, bf16[4,128,512]{2,1,0:T(8,128)(2,1)}, u32[]{:S(2)}, u32[]{:S(2)}) collective-permute-start(bf16[4,128,512]{2,1,0:T(8,128)(2,1)} %collective-permute-done.11.refs_14_), channel_id=1, source_target_pairs={{0,448},{1,57},{8,456},{9,1},{16,464},{17,9},{24,472},{25,17},{32,... | collective-permute-start | bytes 1572872 | tf_op jit(solution)/shard_map/ppermute | solution.py:184
  63.8 1.9 collective-permute-start.2
  66.4 4.6 %collective-permute-start.6 = (bf16[4,128,512]{2,1,0:T(8,128)(2,1)}, bf16[4,128,512]{2,1,0:T(8,128)(2,1)S(1)}, u32[]{:S(2)}, u32[]{:S(2)}) collective-permute-start(bf16[4,128,512]{2,1,0:T(8,128)(2,1)} %collective-permute-done.5.refs_6_), channel_id=1, source_target_pairs={{0,448},{1,57},{8,456},{9,1},{16,464},{17,9},{24,472},{25,17},{32,... | collective-permute-start | bytes 1572872 | tf_op jit(solution)/shard_map/ppermute | solution.py:184
  71.0 1.9 collective-permute-start.9
  73.0 4.6 %collective-permute-start.13 = (bf16[4,128,512]{2,1,0:T(8,128)(2,1)}, bf16[4,128,512]{2,1,0:T(8,128)(2,1)S(1)}, u32[]{:S(2)}, u32[]{:S(2)}) collective-permute-start(bf16[4,128,512]{2,1,0:T(8,128)(2,1)} %collective-permute-done.12.refs_13_), channel_id=1, source_target_pairs={{0,448},{1,57},{8,456},{9,1},{16,464},{17,9},{24,472},{25,17},{32,... | collective-permute-start | bytes 1572872 | tf_op jit(solution)/shard_map/ppermute | solution.py:184
  77.6 1.9 collective-permute-start.3
  80.3 2.4 %collective-permute-done.9.refs_11_ = bf16[4,128,512]{2,1,0:T(8,128)(2,1)S(1)} collective-permute-done((bf16[4,128,512]{2,1,0:T(8,128)(2,1)}, bf16[4,128,512]{2,1,0:T(8,128)(2,1)S(1)}, u32[]{:S(2)}, u32[]{:S(2)}) %collective-permute-start.9) | collective-permute-done | bytes 524320 | tf_op jit(solution)/shard_map/ppermute | solution.py:182
  82.7 1.3 collective-permute-done.13.refs_12_
  84.0 5.2 %collective-permute-done.3.refs_4_ = bf16[4,128,512]{2,1,0:T(8,128)(2,1)S(1)} collective-permute-done((bf16[4,128,512]{2,1,0:T(8,128)(2,1)}, bf16[4,128,512]{2,1,0:T(8,128)(2,1)S(1)}, u32[]{:S(2)}, u32[]{:S(2)}) %collective-permute-start.3) | collective-permute-done | bytes 524320 | tf_op jit(solution)/shard_map/ppermute | solution.py:182
  89.2 3.9 %shard_map.77 = (f32[4,128,512]{2,1,0:T(8,128)S(1)}, f32[4,128,512]{2,1,0:T(8,128)S(1)}) custom-call(s32[73]{0:T(128)S(1)} %pad_add_fusion.meta_ref, bf16[24,128,128]{2,1,0:T(8,128)(2,1)S(1)} %bitcast.39, bf16[4,128,512]{2,1,0:T(8,128)(2,1)S(1)} %get-tuple-element.15.refs_0_, bf16[4,128,512]{2,1,0:T(8,128)(2,1)S(1)} %collective-permute-done.refs_1_, ...), custom_call_target="tpu_custom_call" | custom-call | tf_op jit(solution)/shard_map/pallas_call | solution.py:249
  93.1 9.4 %collective-permute-start.14 = (f32[4,128,512]{2,1,0:T(8,128)S(1)}, f32[4,128,512]{2,1,0:T(8,128)S(1)}, u32[]{:S(2)}, u32[]{:S(2)}) collective-permute-start(f32[4,128,512]{2,1,0:T(8,128)S(1)} %get-tuple-element.8), channel_id=1, source_target_pairs={{0,1},{1,0},{2,3},{3,2},{4,5},{5,4},{6,7},{7,6},{8,9},{9,8},{10,11... | collective-permute-start | bytes 3145736 | tf_op jit(solution)/shard_map/ppermute | solution.py:256
  102.6 2.3 %collective-permute-done.14 = f32[4,128,512]{2,1,0:T(8,128)S(1)} collective-permute-done((f32[4,128,512]{2,1,0:T(8,128)S(1)}, f32[4,128,512]{2,1,0:T(8,128)S(1)}, u32[]{:S(2)}, u32[]{:S(2)}) %collective-permute-start.14) | collective-permute-done | bytes 1048608 | tf_op jit(solution)/shard_map/ppermute | solution.py:256
  106.0 3.9 %all-to-all-start.1 = ((f32[4,128,512]{2,1,0:T(8,128)}), f32[4,128,512]{2,1,0:T(8,128)S(1)}, u32[]{:S(2)}, u32[]{:S(2)}) async-start(f32[4,128,512]{2,1,0:T(8,128)} %add.47), calls=%async_computation.1 | async-start | bytes 2097152 | tf_op jit(solution)/shard_map/all_to_all | solution.py:257
  110.0 14.4 %all-to-all-done.1.parts_ref = f32[4,128,512]{2,1,0:T(8,128)S(1)} async-done(((f32[4,128,512]{2,1,0:T(8,128)}), f32[4,128,512]{2,1,0:T(8,128)S(1)}, u32[]{:S(2)}, u32[]{:S(2)}) %all-to-all-start.1) | async-done | bytes 1048608 | tf_op jit(solution)/shard_map/all_to_all | solution.py:257
  125.3 3.4 %collective-permute-start.15 = (f32[5,128,128]{2,1,0:T(8,128)S(1)}, f32[5,128,128]{2,1,0:T(8,128)S(1)}, u32[]{:S(2)}, u32[]{:S(2)}) collective-permute-start(f32[5,128,128]{2,1,0:T(8,128)S(1)} %get-tuple-element.10), channel_id=1, source_target_pairs={{0,1},{1,0},{2,3},{3,2},{4,5},{5,4},{6,7},{7,6},{8,9},{9,8},{10,11... | collective-permute-start | bytes 983048 | tf_op jit(solution)/shard_map/ppermute | solution.py:267
  128.7 1.2 collective-permute-done.15
  130.0 7.8 %all_to_all.36 = f32[4,160,128]{2,1,0:T(8,128)S(1)} all-to-all(f32[4,160,128]{2,1,0:T(8,128)S(1)} %bitcast.40), channel_id=1, replica_groups={{0,2,4,6},{8,10,12,14},{16,18,20,22},{24,26,28,30},{32,34,36,38},{40,42..., dimensions={0} | all-to-all | bytes 655360 | tf_op jit(solution)/shard_map/all_to_all | solution.py:222
  137.9 19.1 %all_to_all.37 = f32[64,1,320]{2,1,0:T(1,128)S(1)} all-to-all(f32[64,1,320]{2,1,0:T(1,128)S(1)} %all_to_all.25), channel_id=1, replica_groups={{0,8,16,24,32,40,48,56,64,72,80,88,96,104,112,120,128,136,144,152,160,1..., dimensions={0} | all-to-all | bytes 163840 | tf_op jit(solution)/shard_map/all_to_all | solution.py:222
  157.2 18.0 %all_to_all.38 = f32[64,1,320]{2,1,0:T(1,128)S(1)} all-to-all(f32[64,1,320]{2,1,0:T(1,128)S(1)} %broadcast_in_dim.9), channel_id=1, replica_groups={{0,8,16,24,32,40,48,56,64,72,80,88,96,104,112,120,128,136,144,152,160,1..., dimensions={0} | all-to-all | bytes 163840 | tf_op jit(solution)/shard_map/all_to_all | solution.py:222
  175.6 7.8 %all_to_all.39 = f32[4,160,128]{2,1,0:T(8,128)S(1)} all-to-all(f32[4,160,128]{2,1,0:T(8,128)S(1)} %broadcast_in_dim.11), channel_id=1, replica_groups={{0,2,4,6},{8,10,12,14},{16,18,20,22},{24,26,28,30},{32,34,36,38},{40,42..., dimensions={0} | all-to-all | bytes 655360 | tf_op jit(solution)/shard_map/all_to_all | solution.py:222
  183.3 2.4 %collective-permute-start.16 = (f32[5,128,128]{2,1,0:T(8,128)S(1)}, f32[5,128,128]{2,1,0:T(8,128)S(1)}, u32[]{:S(2)}, u32[]{:S(2)}) collective-permute-start(f32[5,128,128]{2,1,0:T(8,128)S(1)} %bitcast.37), channel_id=1, source_target_pairs={{0,1},{1,0},{2,3},{3,2},{4,5},{5,4},{6,7},{7,6},{8,9},{9,8},{10,11... | collective-permute-start | bytes 983048 | tf_op jit(solution)/shard_map/ppermute | solution.py:268
  185.7 1.2 collective-permute-done.16.other_ref
  187.0 21.4 %shard_map.79 = (f32[128,512]{1,0:T(8,128)}, f32[512,512]{1,0:T(8,128)}) custom-call(s32[1]{0:T(128)} %bitcast.core_ref, f32[5,128,128]{2,1,0:T(8,128)S(1)} %bitcast.38, f32[5,128,128]{2,1,0:T(8,128)S(1)} %collective-permute-done.16.other_ref, f32[128,512]{1,0:T(8,128)S(1)} %get-tuple-element.11.applied_ref), custom_call_target="tpu_custom_call" | custom-call | tf_op jit(solution)/shard_map/pallas_call | solution.py:270
  (37 shorter events, 4.6 us)
Async XLA Ops:
  26.8 62.4 %copy-start = (bf16[1,1,24,128,128]{4,3,2,1,0:T(8,128)(2,1)S(1)}, bf16[1,1,24,128,128]{4,3,2,1,0:T(8,128)(2,1)}, u32[]{:S(2)}) copy-start(bf16[1,1,24,128,128]{4,3,2,1,0:T(8,128)(2,1)} %param.8) | copy-start | bytes 2359300
  26.9 19.2 %collective-permute-start.10 = (bf16[4,128,512]{2,1,0:T(8,128)(2,1)S(1)}, bf16[4,128,512]{2,1,0:T(8,128)(2,1)S(1)}, u32[]{:S(2)}, u32[]{:S(2)}) collective-permute-start(bf16[4,128,512]{2,1,0:T(8,128)(2,1)S(1)} %get-tuple-element.14.refs_8_), channel_id=1, source_target_pairs={{0,448},{1,57},{8,456},{9,1},{16,464},{17,9},{24,472},{25,17},{32,... | collective-permute-start | bytes 1572872 | tf_op jit(solution)/shard_map/ppermute | solution.py:184
  37.7 13.0 %collective-permute-start = (bf16[4,128,512]{2,1,0:T(8,128)(2,1)S(1)}, bf16[4,128,512]{2,1,0:T(8,128)(2,1)S(1)}, u32[]{:S(2)}, u32[]{:S(2)}) collective-permute-start(bf16[4,128,512]{2,1,0:T(8,128)(2,1)S(1)} %get-tuple-element.15.refs_0_), channel_id=1, source_target_pairs={{0,64},{1,9},{8,72},{9,17},{16,80},{17,25},{24,88},{25,33},{32,96}... | collective-permute-start | bytes 1572872 | tf_op jit(solution)/shard_map/ppermute | solution.py:182
  39.6 13.0 %collective-permute-start.4 = (bf16[4,128,512]{2,1,0:T(8,128)(2,1)S(1)}, bf16[4,128,512]{2,1,0:T(8,128)(2,1)S(1)}, u32[]{:S(2)}, u32[]{:S(2)}) collective-permute-start(bf16[4,128,512]{2,1,0:T(8,128)(2,1)S(1)} %get-tuple-element.15.refs_0_), channel_id=1, source_target_pairs={{0,448},{1,57},{8,456},{9,1},{16,464},{17,9},{24,472},{25,17},{32,... | collective-permute-start | bytes 1572872 | tf_op jit(solution)/shard_map/ppermute | solution.py:184
  44.2 13.1 %collective-permute-start.7 = (bf16[4,128,512]{2,1,0:T(8,128)(2,1)S(1)}, bf16[4,128,512]{2,1,0:T(8,128)(2,1)}, u32[]{:S(2)}, u32[]{:S(2)}) collective-permute-start(bf16[4,128,512]{2,1,0:T(8,128)(2,1)S(1)} %get-tuple-element.14.refs_8_), channel_id=1, source_target_pairs={{0,64},{1,9},{8,72},{9,17},{16,80},{17,25},{24,88},{25,33},{32,96}... | collective-permute-start | bytes 1572872 | tf_op jit(solution)/shard_map/ppermute | solution.py:182
  46.2 13.1 %collective-permute-start.11 = (bf16[4,128,512]{2,1,0:T(8,128)(2,1)S(1)}, bf16[4,128,512]{2,1,0:T(8,128)(2,1)}, u32[]{:S(2)}, u32[]{:S(2)}) collective-permute-start(bf16[4,128,512]{2,1,0:T(8,128)(2,1)S(1)} %collective-permute-done.10.refs_15_), channel_id=1, source_target_pairs={{0,448},{1,57},{8,456},{9,1},{16,464},{17,9},{24,472},{25,17},{32,... | collective-permute-start | bytes 1572872 | tf_op jit(solution)/shard_map/ppermute | solution.py:184
  50.8 13.1 %collective-permute-start.1 = (bf16[4,128,512]{2,1,0:T(8,128)(2,1)S(1)}, bf16[4,128,512]{2,1,0:T(8,128)(2,1)}, u32[]{:S(2)}, u32[]{:S(2)}) collective-permute-start(bf16[4,128,512]{2,1,0:T(8,128)(2,1)S(1)} %collective-permute-done.refs_1_), channel_id=1, source_target_pairs={{0,64},{1,9},{8,72},{9,17},{16,80},{17,25},{24,88},{25,33},{32,96}... | collective-permute-start | bytes 1572872 | tf_op jit(solution)/shard_map/ppermute | solution.py:182
  52.7 13.7 %collective-permute-start.5 = (bf16[4,128,512]{2,1,0:T(8,128)(2,1)S(1)}, bf16[4,128,512]{2,1,0:T(8,128)(2,1)}, u32[]{:S(2)}, u32[]{:S(2)}) collective-permute-start(bf16[4,128,512]{2,1,0:T(8,128)(2,1)S(1)} %collective-permute-done.4.refs_7_), channel_id=1, source_target_pairs={{0,448},{1,57},{8,456},{9,1},{16,464},{17,9},{24,472},{25,17},{32,... | collective-permute-start | bytes 1572872 | tf_op jit(solution)/shard_map/ppermute | solution.py:184
  57.3 13.7 %collective-permute-start.8 = (bf16[4,128,512]{2,1,0:T(8,128)(2,1)}, bf16[4,128,512]{2,1,0:T(8,128)(2,1)}, u32[]{:S(2)}, u32[]{:S(2)}) collective-permute-start(bf16[4,128,512]{2,1,0:T(8,128)(2,1)} %collective-permute-done.7.refs_9_), channel_id=1, source_target_pairs={{0,64},{1,9},{8,72},{9,17},{16,80},{17,25},{24,88},{25,33},{32,96}... | collective-permute-start | bytes 1572872 | tf_op jit(solution)/shard_map/ppermute | solution.py:182
  59.2 13.7 %collective-permute-start.12 = (bf16[4,128,512]{2,1,0:T(8,128)(2,1)}, bf16[4,128,512]{2,1,0:T(8,128)(2,1)}, u32[]{:S(2)}, u32[]{:S(2)}) collective-permute-start(bf16[4,128,512]{2,1,0:T(8,128)(2,1)} %collective-permute-done.11.refs_14_), channel_id=1, source_target_pairs={{0,448},{1,57},{8,456},{9,1},{16,464},{17,9},{24,472},{25,17},{32,... | collective-permute-start | bytes 1572872 | tf_op jit(solution)/shard_map/ppermute | solution.py:184
  63.8 13.7 %collective-permute-start.2 = (bf16[4,128,512]{2,1,0:T(8,128)(2,1)}, bf16[4,128,512]{2,1,0:T(8,128)(2,1)}, u32[]{:S(2)}, u32[]{:S(2)}) collective-permute-start(bf16[4,128,512]{2,1,0:T(8,128)(2,1)} %collective-permute-done.1.refs_2_), channel_id=1, source_target_pairs={{0,64},{1,9},{8,72},{9,17},{16,80},{17,25},{24,88},{25,33},{32,96}... | collective-permute-start | bytes 1572872 | tf_op jit(solution)/shard_map/ppermute | solution.py:182
  66.4 13.1 %copy-start.2 = (s32[1,1,24]{2,1,0:T(1,128)S(1)}, s32[1,1,24]{2,1,0:T(1,128)}, u32[]{:S(2)}) copy-start(s32[1,1,24]{2,1,0:T(1,128)} %param.10) | copy-start | bytes 292
  66.4 13.8 %collective-permute-start.6 = (bf16[4,128,512]{2,1,0:T(8,128)(2,1)}, bf16[4,128,512]{2,1,0:T(8,128)(2,1)S(1)}, u32[]{:S(2)}, u32[]{:S(2)}) collective-permute-start(bf16[4,128,512]{2,1,0:T(8,128)(2,1)} %collective-permute-done.5.refs_6_), channel_id=1, source_target_pairs={{0,448},{1,57},{8,456},{9,1},{16,464},{17,9},{24,472},{25,17},{32,... | collective-permute-start | bytes 1572872 | tf_op jit(solution)/shard_map/ppermute | solution.py:184
  71.0 11.6 %collective-permute-start.9 = (bf16[4,128,512]{2,1,0:T(8,128)(2,1)}, bf16[4,128,512]{2,1,0:T(8,128)(2,1)S(1)}, u32[]{:S(2)}, u32[]{:S(2)}) collective-permute-start(bf16[4,128,512]{2,1,0:T(8,128)(2,1)} %collective-permute-done.8.refs_10_), channel_id=1, source_target_pairs={{0,64},{1,9},{8,72},{9,17},{16,80},{17,25},{24,88},{25,33},{32,96}... | collective-permute-start | bytes 1572872 | tf_op jit(solution)/shard_map/ppermute | solution.py:182
  73.0 11.0 %collective-permute-start.13 = (bf16[4,128,512]{2,1,0:T(8,128)(2,1)}, bf16[4,128,512]{2,1,0:T(8,128)(2,1)S(1)}, u32[]{:S(2)}, u32[]{:S(2)}) collective-permute-start(bf16[4,128,512]{2,1,0:T(8,128)(2,1)} %collective-permute-done.12.refs_13_), channel_id=1, source_target_pairs={{0,448},{1,57},{8,456},{9,1},{16,464},{17,9},{24,472},{25,17},{32,... | collective-permute-start | bytes 1572872 | tf_op jit(solution)/shard_map/ppermute | solution.py:184
  77.6 11.6 %collective-permute-start.3 = (bf16[4,128,512]{2,1,0:T(8,128)(2,1)}, bf16[4,128,512]{2,1,0:T(8,128)(2,1)S(1)}, u32[]{:S(2)}, u32[]{:S(2)}) collective-permute-start(bf16[4,128,512]{2,1,0:T(8,128)(2,1)} %collective-permute-done.2.refs_3_), channel_id=1, source_target_pairs={{0,64},{1,9},{8,72},{9,17},{16,80},{17,25},{24,88},{25,33},{32,96}... | collective-permute-start | bytes 1572872 | tf_op jit(solution)/shard_map/ppermute | solution.py:182
  79.5 0.7 copy-start.4
  93.1 11.7 %collective-permute-start.14 = (f32[4,128,512]{2,1,0:T(8,128)S(1)}, f32[4,128,512]{2,1,0:T(8,128)S(1)}, u32[]{:S(2)}, u32[]{:S(2)}) collective-permute-start(f32[4,128,512]{2,1,0:T(8,128)S(1)} %get-tuple-element.8), channel_id=1, source_target_pairs={{0,1},{1,0},{2,3},{3,2},{4,5},{5,4},{6,7},{7,6},{8,9},{9,8},{10,11... | collective-permute-start | bytes 3145736 | tf_op jit(solution)/shard_map/ppermute | solution.py:256
  106.0 3.9 %copy-start.1 = (bf16[128,512]{1,0:T(8,128)(2,1)S(1)}, bf16[128,512]{1,0:T(8,128)(2,1)}, u32[]{:S(2)}) copy-start(bf16[128,512]{1,0:T(8,128)(2,1)} %param.6) | copy-start | bytes 393220
  106.0 3.9 %copy-start.3 = (f32[128]{0:T(128)S(1)}, f32[128]{0:T(128)}, u32[]{:S(2)}) copy-start(f32[128]{0:T(128)} %param.7) | copy-start | bytes 1540
  106.0 18.4 %all-to-all-start.1 = ((f32[4,128,512]{2,1,0:T(8,128)}), f32[4,128,512]{2,1,0:T(8,128)S(1)}, u32[]{:S(2)}, u32[]{:S(2)}) async-start(f32[4,128,512]{2,1,0:T(8,128)} %add.47), calls=%async_computation.1 | async-start | bytes 2097152 | tf_op jit(solution)/shard_map/all_to_all | solution.py:257
  125.3 4.7 %collective-permute-start.15 = (f32[5,128,128]{2,1,0:T(8,128)S(1)}, f32[5,128,128]{2,1,0:T(8,128)S(1)}, u32[]{:S(2)}, u32[]{:S(2)}) collective-permute-start(f32[5,128,128]{2,1,0:T(8,128)S(1)} %get-tuple-element.10), channel_id=1, source_target_pairs={{0,1},{1,0},{2,3},{3,2},{4,5},{5,4},{6,7},{7,6},{8,9},{9,8},{10,11... | collective-permute-start | bytes 983048 | tf_op jit(solution)/shard_map/ppermute | solution.py:267
  183.3 3.6 %collective-permute-start.16 = (f32[5,128,128]{2,1,0:T(8,128)S(1)}, f32[5,128,128]{2,1,0:T(8,128)S(1)}, u32[]{:S(2)}, u32[]{:S(2)}) collective-permute-start(f32[5,128,128]{2,1,0:T(8,128)S(1)} %bitcast.37), channel_id=1, source_target_pairs={{0,1},{1,0},{2,3},{3,2},{4,5},{5,4},{6,7},{7,6},{8,9},{9,8},{10,11... | collective-permute-start | bytes 983048 | tf_op jit(solution)/shard_map/ppermute | solution.py:268

commit v6 on v5

--- a/solution.py
+++ b/solution.py
@@ -16,27 +16,32 @@
     return lax.dot_general(left, right, dims, precision=FULL, preferred_element_type=jnp.float32)
 
 
-def tile_products(meta_ref, tiles_ref, *refs):
-    *sources, keep_ref, send_ref, sums = refs
-    slots = tiles_ref.shape[0]
-    per_core = keep_ref.shape[0]
-    sums[...] = jnp.zeros_like(sums)
-
-    def add(t, which, first, last):
+def tile_products(ids, first_place, based, meta_ref, tiles_ref, *refs):
+    sources, out_ref = refs[:len(ids)], refs[-1]
+    slots, places = tiles_ref.shape[0], out_ref.shape[0]
+    if based:
+        out_ref[...] = refs[-2][first_place:first_place + places]
+    else:
+        out_ref[...] = jnp.zeros_like(out_ref)
+
+    def add(t, place, which, first, last):
         if last - first == 1:
-            block = sources[first][meta_ref[2 * slots + t]]
-            sums[meta_ref[t]] += jnp.dot(tiles_ref[t], block, preferred_element_type=jnp.float32)
+            @pl.when(which == ids[first])
+            def _():
+                block = sources[first][meta_ref[2 * slots + t]]
+                out_ref[place] += jnp.dot(tiles_ref[t], block, preferred_element_type=jnp.float32)
             return
         middle = (first + last) // 2
-        pl.when(which < middle)(lambda: add(t, which, first, middle))
-        pl.when(which >= middle)(lambda: add(t, which, middle, last))
+        pl.when(which < ids[middle])(lambda: add(t, place, which, first, middle))
+        pl.when(which >= ids[middle])(lambda: add(t, place, which, middle, last))
 
     @pl.loop(0, meta_ref[3 * slots])
     def _(t):
-        add(t, meta_ref[slots + t], 0, len(sources))
-
-    keep_ref[...] = sums[:per_core]
-    send_ref[...] = sums[per_core:]
+        place = meta_ref[t] - first_place
+
+        @pl.when((place >= 0) & (place < places))
+        def _():
+            add(t, place, meta_ref[slots + t], 0, len(ids))
 
 
 def upper_pairs(nblocks):
@@ -82,15 +87,15 @@
             pivot = spread(cols[k], k)
             recip = 1.0 / pivot
             at = sub == k
-            both = jnp.where(at, -1.0, cols[k])
-            below = jnp.where(sub > k, cols[k], 0.0)
+            both = jnp.where(at, -1.0, cols[k]) * recip
+            below = jnp.where(sub > k, cols[k], 0.0) * recip
             for b in range(k + 1, STRIP):
-                cols[b] = jnp.where(at, 0.0, cols[b]) - (both * spread(cols[b], k)) * recip
+                cols[b] = jnp.where(at, 0.0, cols[b]) - both * spread(cols[b], k)
             row_a, row_e = spread(full_a, k), spread(full_e, k)
-            down_a = down_a - (below * spread(down_a, k)) * recip
-            down_e = down_e - (below * spread(down_e, k)) * recip
-            full_a = jnp.where(at, 0.0, full_a) - (both * row_a) * recip
-            full_e = jnp.where(at, 0.0, full_e) - (both * row_e) * recip
+            down_a = down_a - below * spread(down_a, k)
+            down_e = down_e - below * spread(down_e, k)
+            full_a = jnp.where(at, 0.0, full_a) - both * row_a
+            full_e = jnp.where(at, 0.0, full_e) - both * row_e
             pivots = pivot if pivots is None else jnp.where(sub >= k, pivot, pivots)
         scale = lax.rsqrt(pivots)
         u_ref[base + first:base + first + STRIP, base:base + n] = jnp.where(lane >= sub + first, down_a * scale, 0.0)
@@ -245,15 +250,23 @@
     local = onsite[:, None] * vectors.astype(f32)
     buffers = gather_states(vectors)
 
-    part = jax.ShapeDtypeStruct((halves, width, kstates), f32)
-    keep, send = call(
-        tile_products,
-        [part, part],
-        [sm, vm] + [vm] * len(buffers),
-        [vm((2 * halves, width, kstates), f32)],
-        24,
-    )(meta, tile_values[0, 0], *buffers)
+    tiles = tile_values[0, 0]
+    late = [4, 5, 11, 12]
+    early = [at for at in range(len(buffers)) if at not in late]
+
+    def products(ids, first_place, places, *base):
+        return call(
+            functools.partial(tile_products, ids, first_place, bool(base)),
+            [jax.ShapeDtypeStruct((places, width, kstates), f32)],
+            [sm, vm] + [vm] * (len(ids) + len(base)),
+            (),
+            24,
+        )(meta, tiles, *[buffers[at] for at in ids], *base)[0]
+
+    sums = products(early, 0, 2 * halves)
+    send = products(late, halves, halves, sums)
     other = lax.ppermute(send, "k", [(0, 1), (1, 0)])
+    keep = products(late, 0, halves, sums)
     parts = lax.all_to_all(keep + other, "x", 0, 0, tiled=True)
 
     nblocks = kstates // width

time: 209 us -> 204 us (0.976)
  waiting for transfers between devices: 28.1 us -> 24.2 us
  starting transfers between devices: 70.8 us -> 68.1 us
    ppermute x1, starting transfers between devices: 9.44 us -> 6.31 us  [per_device(): other = lax.ppermute(send, 'k', [(0, 1), (1, 0)])]
    ppermute x7, waiting for transfers between devices: 7.63 us -> 5.25 us  [gather_states(): above[at].append(lax.ppermute(above[at][-1], axes, up))]
    pallas_call x1 -> x3, Pallas kernels: 3.92 us -> 5.4 us  [products(): call(functools.partial(tile_products, ids, first_place, bool(base)), [jax...]
  transfers between devices with their start and end apart: 18 -> 18, of which waited for: 7 -> 6; matrix products, arithmetic and copies ran while one was open for 0% -> 0% of each run, Pallas kernels for 0% -> 2%
where the time goes in v6:
time: 204 us; the launch traced here: 203 us
  blocking collectives  77.8 us (38%)
  starting transfers between devices  68.1 us (33%)
  Pallas kernels  27.9 us (14%)
  waiting for transfers between devices  24.2 us (12%)
    all_to_all x4, blocking collectives, exchange(): lax.all_to_all(pieces, axes, 0, 0, axis_index_groups=groups, tiled=True)  52.5 us
    ppermute x7, starting transfers between devices, gather_states(): below[at].append(lax.ppermute(below[at][-1], axes, down))  38.1 us
    all_to_all x1, blocking collectives, gather_states(): lax.all_to_all(copies, axes, 0, 0, axis_index_groups=line_places(*sizes),...  25.3 us
    pallas_call x1, Pallas kernels, per_device(): call(factor_and_solve, [jax.ShapeDtypeStruct((own_rows, kstates), f32), j...  21.7 us
    all_to_all x1, waiting for transfers between devices, per_device(): parts = lax.all_to_all(keep + other, 'x', 0, 0, tiled=True)  14.4 us
    ppermute x7, starting transfers between devices, gather_states(): above[at].append(lax.ppermute(above[at][-1], axes, up))  13.4 us
    ppermute x1, starting transfers between devices, per_device(): other = lax.ppermute(send, 'k', [(0, 1), (1, 0)])  6.31 us
    pallas_call x3, Pallas kernels, products(): call(functools.partial(tile_products, ids, first_place, bool(base)), [jax...  5.4 us
  transfers between devices with their start and end apart: 18, of which 6 were waited for; matrix products, arithmetic and copies ran while one was open for 0% of the time, Pallas kernels for 2%

profile of v6, /device:TPU:1, one launch (start us, length us, event | category | flops | bytes accessed | tf_op | source)
XLA Modules:
  0.0 202.8 jit_solution(255572395556519928)
XLA Ops:
  0.6 1.0 broadcast_in_dim.8
  1.7 25.3 %all_to_all.35 = bf16[8,128,512]{2,1,0:T(8,128)(2,1)S(1)} all-to-all(bf16[8,128,512]{2,1,0:T(8,128)(2,1)S(1)} %broadcast_in_dim.8), channel_id=1, replica_groups={{0,8,16,24,32,40,48,56},{1,65,129,193,257,321,385,449},{64,72,80,88,96,..., dimensions={0} | all-to-all | bytes 2097152 | tf_op jit(solution)/shard_map/all_to_all | solution.py:179
  27.1 10.7 %collective-permute-start.10 = (bf16[4,128,512]{2,1,0:T(8,128)(2,1)S(1)}, bf16[4,128,512]{2,1,0:T(8,128)(2,1)S(1)}, u32[]{:S(2)}, u32[]{:S(2)}) collective-permute-start(bf16[4,128,512]{2,1,0:T(8,128)(2,1)S(1)} %get-tuple-element.10.refs_6_), channel_id=1, source_target_pairs={{0,448},{1,57},{8,456},{9,1},{16,464},{17,9},{24,472},{25,17},{32,... | collective-permute-start | bytes 1572872 | tf_op jit(solution)/shard_map/ppermute | solution.py:189
  37.7 1.9 collective-permute-start
  39.7 4.6 %collective-permute-start.4 = (bf16[4,128,512]{2,1,0:T(8,128)(2,1)S(1)}, bf16[4,128,512]{2,1,0:T(8,128)(2,1)S(1)}, u32[]{:S(2)}, u32[]{:S(2)}) collective-permute-start(bf16[4,128,512]{2,1,0:T(8,128)(2,1)S(1)} %get-tuple-element.11.refs_0_), channel_id=1, source_target_pairs={{0,448},{1,57},{8,456},{9,1},{16,464},{17,9},{24,472},{25,17},{32,... | collective-permute-start | bytes 1572872 | tf_op jit(solution)/shard_map/ppermute | solution.py:189
  44.3 1.9 collective-permute-start.7
  46.2 4.6 %collective-permute-start.11 = (bf16[4,128,512]{2,1,0:T(8,128)(2,1)S(1)}, bf16[4,128,512]{2,1,0:T(8,128)(2,1)}, u32[]{:S(2)}, u32[]{:S(2)}) collective-permute-start(bf16[4,128,512]{2,1,0:T(8,128)(2,1)S(1)} %collective-permute-done.10.refs_11_), channel_id=1, source_target_pairs={{0,448},{1,57},{8,456},{9,1},{16,464},{17,9},{24,472},{25,17},{32,... | collective-permute-start | bytes 1572872 | tf_op jit(solution)/shard_map/ppermute | solution.py:189
  50.8 1.9 collective-permute-start.1
  52.7 4.6 %collective-permute-start.5 = (bf16[4,128,512]{2,1,0:T(8,128)(2,1)S(1)}, bf16[4,128,512]{2,1,0:T(8,128)(2,1)}, u32[]{:S(2)}, u32[]{:S(2)}) collective-permute-start(bf16[4,128,512]{2,1,0:T(8,128)(2,1)S(1)} %collective-permute-done.4.refs_5_), channel_id=1, source_target_pairs={{0,448},{1,57},{8,456},{9,1},{16,464},{17,9},{24,472},{25,17},{32,... | collective-permute-start | bytes 1572872 | tf_op jit(solution)/shard_map/ppermute | solution.py:189
  57.3 1.9 collective-permute-start.8
  59.3 4.6 %collective-permute-start.12 = (bf16[4,128,512]{2,1,0:T(8,128)(2,1)}, bf16[4,128,512]{2,1,0:T(8,128)(2,1)}, u32[]{:S(2)}, u32[]{:S(2)}) collective-permute-start(bf16[4,128,512]{2,1,0:T(8,128)(2,1)} %collective-permute-done.11.refs_10_), channel_id=1, source_target_pairs={{0,448},{1,57},{8,456},{9,1},{16,464},{17,9},{24,472},{25,17},{32,... | collective-permute-start | bytes 1572872 | tf_op jit(solution)/shard_map/ppermute | solution.py:189
  63.9 1.9 collective-permute-start.2
  66.5 4.6 %collective-permute-start.6 = (bf16[4,128,512]{2,1,0:T(8,128)(2,1)}, bf16[4,128,512]{2,1,0:T(8,128)(2,1)S(1)}, u32[]{:S(2)}, u32[]{:S(2)}) collective-permute-start(bf16[4,128,512]{2,1,0:T(8,128)(2,1)} %collective-permute-done.5.refs_4_), channel_id=1, source_target_pairs={{0,448},{1,57},{8,456},{9,1},{16,464},{17,9},{24,472},{25,17},{32,... | collective-permute-start | bytes 1572872 | tf_op jit(solution)/shard_map/ppermute | solution.py:189
  71.0 1.9 collective-permute-start.9
  73.0 4.6 %collective-permute-start.13 = (bf16[4,128,512]{2,1,0:T(8,128)(2,1)}, bf16[4,128,512]{2,1,0:T(8,128)(2,1)S(1)}, u32[]{:S(2)}, u32[]{:S(2)}) collective-permute-start(bf16[4,128,512]{2,1,0:T(8,128)(2,1)} %collective-permute-done.12.refs_9_), channel_id=1, source_target_pairs={{0,448},{1,57},{8,456},{9,1},{16,464},{17,9},{24,472},{25,17},{32,... | collective-permute-start | bytes 1572872 | tf_op jit(solution)/shard_map/ppermute | solution.py:189
  77.6 1.9 collective-permute-start.3
  79.6 3.6 %shard_map.77.refs_4_ = f32[8,128,512]{2,1,0:T(8,128)S(1)} custom-call(s32[73]{0:T(128)S(1)} %pad_add_fusion.meta_ref, bf16[24,128,128]{2,1,0:T(8,128)(2,1)S(1)} %bitcast.37, bf16[4,128,512]{2,1,0:T(8,128)(2,1)S(1)} %get-tuple-element.11.refs_0_, bf16[4,128,512]{2,1,0:T(8,128)(2,1)S(1)} %collective-permute-done.refs_1_, ...), custom_call_target="tpu_custom_call" | custom-call | tf_op jit(solution)/shard_map/pallas_call | solution.py:258
  84.0 5.2 %collective-permute-done.3.refs_0_ = bf16[4,128,512]{2,1,0:T(8,128)(2,1)S(1)} collective-permute-done((bf16[4,128,512]{2,1,0:T(8,128)(2,1)}, bf16[4,128,512]{2,1,0:T(8,128)(2,1)S(1)}, u32[]{:S(2)}, u32[]{:S(2)}) %collective-permute-start.3) | collective-permute-done | bytes 524320 | tf_op jit(solution)/shard_map/ppermute | solution.py:187
  90.2 6.3 %collective-permute-start.14 = (f32[4,128,512]{2,1,0:T(8,128)S(1)}, f32[4,128,512]{2,1,0:T(8,128)S(1)}, u32[]{:S(2)}, u32[]{:S(2)}) collective-permute-start(f32[4,128,512]{2,1,0:T(8,128)S(1)} %shard_map.79), channel_id=1, source_target_pairs={{0,1},{1,0},{2,3},{3,2},{4,5},{5,4},{6,7},{7,6},{8,9},{9,8},{10,11... | collective-permute-start | bytes 3145736 | tf_op jit(solution)/shard_map/ppermute | solution.py:268
  97.3 1.4 collective-permute-done.14
  98.7 1.2 add.47
  99.9 4.3 %all-to-all-start.1 = ((f32[4,128,512]{2,1,0:T(8,128)}), f32[4,128,512]{2,1,0:T(8,128)S(1)}, u32[]{:S(2)}, u32[]{:S(2)}) async-start(f32[4,128,512]{2,1,0:T(8,128)} %add.47), calls=%async_computation.1 | async-start | bytes 2097152 | tf_op jit(solution)/shard_map/all_to_all | solution.py:270
  104.3 14.4 %all-to-all-done.1.parts_ref = f32[4,128,512]{2,1,0:T(8,128)S(1)} async-done(((f32[4,128,512]{2,1,0:T(8,128)}), f32[4,128,512]{2,1,0:T(8,128)S(1)}, u32[]{:S(2)}, u32[]{:S(2)}) %all-to-all-start.1) | async-done | bytes 1048608 | tf_op jit(solution)/shard_map/all_to_all | solution.py:270
  119.5 3.4 %collective-permute-start.15 = (f32[5,128,128]{2,1,0:T(8,128)S(1)}, f32[5,128,128]{2,1,0:T(8,128)S(1)}, u32[]{:S(2)}, u32[]{:S(2)}) collective-permute-start(f32[5,128,128]{2,1,0:T(8,128)S(1)} %get-tuple-element.6), channel_id=1, source_target_pairs={{0,1},{1,0},{2,3},{3,2},{4,5},{5,4},{6,7},{7,6},{8,9},{9,8},{10,11... | collective-permute-start | bytes 983048 | tf_op jit(solution)/shard_map/ppermute | solution.py:280
  122.9 1.2 collective-permute-done.15
  124.2 7.8 %all_to_all.36 = f32[4,160,128]{2,1,0:T(8,128)S(1)} all-to-all(f32[4,160,128]{2,1,0:T(8,128)S(1)} %bitcast.42), channel_id=1, replica_groups={{0,2,4,6},{8,10,12,14},{16,18,20,22},{24,26,28,30},{32,34,36,38},{40,42..., dimensions={0} | all-to-all | bytes 655360 | tf_op jit(solution)/shard_map/all_to_all | solution.py:227
  132.1 18.8 %all_to_all.37 = f32[64,1,320]{2,1,0:T(1,128)S(1)} all-to-all(f32[64,1,320]{2,1,0:T(1,128)S(1)} %all_to_all.25), channel_id=1, replica_groups={{0,8,16,24,32,40,48,56,64,72,80,88,96,104,112,120,128,136,144,152,160,1..., dimensions={0} | all-to-all | bytes 163840 | tf_op jit(solution)/shard_map/all_to_all | solution.py:227
  151.1 18.2 %all_to_all.38 = f32[64,1,320]{2,1,0:T(1,128)S(1)} all-to-all(f32[64,1,320]{2,1,0:T(1,128)S(1)} %broadcast_in_dim.9), channel_id=1, replica_groups={{0,8,16,24,32,40,48,56,64,72,80,88,96,104,112,120,128,136,144,152,160,1..., dimensions={0} | all-to-all | bytes 163840 | tf_op jit(solution)/shard_map/all_to_all | solution.py:227
  169.6 7.8 %all_to_all.39 = f32[4,160,128]{2,1,0:T(8,128)S(1)} all-to-all(f32[4,160,128]{2,1,0:T(8,128)S(1)} %broadcast_in_dim.11), channel_id=1, replica_groups={{0,2,4,6},{8,10,12,14},{16,18,20,22},{24,26,28,30},{32,34,36,38},{40,42..., dimensions={0} | all-to-all | bytes 655360 | tf_op jit(solution)/shard_map/all_to_all | solution.py:227
  177.4 2.5 %collective-permute-start.16 = (f32[5,128,128]{2,1,0:T(8,128)S(1)}, f32[5,128,128]{2,1,0:T(8,128)S(1)}, u32[]{:S(2)}, u32[]{:S(2)}) collective-permute-start(f32[5,128,128]{2,1,0:T(8,128)S(1)} %bitcast.40), channel_id=1, source_target_pairs={{0,1},{1,0},{2,3},{3,2},{4,5},{5,4},{6,7},{7,6},{8,9},{9,8},{10,11... | collective-permute-start | bytes 983048 | tf_op jit(solution)/shard_map/ppermute | solution.py:281
  180.0 1.2 collective-permute-done.16.other_ref
  181.2 21.7 %shard_map.81 = (f32[128,512]{1,0:T(8,128)}, f32[512,512]{1,0:T(8,128)}) custom-call(s32[1]{0:T(128)} %bitcast.core_ref, f32[5,128,128]{2,1,0:T(8,128)S(1)} %bitcast.41, f32[5,128,128]{2,1,0:T(8,128)S(1)} %collective-permute-done.16.other_ref, f32[128,512]{1,0:T(8,128)S(1)} %get-tuple-element.7.applied_ref), custom_call_target="tpu_custom_call" | custom-call | tf_op jit(solution)/shard_map/pallas_call | solution.py:283
  (39 shorter events, 4.3 us)
Async XLA Ops:
  1.6 77.9 %copy-start.2 = (s32[1,1,24]{2,1,0:T(1,128)S(1)}, s32[1,1,24]{2,1,0:T(1,128)}, u32[]{:S(2)}) copy-start(s32[1,1,24]{2,1,0:T(1,128)} %param.10) | copy-start | bytes 292
  1.6 77.9 %copy-start.4 = (s32[1,1,24]{2,1,0:T(1,128)S(1)}, s32[1,1,24]{2,1,0:T(1,128)}, u32[]{:S(2)}) copy-start(s32[1,1,24]{2,1,0:T(1,128)} %param.9) | copy-start | bytes 292
  1.6 78.0 %copy-start = (bf16[1,1,24,128,128]{4,3,2,1,0:T(8,128)(2,1)S(1)}, bf16[1,1,24,128,128]{4,3,2,1,0:T(8,128)(2,1)}, u32[]{:S(2)}) copy-start(bf16[1,1,24,128,128]{4,3,2,1,0:T(8,128)(2,1)} %param.8) | copy-start | bytes 2359300
  27.1 19.1 %collective-permute-start.10 = (bf16[4,128,512]{2,1,0:T(8,128)(2,1)S(1)}, bf16[4,128,512]{2,1,0:T(8,128)(2,1)S(1)}, u32[]{:S(2)}, u32[]{:S(2)}) collective-permute-start(bf16[4,128,512]{2,1,0:T(8,128)(2,1)S(1)} %get-tuple-element.10.refs_6_), channel_id=1, source_target_pairs={{0,448},{1,57},{8,456},{9,1},{16,464},{17,9},{24,472},{25,17},{32,... | collective-permute-start | bytes 1572872 | tf_op jit(solution)/shard_map/ppermute | solution.py:189
  37.7 13.0 %collective-permute-start = (bf16[4,128,512]{2,1,0:T(8,128)(2,1)S(1)}, bf16[4,128,512]{2,1,0:T(8,128)(2,1)S(1)}, u32[]{:S(2)}, u32[]{:S(2)}) collective-permute-start(bf16[4,128,512]{2,1,0:T(8,128)(2,1)S(1)} %get-tuple-element.11.refs_0_), channel_id=1, source_target_pairs={{0,64},{1,9},{8,72},{9,17},{16,80},{17,25},{24,88},{25,33},{32,96}... | collective-permute-start | bytes 1572872 | tf_op jit(solution)/shard_map/ppermute | solution.py:187
  39.7 13.0 %collective-permute-start.4 = (bf16[4,128,512]{2,1,0:T(8,128)(2,1)S(1)}, bf16[4,128,512]{2,1,0:T(8,128)(2,1)S(1)}, u32[]{:S(2)}, u32[]{:S(2)}) collective-permute-start(bf16[4,128,512]{2,1,0:T(8,128)(2,1)S(1)} %get-tuple-element.11.refs_0_), channel_id=1, source_target_pairs={{0,448},{1,57},{8,456},{9,1},{16,464},{17,9},{24,472},{25,17},{32,... | collective-permute-start | bytes 1572872 | tf_op jit(solution)/shard_map/ppermute | solution.py:189
  44.3 13.1 %collective-permute-start.7 = (bf16[4,128,512]{2,1,0:T(8,128)(2,1)S(1)}, bf16[4,128,512]{2,1,0:T(8,128)(2,1)}, u32[]{:S(2)}, u32[]{:S(2)}) collective-permute-start(bf16[4,128,512]{2,1,0:T(8,128)(2,1)S(1)} %get-tuple-element.10.refs_6_), channel_id=1, source_target_pairs={{0,64},{1,9},{8,72},{9,17},{16,80},{17,25},{24,88},{25,33},{32,96}... | collective-permute-start | bytes 1572872 | tf_op jit(solution)/shard_map/ppermute | solution.py:187
  46.2 13.1 %collective-permute-start.11 = (bf16[4,128,512]{2,1,0:T(8,128)(2,1)S(1)}, bf16[4,128,512]{2,1,0:T(8,128)(2,1)}, u32[]{:S(2)}, u32[]{:S(2)}) collective-permute-start(bf16[4,128,512]{2,1,0:T(8,128)(2,1)S(1)} %collective-permute-done.10.refs_11_), channel_id=1, source_target_pairs={{0,448},{1,57},{8,456},{9,1},{16,464},{17,9},{24,472},{25,17},{32,... | collective-permute-start | bytes 1572872 | tf_op jit(solution)/shard_map/ppermute | solution.py:189
  50.8 13.1 %collective-permute-start.1 = (bf16[4,128,512]{2,1,0:T(8,128)(2,1)S(1)}, bf16[4,128,512]{2,1,0:T(8,128)(2,1)}, u32[]{:S(2)}, u32[]{:S(2)}) collective-permute-start(bf16[4,128,512]{2,1,0:T(8,128)(2,1)S(1)} %collective-permute-done.refs_1_), channel_id=1, source_target_pairs={{0,64},{1,9},{8,72},{9,17},{16,80},{17,25},{24,88},{25,33},{32,96}... | collective-permute-start | bytes 1572872 | tf_op jit(solution)/shard_map/ppermute | solution.py:187
  52.7 13.7 %collective-permute-start.5 = (bf16[4,128,512]{2,1,0:T(8,128)(2,1)S(1)}, bf16[4,128,512]{2,1,0:T(8,128)(2,1)}, u32[]{:S(2)}, u32[]{:S(2)}) collective-permute-start(bf16[4,128,512]{2,1,0:T(8,128)(2,1)S(1)} %collective-permute-done.4.refs_5_), channel_id=1, source_target_pairs={{0,448},{1,57},{8,456},{9,1},{16,464},{17,9},{24,472},{25,17},{32,... | collective-permute-start | bytes 1572872 | tf_op jit(solution)/shard_map/ppermute | solution.py:189
  57.3 13.7 %collective-permute-start.8 = (bf16[4,128,512]{2,1,0:T(8,128)(2,1)}, bf16[4,128,512]{2,1,0:T(8,128)(2,1)}, u32[]{:S(2)}, u32[]{:S(2)}) collective-permute-start(bf16[4,128,512]{2,1,0:T(8,128)(2,1)} %collective-permute-done.7.refs_7_), channel_id=1, source_target_pairs={{0,64},{1,9},{8,72},{9,17},{16,80},{17,25},{24,88},{25,33},{32,96}... | collective-permute-start | bytes 1572872 | tf_op jit(solution)/shard_map/ppermute | solution.py:187
  59.3 13.7 %collective-permute-start.12 = (bf16[4,128,512]{2,1,0:T(8,128)(2,1)}, bf16[4,128,512]{2,1,0:T(8,128)(2,1)}, u32[]{:S(2)}, u32[]{:S(2)}) collective-permute-start(bf16[4,128,512]{2,1,0:T(8,128)(2,1)} %collective-permute-done.11.refs_10_), channel_id=1, source_target_pairs={{0,448},{1,57},{8,456},{9,1},{16,464},{17,9},{24,472},{25,17},{32,... | collective-permute-start | bytes 1572872 | tf_op jit(solution)/shard_map/ppermute | solution.py:189
  63.9 13.7 %collective-permute-start.2 = (bf16[4,128,512]{2,1,0:T(8,128)(2,1)}, bf16[4,128,512]{2,1,0:T(8,128)(2,1)}, u32[]{:S(2)}, u32[]{:S(2)}) collective-permute-start(bf16[4,128,512]{2,1,0:T(8,128)(2,1)} %collective-permute-done.1.refs_2_), channel_id=1, source_target_pairs={{0,64},{1,9},{8,72},{9,17},{16,80},{17,25},{24,88},{25,33},{32,96}... | collective-permute-start | bytes 1572872 | tf_op jit(solution)/shard_map/ppermute | solution.py:187
  66.5 16.8 %collective-permute-start.6 = (bf16[4,128,512]{2,1,0:T(8,128)(2,1)}, bf16[4,128,512]{2,1,0:T(8,128)(2,1)S(1)}, u32[]{:S(2)}, u32[]{:S(2)}) collective-permute-start(bf16[4,128,512]{2,1,0:T(8,128)(2,1)} %collective-permute-done.5.refs_4_), channel_id=1, source_target_pairs={{0,448},{1,57},{8,456},{9,1},{16,464},{17,9},{24,472},{25,17},{32,... | collective-permute-start | bytes 1572872 | tf_op jit(solution)/shard_map/ppermute | solution.py:189
  71.0 12.3 %collective-permute-start.9 = (bf16[4,128,512]{2,1,0:T(8,128)(2,1)}, bf16[4,128,512]{2,1,0:T(8,128)(2,1)S(1)}, u32[]{:S(2)}, u32[]{:S(2)}) collective-permute-start(bf16[4,128,512]{2,1,0:T(8,128)(2,1)} %collective-permute-done.8.refs_8_), channel_id=1, source_target_pairs={{0,64},{1,9},{8,72},{9,17},{16,80},{17,25},{24,88},{25,33},{32,96}... | collective-permute-start | bytes 1572872 | tf_op jit(solution)/shard_map/ppermute | solution.py:187
  73.0 11.0 %collective-permute-start.13 = (bf16[4,128,512]{2,1,0:T(8,128)(2,1)}, bf16[4,128,512]{2,1,0:T(8,128)(2,1)S(1)}, u32[]{:S(2)}, u32[]{:S(2)}) collective-permute-start(bf16[4,128,512]{2,1,0:T(8,128)(2,1)} %collective-permute-done.12.refs_9_), channel_id=1, source_target_pairs={{0,448},{1,57},{8,456},{9,1},{16,464},{17,9},{24,472},{25,17},{32,... | collective-permute-start | bytes 1572872 | tf_op jit(solution)/shard_map/ppermute | solution.py:189
  77.6 11.6 %collective-permute-start.3 = (bf16[4,128,512]{2,1,0:T(8,128)(2,1)}, bf16[4,128,512]{2,1,0:T(8,128)(2,1)S(1)}, u32[]{:S(2)}, u32[]{:S(2)}) collective-permute-start(bf16[4,128,512]{2,1,0:T(8,128)(2,1)} %collective-permute-done.2.refs_3_), channel_id=1, source_target_pairs={{0,64},{1,9},{8,72},{9,17},{16,80},{17,25},{24,88},{25,33},{32,96}... | collective-permute-start | bytes 1572872 | tf_op jit(solution)/shard_map/ppermute | solution.py:187
  90.2 8.6 %collective-permute-start.14 = (f32[4,128,512]{2,1,0:T(8,128)S(1)}, f32[4,128,512]{2,1,0:T(8,128)S(1)}, u32[]{:S(2)}, u32[]{:S(2)}) collective-permute-start(f32[4,128,512]{2,1,0:T(8,128)S(1)} %shard_map.79), channel_id=1, source_target_pairs={{0,1},{1,0},{2,3},{3,2},{4,5},{5,4},{6,7},{7,6},{8,9},{9,8},{10,11... | collective-permute-start | bytes 3145736 | tf_op jit(solution)/shard_map/ppermute | solution.py:268
  97.3 6.9 %copy-start.1 = (bf16[128,512]{1,0:T(8,128)(2,1)S(1)}, bf16[128,512]{1,0:T(8,128)(2,1)}, u32[]{:S(2)}) copy-start(bf16[128,512]{1,0:T(8,128)(2,1)} %param.6) | copy-start | bytes 393220
  97.3 6.9 %copy-start.3 = (f32[128]{0:T(128)S(1)}, f32[128]{0:T(128)}, u32[]{:S(2)}) copy-start(f32[128]{0:T(128)} %param.7) | copy-start | bytes 1540
  99.9 18.8 %all-to-all-start.1 = ((f32[4,128,512]{2,1,0:T(8,128)}), f32[4,128,512]{2,1,0:T(8,128)S(1)}, u32[]{:S(2)}, u32[]{:S(2)}) async-start(f32[4,128,512]{2,1,0:T(8,128)} %add.47), calls=%async_computation.1 | async-start | bytes 2097152 | tf_op jit(solution)/shard_map/all_to_all | solution.py:270
  119.5 4.7 %collective-permute-start.15 = (f32[5,128,128]{2,1,0:T(8,128)S(1)}, f32[5,128,128]{2,1,0:T(8,128)S(1)}, u32[]{:S(2)}, u32[]{:S(2)}) collective-permute-start(f32[5,128,128]{2,1,0:T(8,128)S(1)} %get-tuple-element.6), channel_id=1, source_target_pairs={{0,1},{1,0},{2,3},{3,2},{4,5},{5,4},{6,7},{7,6},{8,9},{9,8},{10,11... | collective-permute-start | bytes 983048 | tf_op jit(solution)/shard_map/ppermute | solution.py:280
  177.4 3.8 %collective-permute-start.16 = (f32[5,128,128]{2,1,0:T(8,128)S(1)}, f32[5,128,128]{2,1,0:T(8,128)S(1)}, u32[]{:S(2)}, u32[]{:S(2)}) collective-permute-start(f32[5,128,128]{2,1,0:T(8,128)S(1)} %bitcast.40), channel_id=1, source_target_pairs={{0,1},{1,0},{2,3},{3,2},{4,5},{5,4},{6,7},{7,6},{8,9},{9,8},{10,11... | collective-permute-start | bytes 983048 | tf_op jit(solution)/shard_map/ppermute | solution.py:281

commit v7 on v6

--- a/solution.py
+++ b/solution.py
@@ -45,25 +45,33 @@
 
 
 def upper_pairs(nblocks):
-    pairs = [(j, k) for j in range(nblocks) for k in range(j, nblocks)]
-    return pairs[:len(pairs) // 2], pairs[len(pairs) // 2:]
-
-
-def gram_blocks(core_ref, parts_ref, local_ref, applied_ref, own_ref, other_ref):
-    n = own_ref.shape[1]
+    return [(j, k) for j in range(nblocks) for k in range(j, nblocks)]
+
+
+def gram_blocks(parts_ref, local_ref, applied_ref, gram_ref):
+    n = gram_ref.shape[1]
     applied = local_ref[...]
     for i in range(parts_ref.shape[0]):
         applied = applied + parts_ref[i]
     applied_ref[...] = applied
     nblocks = applied.shape[1] // n
     rows = [dot_full(applied[:, j * n:(j + 1) * n], applied[:, j * n:], 0, 0) for j in range(nblocks)]
-    for core in (0, 1):
-        @pl.when(core_ref[0] == core)
-        def _():
-            for half, pairs in enumerate(upper_pairs(nblocks)):
-                target = own_ref if half == core else other_ref
-                for at, (j, k) in enumerate(pairs):
-                    target[at] = rows[j][:, (k - j) * n:(k - j + 1) * n]
+    for at, (j, k) in enumerate(upper_pairs(nblocks)):
+        gram_ref[at] = rows[j][:, (k - j) * n:(k - j + 1) * n]
+
+
+def three_parts(value):
+    high = value.astype(jnp.bfloat16)
+    rest = value - high.astype(jnp.float32)
+    middle = rest.astype(jnp.bfloat16)
+    return high, middle, (rest - middle.astype(jnp.float32)).astype(jnp.bfloat16)
+
+
+def dot_few_rows(left, right):
+    h, m, l = three_parts(left)
+    high, middle, low = three_parts(right)
+    stacked = jnp.concatenate([h, h, m, h, m, l]), jnp.concatenate([high, middle, high, low, middle, high])
+    return lax.dot_general(*stacked, (((0,), (0,)), ((), ())), preferred_element_type=jnp.float32)
 
 
 def factor_diagonal(a_ref, inverse_ref, u_ref, base, n):
@@ -100,28 +108,26 @@
         scale = lax.rsqrt(pivots)
         u_ref[base + first:base + first + STRIP, base:base + n] = jnp.where(lane >= sub + first, down_a * scale, 0.0)
         inverse_ref[here, :] = down_e * scale
-        spread_a = [spread(full_a, k) for k in range(STRIP)]
-        spread_e = [spread(full_e, k) for k in range(STRIP)]
-        for i in range(s + 1, strips):
-            next_a, next_e = rows_a[i], rows_e[i]
+        if s + 1 < strips:
+            here_a = rows_a[s]
             for k in range(STRIP):
-                c = jnp.broadcast_to(rows_a[i][:, first + k:first + k + 1], (STRIP, n))
-                next_a = next_a - c * spread_a[k]
-                next_e = next_e - c * spread_e[k]
-            rows_a[i], rows_e[i] = next_a, next_e
-
-
-def factor_and_solve(core_ref, own_ref, other_ref, applied_ref, states_ref, u_ref, work, inverse):
-    n = own_ref.shape[1]
+                c = jnp.broadcast_to(rows_a[s + 1][:, first + k:first + k + 1], (STRIP, n))
+                taken_a = c * spread(full_a, k) + (taken_a if k else 0.0)
+                taken_e = c * spread(full_e, k) + (taken_e if k else 0.0)
+            rows_a[s + 1], rows_e[s + 1] = rows_a[s + 1] - taken_a, rows_e[s + 1] - taken_e
+        if s + 2 < strips:
+            taken = dot_few_rows(here_a, jnp.concatenate([full_a, full_e], axis=1))
+            for i in range(s + 2, strips):
+                rows_a[i] = rows_a[i] - taken[STRIP * i:STRIP * (i + 1), :n]
+                rows_e[i] = rows_e[i] - taken[STRIP * i:STRIP * (i + 1), n:]
+
+
+def factor_and_solve(gram_ref, applied_ref, states_ref, u_ref, work, inverse):
+    n = gram_ref.shape[1]
     size = u_ref.shape[0]
     nblocks = size // n
-    for core in (0, 1):
-        @pl.when(core_ref[0] == core)
-        def _():
-            for half, pairs in enumerate(upper_pairs(nblocks)):
-                source = own_ref if half == core else other_ref
-                for at, (j, k) in enumerate(pairs):
-                    work[n * j:n * (j + 1), n * k:n * (k + 1)] = source[at]
+    for at, (j, k) in enumerate(upper_pairs(nblocks)):
+        work[n * j:n * (j + 1), n * k:n * (k + 1)] = gram_ref[at]
     states_ref[...] = applied_ref[...]
     u_ref[...] = jnp.zeros_like(u_ref)
     for j in range(nblocks):
@@ -270,22 +276,24 @@
     parts = lax.all_to_all(keep + other, "x", 0, 0, tiled=True)
 
     nblocks = kstates // width
-    half = jax.ShapeDtypeStruct((nblocks * (nblocks + 1) // 4, width, width), f32)
-    core = k.astype(jnp.int32).reshape(1)
-    applied, own, other = call(
+    blocks = nblocks * (nblocks + 1) // 2
+    applied, gram = call(
         gram_blocks,
-        [jax.ShapeDtypeStruct((own_rows, kstates), f32), half, half],
-        [sm, vm, vm],
-    )(core, parts, local)
-    own = sum_halves(own + lax.ppermute(other, "k", [(0, 1), (1, 0)]))
-    other = lax.ppermute(own, "k", [(0, 1), (1, 0)])
+        [jax.ShapeDtypeStruct((own_rows, kstates), f32), jax.ShapeDtypeStruct((blocks, width, width), f32)],
+        [vm, vm],
+    )(parts, local)
+    cores = lax.axis_size("k")
+    halves_of_gram = gram.reshape((cores, blocks // cores) + gram.shape[1:])
+    half = sum_halves(lax.all_to_all(halves_of_gram, "k", 0, 0, tiled=True).sum(0))
+    both = jnp.broadcast_to(half[None], (cores,) + half.shape)
+    gram = lax.all_to_all(both, "k", 0, 0, tiled=True).reshape(gram.shape)
 
     states, upper = call(
         factor_and_solve,
         [jax.ShapeDtypeStruct((own_rows, kstates), f32), jax.ShapeDtypeStruct((kstates, kstates), f32)],
-        [sm, vm, vm, vm],
+        [vm, vm],
         [vm((kstates, kstates), f32), vm((width, width), f32)],
-    )(core, own, other, applied)
+    )(gram, applied)
     return (states, upper)
 
 

time: 204 us -> 201 us (0.985)
  blocking collectives: 77.8 us -> 87.8 us
  starting transfers between devices: 68.1 us -> 62.2 us
  Pallas kernels: 27.9 us -> 23 us
    all_to_all x0 -> x2, blocking collectives: none -> 9.58 us  [the longest x1 5.09 us: per_device(): lax.all_to_all(halves_of_gram, 'k', 0, 0, tiled=True).sum(0)]
    ppermute x2 -> x0, starting transfers between devices: 5.96 us -> none  [the longest x1 3.42 us: per_device(): own = sum_halves(own + lax.ppermute(other, 'k', [(0, 1), (1, 0)]))]
    pallas_call x1, Pallas kernels: 21.7 us -> 16.8 us  [per_device(): call(factor_and_solve, [jax.ShapeDtypeStruct((own_rows, kstates), f32), j...]
    ppermute x2 -> x0, waiting for transfers between devices: 2.47 us -> none  [the longest x1 1.23 us: per_device(): own = sum_halves(own + lax.ppermute(other, 'k', [(0, 1), (1, 0)]))]
  transfers between devices with their start and end apart: 18 -> 16, of which waited for: 6 -> 4; matrix products, arithmetic and copies ran while one was open for 0% -> 0% of each run, Pallas kernels for 2% -> 2%
where the time goes in v7:
time: 201 us; the launch traced here: 200 us
  blocking collectives  87.8 us (44%)
  starting transfers between devices  62.2 us (31%)
  Pallas kernels  23 us (11%)
  waiting for transfers between devices  22.4 us (11%)
    all_to_all x4, blocking collectives, exchange(): lax.all_to_all(pieces, axes, 0, 0, axis_index_groups=groups, tiled=True)  52.9 us
    ppermute x7, starting transfers between devices, gather_states(): below[at].append(lax.ppermute(below[at][-1], axes, down))  38.1 us
    all_to_all x1, blocking collectives, gather_states(): lax.all_to_all(copies, axes, 0, 0, axis_index_groups=line_places(*sizes),...  25.3 us
    pallas_call x1, Pallas kernels, per_device(): call(factor_and_solve, [jax.ShapeDtypeStruct((own_rows, kstates), f32), j...  16.8 us
    all_to_all x1, waiting for transfers between devices, per_device(): parts = lax.all_to_all(keep + other, 'x', 0, 0, tiled=True)  14.7 us
    ppermute x7, starting transfers between devices, gather_states(): above[at].append(lax.ppermute(above[at][-1], axes, up))  13.4 us
    ppermute x1, starting transfers between devices, per_device(): other = lax.ppermute(send, 'k', [(0, 1), (1, 0)])  7.11 us
    pallas_call x3, Pallas kernels, products(): call(functools.partial(tile_products, ids, first_place, bool(base)), [jax...  5.42 us
  transfers between devices with their start and end apart: 16, of which 4 were waited for; matrix products, arithmetic and copies ran while one was open for 0% of the time, Pallas kernels for 2%

profile of v7, /device:TPU:1, one launch (start us, length us, event | category | flops | bytes accessed | tf_op | source)
XLA Modules:
  0.0 200.3 jit_solution(12517859201181333398)
XLA Ops:
  1.7 25.3 %all_to_all.46 = bf16[8,128,512]{2,1,0:T(8,128)(2,1)S(1)} all-to-all(bf16[8,128,512]{2,1,0:T(8,128)(2,1)S(1)} %broadcast_in_dim.12), channel_id=1, replica_groups={{0,8,16,24,32,40,48,56},{1,65,129,193,257,321,385,449},{64,72,80,88,96,..., dimensions={0} | all-to-all | bytes 2097152 | tf_op jit(solution)/shard_map/all_to_all | solution.py:185
  27.1 10.7 %collective-permute-start.10 = (bf16[4,128,512]{2,1,0:T(8,128)(2,1)S(1)}, bf16[4,128,512]{2,1,0:T(8,128)(2,1)S(1)}, u32[]{:S(2)}, u32[]{:S(2)}) collective-permute-start(bf16[4,128,512]{2,1,0:T(8,128)(2,1)S(1)} %get-tuple-element.8.refs_6_), channel_id=1, source_target_pairs={{0,448},{1,57},{8,456},{9,1},{16,464},{17,9},{24,472},{25,17},{32,... | collective-permute-start | bytes 1572872 | tf_op jit(solution)/shard_map/ppermute | solution.py:195
  37.7 1.9 collective-permute-start
  39.7 4.6 %collective-permute-start.4 = (bf16[4,128,512]{2,1,0:T(8,128)(2,1)S(1)}, bf16[4,128,512]{2,1,0:T(8,128)(2,1)S(1)}, u32[]{:S(2)}, u32[]{:S(2)}) collective-permute-start(bf16[4,128,512]{2,1,0:T(8,128)(2,1)S(1)} %get-tuple-element.9.refs_0_), channel_id=1, source_target_pairs={{0,448},{1,57},{8,456},{9,1},{16,464},{17,9},{24,472},{25,17},{32,... | collective-permute-start | bytes 1572872 | tf_op jit(solution)/shard_map/ppermute | solution.py:195
  44.3 1.9 collective-permute-start.7
  46.2 4.6 %collective-permute-start.11 = (bf16[4,128,512]{2,1,0:T(8,128)(2,1)S(1)}, bf16[4,128,512]{2,1,0:T(8,128)(2,1)}, u32[]{:S(2)}, u32[]{:S(2)}) collective-permute-start(bf16[4,128,512]{2,1,0:T(8,128)(2,1)S(1)} %collective-permute-done.10.refs_11_), channel_id=1, source_target_pairs={{0,448},{1,57},{8,456},{9,1},{16,464},{17,9},{24,472},{25,17},{32,... | collective-permute-start | bytes 1572872 | tf_op jit(solution)/shard_map/ppermute | solution.py:195
  50.8 1.9 collective-permute-start.1
  52.7 4.6 %collective-permute-start.5 = (bf16[4,128,512]{2,1,0:T(8,128)(2,1)S(1)}, bf16[4,128,512]{2,1,0:T(8,128)(2,1)}, u32[]{:S(2)}, u32[]{:S(2)}) collective-permute-start(bf16[4,128,512]{2,1,0:T(8,128)(2,1)S(1)} %collective-permute-done.4.refs_5_), channel_id=1, source_target_pairs={{0,448},{1,57},{8,456},{9,1},{16,464},{17,9},{24,472},{25,17},{32,... | collective-permute-start | bytes 1572872 | tf_op jit(solution)/shard_map/ppermute | solution.py:195
  57.3 1.9 collective-permute-start.8
  59.3 4.6 %collective-permute-start.12 = (bf16[4,128,512]{2,1,0:T(8,128)(2,1)}, bf16[4,128,512]{2,1,0:T(8,128)(2,1)}, u32[]{:S(2)}, u32[]{:S(2)}) collective-permute-start(bf16[4,128,512]{2,1,0:T(8,128)(2,1)} %collective-permute-done.11.refs_10_), channel_id=1, source_target_pairs={{0,448},{1,57},{8,456},{9,1},{16,464},{17,9},{24,472},{25,17},{32,... | collective-permute-start | bytes 1572872 | tf_op jit(solution)/shard_map/ppermute | solution.py:195
  63.9 1.9 collective-permute-start.2
  66.5 4.6 %collective-permute-start.6 = (bf16[4,128,512]{2,1,0:T(8,128)(2,1)}, bf16[4,128,512]{2,1,0:T(8,128)(2,1)S(1)}, u32[]{:S(2)}, u32[]{:S(2)}) collective-permute-start(bf16[4,128,512]{2,1,0:T(8,128)(2,1)} %collective-permute-done.5.refs_4_), channel_id=1, source_target_pairs={{0,448},{1,57},{8,456},{9,1},{16,464},{17,9},{24,472},{25,17},{32,... | collective-permute-start | bytes 1572872 | tf_op jit(solution)/shard_map/ppermute | solution.py:195
  71.0 1.9 collective-permute-start.9
  73.0 4.6 %collective-permute-start.13 = (bf16[4,128,512]{2,1,0:T(8,128)(2,1)}, bf16[4,128,512]{2,1,0:T(8,128)(2,1)S(1)}, u32[]{:S(2)}, u32[]{:S(2)}) collective-permute-start(bf16[4,128,512]{2,1,0:T(8,128)(2,1)} %collective-permute-done.12.refs_9_), channel_id=1, source_target_pairs={{0,448},{1,57},{8,456},{9,1},{16,464},{17,9},{24,472},{25,17},{32,... | collective-permute-start | bytes 1572872 | tf_op jit(solution)/shard_map/ppermute | solution.py:195
  77.6 1.9 collective-permute-start.3
  79.6 3.0 %shard_map.77.refs_4_ = f32[8,128,512]{2,1,0:T(8,128)S(1)} custom-call(s32[73]{0:T(128)S(1)} %pad_add_fusion.meta_ref, bf16[24,128,128]{2,1,0:T(8,128)(2,1)S(1)} %bitcast.38, bf16[4,128,512]{2,1,0:T(8,128)(2,1)S(1)} %get-tuple-element.9.refs_0_, bf16[4,128,512]{2,1,0:T(8,128)(2,1)S(1)} %collective-permute-done.refs_1_, ...), custom_call_target="tpu_custom_call" | custom-call | tf_op jit(solution)/shard_map/pallas_call | solution.py:264
  82.7 1.3 collective-permute-done.13.refs_3_
  84.0 5.2 %collective-permute-done.3.refs_0_ = bf16[4,128,512]{2,1,0:T(8,128)(2,1)S(1)} collective-permute-done((bf16[4,128,512]{2,1,0:T(8,128)(2,1)}, bf16[4,128,512]{2,1,0:T(8,128)(2,1)S(1)}, u32[]{:S(2)}, u32[]{:S(2)}) %collective-permute-start.3) | collective-permute-done | bytes 524320 | tf_op jit(solution)/shard_map/ppermute | solution.py:193
  89.2 1.3 shard_map.79
  90.5 7.1 %collective-permute-start.14 = (f32[4,128,512]{2,1,0:T(8,128)S(1)}, f32[4,128,512]{2,1,0:T(8,128)S(1)}, u32[]{:S(2)}, u32[]{:S(2)}) collective-permute-start(f32[4,128,512]{2,1,0:T(8,128)S(1)} %shard_map.79), channel_id=1, source_target_pairs={{0,1},{1,0},{2,3},{3,2},{4,5},{5,4},{6,7},{7,6},{8,9},{9,8},{10,11... | collective-permute-start | bytes 3145736 | tf_op jit(solution)/shard_map/ppermute | solution.py:274
  97.6 1.1 shard_map.78
  98.8 1.1 collective-permute-done.14
  99.9 1.2 add.44
  101.1 3.5 %all-to-all-start.1 = ((f32[4,128,512]{2,1,0:T(8,128)}), f32[4,128,512]{2,1,0:T(8,128)S(1)}, u32[]{:S(2)}, u32[]{:S(2)}) async-start(f32[4,128,512]{2,1,0:T(8,128)} %add.44), calls=%async_computation.1 | async-start | bytes 2097152 | tf_op jit(solution)/shard_map/all_to_all | solution.py:276
  104.7 14.7 %all-to-all-done.1.parts_ref = f32[4,128,512]{2,1,0:T(8,128)S(1)} async-done(((f32[4,128,512]{2,1,0:T(8,128)}), f32[4,128,512]{2,1,0:T(8,128)S(1)}, u32[]{:S(2)}, u32[]{:S(2)}) %all-to-all-start.1) | async-done | bytes 1048608 | tf_op jit(solution)/shard_map/all_to_all | solution.py:276
  120.2 5.1 %all_to_all.47 = f32[2,5,128,128]{3,2,1,0:T(8,128)S(1)} all-to-all(f32[2,5,128,128]{3,2,1,0:T(8,128)S(1)} %bitcast.42), channel_id=1, replica_groups=mesh['y'=8,'z'=8,'x'=4,'k'=2] {'k'}, dimensions={0} | all-to-all | bytes 1310720 | tf_op jit(solution)/shard_map/all_to_all | solution.py:287
  125.3 7.8 %all_to_all.48 = f32[4,160,128]{2,1,0:T(8,128)S(1)} all-to-all(f32[4,160,128]{2,1,0:T(8,128)S(1)} %bitcast.43), channel_id=1, replica_groups={{0,2,4,6},{8,10,12,14},{16,18,20,22},{24,26,28,30},{32,34,36,38},{40,42..., dimensions={0} | all-to-all | bytes 655360 | tf_op jit(solution)/shard_map/all_to_all | solution.py:233
  133.2 19.3 %all_to_all.49 = f32[64,1,320]{2,1,0:T(1,128)S(1)} all-to-all(f32[64,1,320]{2,1,0:T(1,128)S(1)} %all_to_all.37), channel_id=1, replica_groups={{0,8,16,24,32,40,48,56,64,72,80,88,96,104,112,120,128,136,144,152,160,1..., dimensions={0} | all-to-all | bytes 163840 | tf_op jit(solution)/shard_map/all_to_all | solution.py:233
  152.7 18.1 %all_to_all.50 = f32[64,1,320]{2,1,0:T(1,128)S(1)} all-to-all(f32[64,1,320]{2,1,0:T(1,128)S(1)} %broadcast_in_dim.13), channel_id=1, replica_groups={{0,8,16,24,32,40,48,56,64,72,80,88,96,104,112,120,128,136,144,152,160,1..., dimensions={0} | all-to-all | bytes 163840 | tf_op jit(solution)/shard_map/all_to_all | solution.py:233
  171.2 7.8 %all_to_all.51 = f32[4,160,128]{2,1,0:T(8,128)S(1)} all-to-all(f32[4,160,128]{2,1,0:T(8,128)S(1)} %broadcast_in_dim.30), channel_id=1, replica_groups={{0,2,4,6},{8,10,12,14},{16,18,20,22},{24,26,28,30},{32,34,36,38},{40,42..., dimensions={0} | all-to-all | bytes 655360 | tf_op jit(solution)/shard_map/all_to_all | solution.py:233
  179.0 4.5 %all_to_all.52 = f32[2,5,128,128]{3,2,1,0:T(8,128)S(1)} all-to-all(f32[2,5,128,128]{3,2,1,0:T(8,128)S(1)} %broadcast_in_dim.32), channel_id=1, replica_groups=mesh['y'=8,'z'=8,'x'=4,'k'=2] {'k'}, dimensions={0} | all-to-all | bytes 1310720 | tf_op jit(solution)/shard_map/all_to_all | solution.py:289
  183.5 16.8 %shard_map.81 = (f32[128,512]{1,0:T(8,128)}, f32[512,512]{1,0:T(8,128)}) custom-call(f32[10,128,128]{2,1,0:T(8,128)S(1)} %bitcast.41, f32[128,512]{1,0:T(8,128)S(1)} %get-tuple-element.5.applied_ref), custom_call_target="tpu_custom_call" | custom-call | tf_op jit(solution)/shard_map/pallas_call | solution.py:291
  (38 shorter events, 2.8 us)
Async XLA Ops:
  1.6 77.9 %copy-start.2 = (s32[1,1,24]{2,1,0:T(1,128)S(1)}, s32[1,1,24]{2,1,0:T(1,128)}, u32[]{:S(2)}) copy-start(s32[1,1,24]{2,1,0:T(1,128)} %param.10) | copy-start | bytes 292
  1.6 77.9 %copy-start.4 = (s32[1,1,24]{2,1,0:T(1,128)S(1)}, s32[1,1,24]{2,1,0:T(1,128)}, u32[]{:S(2)}) copy-start(s32[1,1,24]{2,1,0:T(1,128)} %param.9) | copy-start | bytes 292
  1.6 78.0 %copy-start = (bf16[1,1,24,128,128]{4,3,2,1,0:T(8,128)(2,1)S(1)}, bf16[1,1,24,128,128]{4,3,2,1,0:T(8,128)(2,1)}, u32[]{:S(2)}) copy-start(bf16[1,1,24,128,128]{4,3,2,1,0:T(8,128)(2,1)} %param.8) | copy-start | bytes 2359300
  27.1 19.1 %collective-permute-start.10 = (bf16[4,128,512]{2,1,0:T(8,128)(2,1)S(1)}, bf16[4,128,512]{2,1,0:T(8,128)(2,1)S(1)}, u32[]{:S(2)}, u32[]{:S(2)}) collective-permute-start(bf16[4,128,512]{2,1,0:T(8,128)(2,1)S(1)} %get-tuple-element.8.refs_6_), channel_id=1, source_target_pairs={{0,448},{1,57},{8,456},{9,1},{16,464},{17,9},{24,472},{25,17},{32,... | collective-permute-start | bytes 1572872 | tf_op jit(solution)/shard_map/ppermute | solution.py:195
  37.7 13.0 %collective-permute-start = (bf16[4,128,512]{2,1,0:T(8,128)(2,1)S(1)}, bf16[4,128,512]{2,1,0:T(8,128)(2,1)S(1)}, u32[]{:S(2)}, u32[]{:S(2)}) collective-permute-start(bf16[4,128,512]{2,1,0:T(8,128)(2,1)S(1)} %get-tuple-element.9.refs_0_), channel_id=1, source_target_pairs={{0,64},{1,9},{8,72},{9,17},{16,80},{17,25},{24,88},{25,33},{32,96}... | collective-permute-start | bytes 1572872 | tf_op jit(solution)/shard_map/ppermute | solution.py:193
  39.7 13.0 %collective-permute-start.4 = (bf16[4,128,512]{2,1,0:T(8,128)(2,1)S(1)}, bf16[4,128,512]{2,1,0:T(8,128)(2,1)S(1)}, u32[]{:S(2)}, u32[]{:S(2)}) collective-permute-start(bf16[4,128,512]{2,1,0:T(8,128)(2,1)S(1)} %get-tuple-element.9.refs_0_), channel_id=1, source_target_pairs={{0,448},{1,57},{8,456},{9,1},{16,464},{17,9},{24,472},{25,17},{32,... | collective-permute-start | bytes 1572872 | tf_op jit(solution)/shard_map/ppermute | solution.py:195
  44.3 13.1 %collective-permute-start.7 = (bf16[4,128,512]{2,1,0:T(8,128)(2,1)S(1)}, bf16[4,128,512]{2,1,0:T(8,128)(2,1)}, u32[]{:S(2)}, u32[]{:S(2)}) collective-permute-start(bf16[4,128,512]{2,1,0:T(8,128)(2,1)S(1)} %get-tuple-element.8.refs_6_), channel_id=1, source_target_pairs={{0,64},{1,9},{8,72},{9,17},{16,80},{17,25},{24,88},{25,33},{32,96}... | collective-permute-start | bytes 1572872 | tf_op jit(solution)/shard_map/ppermute | solution.py:193
  46.2 13.1 %collective-permute-start.11 = (bf16[4,128,512]{2,1,0:T(8,128)(2,1)S(1)}, bf16[4,128,512]{2,1,0:T(8,128)(2,1)}, u32[]{:S(2)}, u32[]{:S(2)}) collective-permute-start(bf16[4,128,512]{2,1,0:T(8,128)(2,1)S(1)} %collective-permute-done.10.refs_11_), channel_id=1, source_target_pairs={{0,448},{1,57},{8,456},{9,1},{16,464},{17,9},{24,472},{25,17},{32,... | collective-permute-start | bytes 1572872 | tf_op jit(solution)/shard_map/ppermute | solution.py:195
  50.8 13.1 %collective-permute-start.1 = (bf16[4,128,512]{2,1,0:T(8,128)(2,1)S(1)}, bf16[4,128,512]{2,1,0:T(8,128)(2,1)}, u32[]{:S(2)}, u32[]{:S(2)}) collective-permute-start(bf16[4,128,512]{2,1,0:T(8,128)(2,1)S(1)} %collective-permute-done.refs_1_), channel_id=1, source_target_pairs={{0,64},{1,9},{8,72},{9,17},{16,80},{17,25},{24,88},{25,33},{32,96}... | collective-permute-start | bytes 1572872 | tf_op jit(solution)/shard_map/ppermute | solution.py:193
  52.7 13.7 %collective-permute-start.5 = (bf16[4,128,512]{2,1,0:T(8,128)(2,1)S(1)}, bf16[4,128,512]{2,1,0:T(8,128)(2,1)}, u32[]{:S(2)}, u32[]{:S(2)}) collective-permute-start(bf16[4,128,512]{2,1,0:T(8,128)(2,1)S(1)} %collective-permute-done.4.refs_5_), channel_id=1, source_target_pairs={{0,448},{1,57},{8,456},{9,1},{16,464},{17,9},{24,472},{25,17},{32,... | collective-permute-start | bytes 1572872 | tf_op jit(solution)/shard_map/ppermute | solution.py:195
  57.3 13.7 %collective-permute-start.8 = (bf16[4,128,512]{2,1,0:T(8,128)(2,1)}, bf16[4,128,512]{2,1,0:T(8,128)(2,1)}, u32[]{:S(2)}, u32[]{:S(2)}) collective-permute-start(bf16[4,128,512]{2,1,0:T(8,128)(2,1)} %collective-permute-done.7.refs_7_), channel_id=1, source_target_pairs={{0,64},{1,9},{8,72},{9,17},{16,80},{17,25},{24,88},{25,33},{32,96}... | collective-permute-start | bytes 1572872 | tf_op jit(solution)/shard_map/ppermute | solution.py:193
  59.3 13.7 %collective-permute-start.12 = (bf16[4,128,512]{2,1,0:T(8,128)(2,1)}, bf16[4,128,512]{2,1,0:T(8,128)(2,1)}, u32[]{:S(2)}, u32[]{:S(2)}) collective-permute-start(bf16[4,128,512]{2,1,0:T(8,128)(2,1)} %collective-permute-done.11.refs_10_), channel_id=1, source_target_pairs={{0,448},{1,57},{8,456},{9,1},{16,464},{17,9},{24,472},{25,17},{32,... | collective-permute-start | bytes 1572872 | tf_op jit(solution)/shard_map/ppermute | solution.py:195
  63.9 13.7 %collective-permute-start.2 = (bf16[4,128,512]{2,1,0:T(8,128)(2,1)}, bf16[4,128,512]{2,1,0:T(8,128)(2,1)}, u32[]{:S(2)}, u32[]{:S(2)}) collective-permute-start(bf16[4,128,512]{2,1,0:T(8,128)(2,1)} %collective-permute-done.1.refs_2_), channel_id=1, source_target_pairs={{0,64},{1,9},{8,72},{9,17},{16,80},{17,25},{24,88},{25,33},{32,96}... | collective-permute-start | bytes 1572872 | tf_op jit(solution)/shard_map/ppermute | solution.py:193
  66.5 16.2 %collective-permute-start.6 = (bf16[4,128,512]{2,1,0:T(8,128)(2,1)}, bf16[4,128,512]{2,1,0:T(8,128)(2,1)S(1)}, u32[]{:S(2)}, u32[]{:S(2)}) collective-permute-start(bf16[4,128,512]{2,1,0:T(8,128)(2,1)} %collective-permute-done.5.refs_4_), channel_id=1, source_target_pairs={{0,448},{1,57},{8,456},{9,1},{16,464},{17,9},{24,472},{25,17},{32,... | collective-permute-start | bytes 1572872 | tf_op jit(solution)/shard_map/ppermute | solution.py:195
  71.0 11.6 %collective-permute-start.9 = (bf16[4,128,512]{2,1,0:T(8,128)(2,1)}, bf16[4,128,512]{2,1,0:T(8,128)(2,1)S(1)}, u32[]{:S(2)}, u32[]{:S(2)}) collective-permute-start(bf16[4,128,512]{2,1,0:T(8,128)(2,1)} %collective-permute-done.8.refs_8_), channel_id=1, source_target_pairs={{0,64},{1,9},{8,72},{9,17},{16,80},{17,25},{24,88},{25,33},{32,96}... | collective-permute-start | bytes 1572872 | tf_op jit(solution)/shard_map/ppermute | solution.py:193
  73.0 11.0 %collective-permute-start.13 = (bf16[4,128,512]{2,1,0:T(8,128)(2,1)}, bf16[4,128,512]{2,1,0:T(8,128)(2,1)S(1)}, u32[]{:S(2)}, u32[]{:S(2)}) collective-permute-start(bf16[4,128,512]{2,1,0:T(8,128)(2,1)} %collective-permute-done.12.refs_9_), channel_id=1, source_target_pairs={{0,448},{1,57},{8,456},{9,1},{16,464},{17,9},{24,472},{25,17},{32,... | collective-permute-start | bytes 1572872 | tf_op jit(solution)/shard_map/ppermute | solution.py:195
  77.6 11.6 %collective-permute-start.3 = (bf16[4,128,512]{2,1,0:T(8,128)(2,1)}, bf16[4,128,512]{2,1,0:T(8,128)(2,1)S(1)}, u32[]{:S(2)}, u32[]{:S(2)}) collective-permute-start(bf16[4,128,512]{2,1,0:T(8,128)(2,1)} %collective-permute-done.2.refs_3_), channel_id=1, source_target_pairs={{0,64},{1,9},{8,72},{9,17},{16,80},{17,25},{24,88},{25,33},{32,96}... | collective-permute-start | bytes 1572872 | tf_op jit(solution)/shard_map/ppermute | solution.py:193
  90.5 9.4 %collective-permute-start.14 = (f32[4,128,512]{2,1,0:T(8,128)S(1)}, f32[4,128,512]{2,1,0:T(8,128)S(1)}, u32[]{:S(2)}, u32[]{:S(2)}) collective-permute-start(f32[4,128,512]{2,1,0:T(8,128)S(1)} %shard_map.79), channel_id=1, source_target_pairs={{0,1},{1,0},{2,3},{3,2},{4,5},{5,4},{6,7},{7,6},{8,9},{9,8},{10,11... | collective-permute-start | bytes 3145736 | tf_op jit(solution)/shard_map/ppermute | solution.py:274
  98.8 5.8 %copy-start.1 = (bf16[128,512]{1,0:T(8,128)(2,1)S(1)}, bf16[128,512]{1,0:T(8,128)(2,1)}, u32[]{:S(2)}) copy-start(bf16[128,512]{1,0:T(8,128)(2,1)} %param.6) | copy-start | bytes 393220
  98.8 5.8 %copy-start.3 = (f32[128]{0:T(128)S(1)}, f32[128]{0:T(128)}, u32[]{:S(2)}) copy-start(f32[128]{0:T(128)} %param.7) | copy-start | bytes 1540
  101.1 18.3 %all-to-all-start.1 = ((f32[4,128,512]{2,1,0:T(8,128)}), f32[4,128,512]{2,1,0:T(8,128)S(1)}, u32[]{:S(2)}, u32[]{:S(2)}) async-start(f32[4,128,512]{2,1,0:T(8,128)} %add.44), calls=%async_computation.1 | async-start | bytes 2097152 | tf_op jit(solution)/shard_map/all_to_all | solution.py:276

commit v8 on v7

--- a/solution.py
+++ b/solution.py
@@ -8,7 +8,7 @@
 from jax.sharding import Mesh, PartitionSpec as P
 
 FULL = lax.Precision.HIGHEST
-STRIP = 8
+STRIP = 16
 
 
 def dot_full(left, right, left_dim, right_dim):
@@ -45,19 +45,25 @@
 
 
 def upper_pairs(nblocks):
-    return [(j, k) for j in range(nblocks) for k in range(j, nblocks)]
-
-
-def gram_blocks(parts_ref, local_ref, applied_ref, gram_ref):
-    n = gram_ref.shape[1]
+    pairs = [(j, k) for j in range(nblocks) for k in range(j, nblocks)]
+    return pairs[:len(pairs) // 2], pairs[len(pairs) // 2:]
+
+
+def gram_blocks(core_ref, parts_ref, local_ref, applied_ref, own_ref, other_ref):
+    n = own_ref.shape[1]
     applied = local_ref[...]
     for i in range(parts_ref.shape[0]):
         applied = applied + parts_ref[i]
     applied_ref[...] = applied
     nblocks = applied.shape[1] // n
     rows = [dot_full(applied[:, j * n:(j + 1) * n], applied[:, j * n:], 0, 0) for j in range(nblocks)]
-    for at, (j, k) in enumerate(upper_pairs(nblocks)):
-        gram_ref[at] = rows[j][:, (k - j) * n:(k - j + 1) * n]
+    for core in (0, 1):
+        @pl.when(core_ref[0] == core)
+        def _():
+            for half, pairs in enumerate(upper_pairs(nblocks)):
+                target = own_ref if half == core else other_ref
+                for at, (j, k) in enumerate(pairs):
+                    target[at] = rows[j][:, (k - j) * n:(k - j + 1) * n]
 
 
 def three_parts(value):
@@ -126,7 +132,7 @@
     n = gram_ref.shape[1]
     size = u_ref.shape[0]
     nblocks = size // n
-    for at, (j, k) in enumerate(upper_pairs(nblocks)):
+    for at, (j, k) in enumerate(sum(upper_pairs(nblocks), [])):
         work[n * j:n * (j + 1), n * k:n * (k + 1)] = gram_ref[at]
     states_ref[...] = applied_ref[...]
     u_ref[...] = jnp.zeros_like(u_ref)
@@ -276,17 +282,14 @@
     parts = lax.all_to_all(keep + other, "x", 0, 0, tiled=True)
 
     nblocks = kstates // width
-    blocks = nblocks * (nblocks + 1) // 2
-    applied, gram = call(
+    half = jax.ShapeDtypeStruct((nblocks * (nblocks + 1) // 4, width, width), f32)
+    applied, own, other = call(
         gram_blocks,
-        [jax.ShapeDtypeStruct((own_rows, kstates), f32), jax.ShapeDtypeStruct((blocks, width, width), f32)],
-        [vm, vm],
-    )(parts, local)
-    cores = lax.axis_size("k")
-    halves_of_gram = gram.reshape((cores, blocks // cores) + gram.shape[1:])
-    half = sum_halves(lax.all_to_all(halves_of_gram, "k", 0, 0, tiled=True).sum(0))
-    both = jnp.broadcast_to(half[None], (cores,) + half.shape)
-    gram = lax.all_to_all(both, "k", 0, 0, tiled=True).reshape(gram.shape)
+        [jax.ShapeDtypeStruct((own_rows, kstates), f32), half, half],
+        [sm, vm, vm],
+    )(k.astype(jnp.int32).reshape(1), parts, local)
+    own = sum_halves(own + lax.ppermute(other, "k", [(0, 1), (1, 0)]))
+    gram = lax.all_gather(own, "k", axis=0, tiled=True)
 
     states, upper = call(
         factor_and_solve,

time: 201 us -> 197 us (0.980)
  blocking collectives: 87.8 us -> 81.7 us
  starting transfers between devices: 62.2 us -> 65.4 us
    all_to_all x2 -> x0, blocking collectives: 9.58 us -> none  [the longest x1 5.09 us: per_device(): lax.all_to_all(halves_of_gram, 'k', 0, 0, tiled=True).sum(0)]
    ppermute x0 -> x1, starting transfers between devices: none -> 3.42 us  [per_device(): own = sum_halves(own + lax.ppermute(other, 'k', [(0, 1), (1, 0)]))]
    all_gather x0 -> x1, blocking collectives: none -> 2.6 us  [per_device(): gram = lax.all_gather(own, 'k', axis=0, tiled=True)]
  transfers between devices with their start and end apart: 16 -> 17, of which waited for: 4 -> 5; matrix products, arithmetic and copies ran while one was open for 0% -> 0% of each run, Pallas kernels for 2% -> 2%
where the time goes in v8:
time: 197 us; the launch traced here: 196 us
  blocking collectives  81.7 us (41%)
  starting transfers between devices  65.4 us (33%)
  waiting for transfers between devices  22.8 us (12%)
  Pallas kernels  21.2 us (11%)
    all_to_all x4, blocking collectives, exchange(): lax.all_to_all(pieces, axes, 0, 0, axis_index_groups=groups, tiled=True)  53.8 us
    ppermute x7, starting transfers between devices, gather_states(): below[at].append(lax.ppermute(below[at][-1], axes, down))  38.1 us
    all_to_all x1, blocking collectives, gather_states(): lax.all_to_all(copies, axes, 0, 0, axis_index_groups=line_places(*sizes),...  25.3 us
    pallas_call x1, Pallas kernels, per_device(): call(factor_and_solve, [jax.ShapeDtypeStruct((own_rows, kstates), f32), j...  15 us
    all_to_all x1, waiting for transfers between devices, per_device(): parts = lax.all_to_all(keep + other, 'x', 0, 0, tiled=True)  14.4 us
    ppermute x7, starting transfers between devices, gather_states(): above[at].append(lax.ppermute(above[at][-1], axes, up))  13.4 us
    ppermute x1, starting transfers between devices, per_device(): other = lax.ppermute(send, 'k', [(0, 1), (1, 0)])  6.69 us
    pallas_call x3, Pallas kernels, products(): call(functools.partial(tile_products, ids, first_place, bool(base)), [jax...  5.39 us
  transfers between devices with their start and end apart: 17, of which 5 were waited for; matrix products, arithmetic and copies ran while one was open for 0% of the time, Pallas kernels for 2%

profile of v8, /device:TPU:1, one launch (start us, length us, event | category | flops | bytes accessed | tf_op | source)
XLA Modules:
  0.0 195.9 jit_solution(5143034959414042653)
XLA Ops:
  0.6 1.0 broadcast_in_dim.8
  1.7 25.3 %all_to_all.35 = bf16[8,128,512]{2,1,0:T(8,128)(2,1)S(1)} all-to-all(bf16[8,128,512]{2,1,0:T(8,128)(2,1)S(1)} %broadcast_in_dim.8), channel_id=1, replica_groups={{0,8,16,24,32,40,48,56},{1,65,129,193,257,321,385,449},{64,72,80,88,96,..., dimensions={0} | all-to-all | bytes 2097152 | tf_op jit(solution)/shard_map/all_to_all | solution.py:191
  27.1 10.7 %collective-permute-start.10 = (bf16[4,128,512]{2,1,0:T(8,128)(2,1)S(1)}, bf16[4,128,512]{2,1,0:T(8,128)(2,1)S(1)}, u32[]{:S(2)}, u32[]{:S(2)}) collective-permute-start(bf16[4,128,512]{2,1,0:T(8,128)(2,1)S(1)} %get-tuple-element.10.refs_6_), channel_id=1, source_target_pairs={{0,448},{1,57},{8,456},{9,1},{16,464},{17,9},{24,472},{25,17},{32,... | collective-permute-start | bytes 1572872 | tf_op jit(solution)/shard_map/ppermute | solution.py:201
  37.7 1.9 collective-permute-start
  39.7 4.6 %collective-permute-start.4 = (bf16[4,128,512]{2,1,0:T(8,128)(2,1)S(1)}, bf16[4,128,512]{2,1,0:T(8,128)(2,1)S(1)}, u32[]{:S(2)}, u32[]{:S(2)}) collective-permute-start(bf16[4,128,512]{2,1,0:T(8,128)(2,1)S(1)} %get-tuple-element.11.refs_0_), channel_id=1, source_target_pairs={{0,448},{1,57},{8,456},{9,1},{16,464},{17,9},{24,472},{25,17},{32,... | collective-permute-start | bytes 1572872 | tf_op jit(solution)/shard_map/ppermute | solution.py:201
  44.3 1.9 collective-permute-start.7
  46.2 4.6 %collective-permute-start.11 = (bf16[4,128,512]{2,1,0:T(8,128)(2,1)S(1)}, bf16[4,128,512]{2,1,0:T(8,128)(2,1)}, u32[]{:S(2)}, u32[]{:S(2)}) collective-permute-start(bf16[4,128,512]{2,1,0:T(8,128)(2,1)S(1)} %collective-permute-done.10.refs_11_), channel_id=1, source_target_pairs={{0,448},{1,57},{8,456},{9,1},{16,464},{17,9},{24,472},{25,17},{32,... | collective-permute-start | bytes 1572872 | tf_op jit(solution)/shard_map/ppermute | solution.py:201
  50.8 1.9 collective-permute-start.1
  52.7 4.6 %collective-permute-start.5 = (bf16[4,128,512]{2,1,0:T(8,128)(2,1)S(1)}, bf16[4,128,512]{2,1,0:T(8,128)(2,1)}, u32[]{:S(2)}, u32[]{:S(2)}) collective-permute-start(bf16[4,128,512]{2,1,0:T(8,128)(2,1)S(1)} %collective-permute-done.4.refs_5_), channel_id=1, source_target_pairs={{0,448},{1,57},{8,456},{9,1},{16,464},{17,9},{24,472},{25,17},{32,... | collective-permute-start | bytes 1572872 | tf_op jit(solution)/shard_map/ppermute | solution.py:201
  57.3 1.9 collective-permute-start.8
  59.3 4.6 %collective-permute-start.12 = (bf16[4,128,512]{2,1,0:T(8,128)(2,1)}, bf16[4,128,512]{2,1,0:T(8,128)(2,1)}, u32[]{:S(2)}, u32[]{:S(2)}) collective-permute-start(bf16[4,128,512]{2,1,0:T(8,128)(2,1)} %collective-permute-done.11.refs_10_), channel_id=1, source_target_pairs={{0,448},{1,57},{8,456},{9,1},{16,464},{17,9},{24,472},{25,17},{32,... | collective-permute-start | bytes 1572872 | tf_op jit(solution)/shard_map/ppermute | solution.py:201
  63.9 1.9 collective-permute-start.2
  66.5 4.6 %collective-permute-start.6 = (bf16[4,128,512]{2,1,0:T(8,128)(2,1)}, bf16[4,128,512]{2,1,0:T(8,128)(2,1)S(1)}, u32[]{:S(2)}, u32[]{:S(2)}) collective-permute-start(bf16[4,128,512]{2,1,0:T(8,128)(2,1)} %collective-permute-done.5.refs_4_), channel_id=1, source_target_pairs={{0,448},{1,57},{8,456},{9,1},{16,464},{17,9},{24,472},{25,17},{32,... | collective-permute-start | bytes 1572872 | tf_op jit(solution)/shard_map/ppermute | solution.py:201
  71.0 1.9 collective-permute-start.9
  73.0 4.6 %collective-permute-start.13 = (bf16[4,128,512]{2,1,0:T(8,128)(2,1)}, bf16[4,128,512]{2,1,0:T(8,128)(2,1)S(1)}, u32[]{:S(2)}, u32[]{:S(2)}) collective-permute-start(bf16[4,128,512]{2,1,0:T(8,128)(2,1)} %collective-permute-done.12.refs_9_), channel_id=1, source_target_pairs={{0,448},{1,57},{8,456},{9,1},{16,464},{17,9},{24,472},{25,17},{32,... | collective-permute-start | bytes 1572872 | tf_op jit(solution)/shard_map/ppermute | solution.py:201
  77.6 1.9 collective-permute-start.3
  79.6 3.3 %shard_map.77.refs_4_ = f32[8,128,512]{2,1,0:T(8,128)S(1)} custom-call(s32[73]{0:T(128)S(1)} %pad_add_fusion.meta_ref, bf16[24,128,128]{2,1,0:T(8,128)(2,1)S(1)} %bitcast.37, bf16[4,128,512]{2,1,0:T(8,128)(2,1)S(1)} %get-tuple-element.11.refs_0_, bf16[4,128,512]{2,1,0:T(8,128)(2,1)S(1)} %collective-permute-done.refs_1_, ...), custom_call_target="tpu_custom_call" | custom-call | tf_op jit(solution)/shard_map/pallas_call | solution.py:270
  83.0 1.0 collective-permute-done.13.refs_3_
  84.0 5.2 %collective-permute-done.3.refs_0_ = bf16[4,128,512]{2,1,0:T(8,128)(2,1)S(1)} collective-permute-done((bf16[4,128,512]{2,1,0:T(8,128)(2,1)}, bf16[4,128,512]{2,1,0:T(8,128)(2,1)S(1)}, u32[]{:S(2)}, u32[]{:S(2)}) %collective-permute-start.3) | collective-permute-done | bytes 524320 | tf_op jit(solution)/shard_map/ppermute | solution.py:199
  90.0 6.7 %collective-permute-start.14 = (f32[4,128,512]{2,1,0:T(8,128)S(1)}, f32[4,128,512]{2,1,0:T(8,128)S(1)}, u32[]{:S(2)}, u32[]{:S(2)}) collective-permute-start(f32[4,128,512]{2,1,0:T(8,128)S(1)} %shard_map.79), channel_id=1, source_target_pairs={{0,1},{1,0},{2,3},{3,2},{4,5},{5,4},{6,7},{7,6},{8,9},{9,8},{10,11... | collective-permute-start | bytes 3145736 | tf_op jit(solution)/shard_map/ppermute | solution.py:280
  96.7 1.3 shard_map.78
  98.9 1.2 add.47
  100.1 3.7 %all-to-all-start.1 = ((f32[4,128,512]{2,1,0:T(8,128)}), f32[4,128,512]{2,1,0:T(8,128)S(1)}, u32[]{:S(2)}, u32[]{:S(2)}) async-start(f32[4,128,512]{2,1,0:T(8,128)} %add.47), calls=%async_computation.1 | async-start | bytes 2097152 | tf_op jit(solution)/shard_map/all_to_all | solution.py:282
  103.9 14.4 %all-to-all-done.1.parts_ref = f32[4,128,512]{2,1,0:T(8,128)S(1)} async-done(((f32[4,128,512]{2,1,0:T(8,128)}), f32[4,128,512]{2,1,0:T(8,128)S(1)}, u32[]{:S(2)}, u32[]{:S(2)}) %all-to-all-start.1) | async-done | bytes 1048608 | tf_op jit(solution)/shard_map/all_to_all | solution.py:282
  119.1 3.4 %collective-permute-start.15 = (f32[5,128,128]{2,1,0:T(8,128)S(1)}, f32[5,128,128]{2,1,0:T(8,128)S(1)}, u32[]{:S(2)}, u32[]{:S(2)}) collective-permute-start(f32[5,128,128]{2,1,0:T(8,128)S(1)} %get-tuple-element.6), channel_id=1, source_target_pairs={{0,1},{1,0},{2,3},{3,2},{4,5},{5,4},{6,7},{7,6},{8,9},{9,8},{10,11... | collective-permute-start | bytes 983048 | tf_op jit(solution)/shard_map/ppermute | solution.py:291
  122.6 1.2 collective-permute-done.15
  123.9 7.8 %all_to_all.36 = f32[4,160,128]{2,1,0:T(8,128)S(1)} all-to-all(f32[4,160,128]{2,1,0:T(8,128)S(1)} %bitcast.40), channel_id=1, replica_groups={{0,2,4,6},{8,10,12,14},{16,18,20,22},{24,26,28,30},{32,34,36,38},{40,42..., dimensions={0} | all-to-all | bytes 655360 | tf_op jit(solution)/shard_map/all_to_all | solution.py:239
  131.8 20.0 %all_to_all.37 = f32[64,1,320]{2,1,0:T(1,128)S(1)} all-to-all(f32[64,1,320]{2,1,0:T(1,128)S(1)} %all_to_all.25), channel_id=1, replica_groups={{0,8,16,24,32,40,48,56,64,72,80,88,96,104,112,120,128,136,144,152,160,1..., dimensions={0} | all-to-all | bytes 163840 | tf_op jit(solution)/shard_map/all_to_all | solution.py:239
  152.0 18.2 %all_to_all.38 = f32[64,1,320]{2,1,0:T(1,128)S(1)} all-to-all(f32[64,1,320]{2,1,0:T(1,128)S(1)} %broadcast_in_dim.9), channel_id=1, replica_groups={{0,8,16,24,32,40,48,56,64,72,80,88,96,104,112,120,128,136,144,152,160,1..., dimensions={0} | all-to-all | bytes 163840 | tf_op jit(solution)/shard_map/all_to_all | solution.py:239
  170.6 7.8 %all_to_all.39 = f32[4,160,128]{2,1,0:T(8,128)S(1)} all-to-all(f32[4,160,128]{2,1,0:T(8,128)S(1)} %broadcast_in_dim.11), channel_id=1, replica_groups={{0,2,4,6},{8,10,12,14},{16,18,20,22},{24,26,28,30},{32,34,36,38},{40,42..., dimensions={0} | all-to-all | bytes 655360 | tf_op jit(solution)/shard_map/all_to_all | solution.py:239
  178.3 2.6 %all_gather.3.gram_ref = f32[10,128,128]{2,1,0:T(8,128)S(1)} all-gather(f32[5,128,128]{2,1,0:T(8,128)S(1)} %bitcast.41), channel_id=1, replica_groups=mesh['y'=8,'z'=8,'x'=4,'k'=2] {'k'}, dimensions={0}, use_global_device_ids=true | all-gather | bytes 983040 | tf_op jit(solution)/shard_map/all_gather | solution.py:292
  180.9 15.0 %shard_map.81 = (f32[128,512]{1,0:T(8,128)}, f32[512,512]{1,0:T(8,128)}) custom-call(f32[10,128,128]{2,1,0:T(8,128)S(1)} %all_gather.3.gram_ref, f32[128,512]{1,0:T(8,128)S(1)} %get-tuple-element.7.applied_ref), custom_call_target="tpu_custom_call" | custom-call | tf_op jit(solution)/shard_map/pallas_call | solution.py:294
  (38 shorter events, 3.5 us)
Async XLA Ops:
  1.6 77.9 %copy-start.2 = (s32[1,1,24]{2,1,0:T(1,128)S(1)}, s32[1,1,24]{2,1,0:T(1,128)}, u32[]{:S(2)}) copy-start(s32[1,1,24]{2,1,0:T(1,128)} %param.10) | copy-start | bytes 292
  1.6 77.9 %copy-start.4 = (s32[1,1,24]{2,1,0:T(1,128)S(1)}, s32[1,1,24]{2,1,0:T(1,128)}, u32[]{:S(2)}) copy-start(s32[1,1,24]{2,1,0:T(1,128)} %param.9) | copy-start | bytes 292
  1.6 78.0 %copy-start = (bf16[1,1,24,128,128]{4,3,2,1,0:T(8,128)(2,1)S(1)}, bf16[1,1,24,128,128]{4,3,2,1,0:T(8,128)(2,1)}, u32[]{:S(2)}) copy-start(bf16[1,1,24,128,128]{4,3,2,1,0:T(8,128)(2,1)} %param.8) | copy-start | bytes 2359300
  27.1 19.1 %collective-permute-start.10 = (bf16[4,128,512]{2,1,0:T(8,128)(2,1)S(1)}, bf16[4,128,512]{2,1,0:T(8,128)(2,1)S(1)}, u32[]{:S(2)}, u32[]{:S(2)}) collective-permute-start(bf16[4,128,512]{2,1,0:T(8,128)(2,1)S(1)} %get-tuple-element.10.refs_6_), channel_id=1, source_target_pairs={{0,448},{1,57},{8,456},{9,1},{16,464},{17,9},{24,472},{25,17},{32,... | collective-permute-start | bytes 1572872 | tf_op jit(solution)/shard_map/ppermute | solution.py:201
  37.7 13.0 %collective-permute-start = (bf16[4,128,512]{2,1,0:T(8,128)(2,1)S(1)}, bf16[4,128,512]{2,1,0:T(8,128)(2,1)S(1)}, u32[]{:S(2)}, u32[]{:S(2)}) collective-permute-start(bf16[4,128,512]{2,1,0:T(8,128)(2,1)S(1)} %get-tuple-element.11.refs_0_), channel_id=1, source_target_pairs={{0,64},{1,9},{8,72},{9,17},{16,80},{17,25},{24,88},{25,33},{32,96}... | collective-permute-start | bytes 1572872 | tf_op jit(solution)/shard_map/ppermute | solution.py:199
  39.7 13.0 %collective-permute-start.4 = (bf16[4,128,512]{2,1,0:T(8,128)(2,1)S(1)}, bf16[4,128,512]{2,1,0:T(8,128)(2,1)S(1)}, u32[]{:S(2)}, u32[]{:S(2)}) collective-permute-start(bf16[4,128,512]{2,1,0:T(8,128)(2,1)S(1)} %get-tuple-element.11.refs_0_), channel_id=1, source_target_pairs={{0,448},{1,57},{8,456},{9,1},{16,464},{17,9},{24,472},{25,17},{32,... | collective-permute-start | bytes 1572872 | tf_op jit(solution)/shard_map/ppermute | solution.py:201
  44.3 13.1 %collective-permute-start.7 = (bf16[4,128,512]{2,1,0:T(8,128)(2,1)S(1)}, bf16[4,128,512]{2,1,0:T(8,128)(2,1)}, u32[]{:S(2)}, u32[]{:S(2)}) collective-permute-start(bf16[4,128,512]{2,1,0:T(8,128)(2,1)S(1)} %get-tuple-element.10.refs_6_), channel_id=1, source_target_pairs={{0,64},{1,9},{8,72},{9,17},{16,80},{17,25},{24,88},{25,33},{32,96}... | collective-permute-start | bytes 1572872 | tf_op jit(solution)/shard_map/ppermute | solution.py:199
  46.2 13.1 %collective-permute-start.11 = (bf16[4,128,512]{2,1,0:T(8,128)(2,1)S(1)}, bf16[4,128,512]{2,1,0:T(8,128)(2,1)}, u32[]{:S(2)}, u32[]{:S(2)}) collective-permute-start(bf16[4,128,512]{2,1,0:T(8,128)(2,1)S(1)} %collective-permute-done.10.refs_11_), channel_id=1, source_target_pairs={{0,448},{1,57},{8,456},{9,1},{16,464},{17,9},{24,472},{25,17},{32,... | collective-permute-start | bytes 1572872 | tf_op jit(solution)/shard_map/ppermute | solution.py:201
  50.8 13.1 %collective-permute-start.1 = (bf16[4,128,512]{2,1,0:T(8,128)(2,1)S(1)}, bf16[4,128,512]{2,1,0:T(8,128)(2,1)}, u32[]{:S(2)}, u32[]{:S(2)}) collective-permute-start(bf16[4,128,512]{2,1,0:T(8,128)(2,1)S(1)} %collective-permute-done.refs_1_), channel_id=1, source_target_pairs={{0,64},{1,9},{8,72},{9,17},{16,80},{17,25},{24,88},{25,33},{32,96}... | collective-permute-start | bytes 1572872 | tf_op jit(solution)/shard_map/ppermute | solution.py:199
  52.7 13.7 %collective-permute-start.5 = (bf16[4,128,512]{2,1,0:T(8,128)(2,1)S(1)}, bf16[4,128,512]{2,1,0:T(8,128)(2,1)}, u32[]{:S(2)}, u32[]{:S(2)}) collective-permute-start(bf16[4,128,512]{2,1,0:T(8,128)(2,1)S(1)} %collective-permute-done.4.refs_5_), channel_id=1, source_target_pairs={{0,448},{1,57},{8,456},{9,1},{16,464},{17,9},{24,472},{25,17},{32,... | collective-permute-start | bytes 1572872 | tf_op jit(solution)/shard_map/ppermute | solution.py:201
  57.3 13.7 %collective-permute-start.8 = (bf16[4,128,512]{2,1,0:T(8,128)(2,1)}, bf16[4,128,512]{2,1,0:T(8,128)(2,1)}, u32[]{:S(2)}, u32[]{:S(2)}) collective-permute-start(bf16[4,128,512]{2,1,0:T(8,128)(2,1)} %collective-permute-done.7.refs_7_), channel_id=1, source_target_pairs={{0,64},{1,9},{8,72},{9,17},{16,80},{17,25},{24,88},{25,33},{32,96}... | collective-permute-start | bytes 1572872 | tf_op jit(solution)/shard_map/ppermute | solution.py:199
  59.3 13.7 %collective-permute-start.12 = (bf16[4,128,512]{2,1,0:T(8,128)(2,1)}, bf16[4,128,512]{2,1,0:T(8,128)(2,1)}, u32[]{:S(2)}, u32[]{:S(2)}) collective-permute-start(bf16[4,128,512]{2,1,0:T(8,128)(2,1)} %collective-permute-done.11.refs_10_), channel_id=1, source_target_pairs={{0,448},{1,57},{8,456},{9,1},{16,464},{17,9},{24,472},{25,17},{32,... | collective-permute-start | bytes 1572872 | tf_op jit(solution)/shard_map/ppermute | solution.py:201
  63.9 13.7 %collective-permute-start.2 = (bf16[4,128,512]{2,1,0:T(8,128)(2,1)}, bf16[4,128,512]{2,1,0:T(8,128)(2,1)}, u32[]{:S(2)}, u32[]{:S(2)}) collective-permute-start(bf16[4,128,512]{2,1,0:T(8,128)(2,1)} %collective-permute-done.1.refs_2_), channel_id=1, source_target_pairs={{0,64},{1,9},{8,72},{9,17},{16,80},{17,25},{24,88},{25,33},{32,96}... | collective-permute-start | bytes 1572872 | tf_op jit(solution)/shard_map/ppermute | solution.py:199
  66.5 16.5 %collective-permute-start.6 = (bf16[4,128,512]{2,1,0:T(8,128)(2,1)}, bf16[4,128,512]{2,1,0:T(8,128)(2,1)S(1)}, u32[]{:S(2)}, u32[]{:S(2)}) collective-permute-start(bf16[4,128,512]{2,1,0:T(8,128)(2,1)} %collective-permute-done.5.refs_4_), channel_id=1, source_target_pairs={{0,448},{1,57},{8,456},{9,1},{16,464},{17,9},{24,472},{25,17},{32,... | collective-permute-start | bytes 1572872 | tf_op jit(solution)/shard_map/ppermute | solution.py:201
  71.0 11.9 %collective-permute-start.9 = (bf16[4,128,512]{2,1,0:T(8,128)(2,1)}, bf16[4,128,512]{2,1,0:T(8,128)(2,1)S(1)}, u32[]{:S(2)}, u32[]{:S(2)}) collective-permute-start(bf16[4,128,512]{2,1,0:T(8,128)(2,1)} %collective-permute-done.8.refs_8_), channel_id=1, source_target_pairs={{0,64},{1,9},{8,72},{9,17},{16,80},{17,25},{24,88},{25,33},{32,96}... | collective-permute-start | bytes 1572872 | tf_op jit(solution)/shard_map/ppermute | solution.py:199
  73.0 11.0 %collective-permute-start.13 = (bf16[4,128,512]{2,1,0:T(8,128)(2,1)}, bf16[4,128,512]{2,1,0:T(8,128)(2,1)S(1)}, u32[]{:S(2)}, u32[]{:S(2)}) collective-permute-start(bf16[4,128,512]{2,1,0:T(8,128)(2,1)} %collective-permute-done.12.refs_9_), channel_id=1, source_target_pairs={{0,448},{1,57},{8,456},{9,1},{16,464},{17,9},{24,472},{25,17},{32,... | collective-permute-start | bytes 1572872 | tf_op jit(solution)/shard_map/ppermute | solution.py:201
  77.6 11.6 %collective-permute-start.3 = (bf16[4,128,512]{2,1,0:T(8,128)(2,1)}, bf16[4,128,512]{2,1,0:T(8,128)(2,1)S(1)}, u32[]{:S(2)}, u32[]{:S(2)}) collective-permute-start(bf16[4,128,512]{2,1,0:T(8,128)(2,1)} %collective-permute-done.2.refs_3_), channel_id=1, source_target_pairs={{0,64},{1,9},{8,72},{9,17},{16,80},{17,25},{24,88},{25,33},{32,96}... | collective-permute-start | bytes 1572872 | tf_op jit(solution)/shard_map/ppermute | solution.py:199
  90.0 9.0 %collective-permute-start.14 = (f32[4,128,512]{2,1,0:T(8,128)S(1)}, f32[4,128,512]{2,1,0:T(8,128)S(1)}, u32[]{:S(2)}, u32[]{:S(2)}) collective-permute-start(f32[4,128,512]{2,1,0:T(8,128)S(1)} %shard_map.79), channel_id=1, source_target_pairs={{0,1},{1,0},{2,3},{3,2},{4,5},{5,4},{6,7},{7,6},{8,9},{9,8},{10,11... | collective-permute-start | bytes 3145736 | tf_op jit(solution)/shard_map/ppermute | solution.py:280
  98.0 5.8 %copy-start.1 = (bf16[128,512]{1,0:T(8,128)(2,1)S(1)}, bf16[128,512]{1,0:T(8,128)(2,1)}, u32[]{:S(2)}) copy-start(bf16[128,512]{1,0:T(8,128)(2,1)} %param.6) | copy-start | bytes 393220
  98.0 5.8 %copy-start.3 = (f32[128]{0:T(128)S(1)}, f32[128]{0:T(128)}, u32[]{:S(2)}) copy-start(f32[128]{0:T(128)} %param.7) | copy-start | bytes 1540
  100.1 18.2 %all-to-all-start.1 = ((f32[4,128,512]{2,1,0:T(8,128)}), f32[4,128,512]{2,1,0:T(8,128)S(1)}, u32[]{:S(2)}, u32[]{:S(2)}) async-start(f32[4,128,512]{2,1,0:T(8,128)} %add.47), calls=%async_computation.1 | async-start | bytes 2097152 | tf_op jit(solution)/shard_map/all_to_all | solution.py:282
  119.1 4.7 %collective-permute-start.15 = (f32[5,128,128]{2,1,0:T(8,128)S(1)}, f32[5,128,128]{2,1,0:T(8,128)S(1)}, u32[]{:S(2)}, u32[]{:S(2)}) collective-permute-start(f32[5,128,128]{2,1,0:T(8,128)S(1)} %get-tuple-element.6), channel_id=1, source_target_pairs={{0,1},{1,0},{2,3},{3,2},{4,5},{5,4},{6,7},{7,6},{8,9},{9,8},{10,11... | collective-permute-start | bytes 983048 | tf_op jit(solution)/shard_map/ppermute | solution.py:291

commit v9 on v8

--- a/solution.py
+++ b/solution.py
@@ -241,9 +241,10 @@
     def copies(piece, groups):
         return jnp.broadcast_to(piece[None], (len(groups[0]),) + piece.shape)
 
-    part = exchange(value.reshape(len(four[0]), -1, value.shape[-1]), four).sum(0)
-    piece = exchange(part.reshape(len(same[0]), -1), same).sum(0)
-    part = exchange(copies(piece, same), same).reshape(part.shape)
+    fours = len(four[0])
+    every = [sum(same[:fours], []), sum(same[fours:], [])]
+    piece = exchange(value.reshape(len(every[0]), -1), every).sum(0)
+    part = exchange(copies(piece, same), same).reshape(-1, value.shape[-1])
     return exchange(copies(part, four), four).reshape(value.shape)
 
 
@@ -288,7 +289,8 @@
         [jax.ShapeDtypeStruct((own_rows, kstates), f32), half, half],
         [sm, vm, vm],
     )(k.astype(jnp.int32).reshape(1), parts, local)
-    own = sum_halves(own + lax.ppermute(other, "k", [(0, 1), (1, 0)]))
+    others = lax.all_gather(other, "k", axis=0)
+    own = sum_halves(own + lax.dynamic_index_in_dim(others, 1 - k, 0, keepdims=False))
     gram = lax.all_gather(own, "k", axis=0, tiled=True)
 
     states, upper = call(

time: 197 us -> 197 us (level)
  blocking collectives: 81.7 us -> 85.1 us
  starting transfers between devices: 65.4 us -> 62.1 us
    ppermute x1 -> x0, starting transfers between devices: 3.42 us -> none  [per_device(): own = sum_halves(own + lax.ppermute(other, 'k', [(0, 1), (1, 0)]))]
    all_gather x0 -> x1, blocking collectives: none -> 3.15 us  [per_device(): others = lax.all_gather(other, 'k', axis=0)]
    all_to_all x4 -> x3, blocking collectives: 53.8 us -> 54.1 us  [exchange(): lax.all_to_all(pieces, axes, 0, 0, axis_index_groups=groups, tiled=True)]
  transfers between devices with their start and end apart: 17 -> 16, of which waited for: 5 -> 3; matrix products, arithmetic and copies ran while one was open for 0% -> 0% of each run, Pallas kernels for 2% -> 3%
where the time goes in v9:
time: 197 us; the launch traced here: 196 us
  blocking collectives  85.1 us (43%)
  starting transfers between devices  62.1 us (32%)
  Pallas kernels  22.2 us (11%)
  waiting for transfers between devices  20.9 us (11%)
    all_to_all x3, blocking collectives, exchange(): lax.all_to_all(pieces, axes, 0, 0, axis_index_groups=groups, tiled=True)  54.1 us
    ppermute x7, starting transfers between devices, gather_states(): below[at].append(lax.ppermute(below[at][-1], axes, down))  38.1 us
    all_to_all x1, blocking collectives, gather_states(): lax.all_to_all(copies, axes, 0, 0, axis_index_groups=line_places(*sizes),...  25.3 us
    pallas_call x1, Pallas kernels, per_device(): call(factor_and_solve, [jax.ShapeDtypeStruct((own_rows, kstates), f32), j...  15 us
    all_to_all x1, waiting for transfers between devices, per_device(): parts = lax.all_to_all(keep + other, 'x', 0, 0, tiled=True)  14.6 us
    ppermute x7, starting transfers between devices, gather_states(): above[at].append(lax.ppermute(above[at][-1], axes, up))  13.4 us
    ppermute x1, starting transfers between devices, per_device(): other = lax.ppermute(send, 'k', [(0, 1), (1, 0)])  7 us
    pallas_call x3, Pallas kernels, products(): call(functools.partial(tile_products, ids, first_place, bool(base)), [jax...  6.43 us
  transfers between devices with their start and end apart: 16, of which 3 were waited for; matrix products, arithmetic and copies ran while one was open for 0% of the time, Pallas kernels for 3%

profile of v9, /device:TPU:1, one launch (start us, length us, event | category | flops | bytes accessed | tf_op | source)
XLA Modules:
  0.0 195.7 jit_solution(2338944177307422230)
XLA Ops:
  0.6 1.0 broadcast_in_dim.8
  1.7 25.3 %all_to_all.31 = bf16[8,128,512]{2,1,0:T(8,128)(2,1)S(1)} all-to-all(bf16[8,128,512]{2,1,0:T(8,128)(2,1)S(1)} %broadcast_in_dim.8), channel_id=1, replica_groups={{0,8,16,24,32,40,48,56},{1,65,129,193,257,321,385,449},{64,72,80,88,96,..., dimensions={0} | all-to-all | bytes 2097152 | tf_op jit(solution)/shard_map/all_to_all | solution.py:191
  27.1 10.7 %collective-permute-start.10 = (bf16[4,128,512]{2,1,0:T(8,128)(2,1)S(1)}, bf16[4,128,512]{2,1,0:T(8,128)(2,1)S(1)}, u32[]{:S(2)}, u32[]{:S(2)}) collective-permute-start(bf16[4,128,512]{2,1,0:T(8,128)(2,1)S(1)} %get-tuple-element.10.refs_6_), channel_id=1, source_target_pairs={{0,448},{1,57},{8,456},{9,1},{16,464},{17,9},{24,472},{25,17},{32,... | collective-permute-start | bytes 1572872 | tf_op jit(solution)/shard_map/ppermute | solution.py:201
  37.7 1.9 collective-permute-start
  39.7 4.6 %collective-permute-start.4 = (bf16[4,128,512]{2,1,0:T(8,128)(2,1)S(1)}, bf16[4,128,512]{2,1,0:T(8,128)(2,1)S(1)}, u32[]{:S(2)}, u32[]{:S(2)}) collective-permute-start(bf16[4,128,512]{2,1,0:T(8,128)(2,1)S(1)} %get-tuple-element.11.refs_0_), channel_id=1, source_target_pairs={{0,448},{1,57},{8,456},{9,1},{16,464},{17,9},{24,472},{25,17},{32,... | collective-permute-start | bytes 1572872 | tf_op jit(solution)/shard_map/ppermute | solution.py:201
  44.3 1.9 collective-permute-start.7
  46.2 4.6 %collective-permute-start.11 = (bf16[4,128,512]{2,1,0:T(8,128)(2,1)S(1)}, bf16[4,128,512]{2,1,0:T(8,128)(2,1)}, u32[]{:S(2)}, u32[]{:S(2)}) collective-permute-start(bf16[4,128,512]{2,1,0:T(8,128)(2,1)S(1)} %collective-permute-done.10.refs_11_), channel_id=1, source_target_pairs={{0,448},{1,57},{8,456},{9,1},{16,464},{17,9},{24,472},{25,17},{32,... | collective-permute-start | bytes 1572872 | tf_op jit(solution)/shard_map/ppermute | solution.py:201
  50.8 1.9 collective-permute-start.1
  52.7 4.6 %collective-permute-start.5 = (bf16[4,128,512]{2,1,0:T(8,128)(2,1)S(1)}, bf16[4,128,512]{2,1,0:T(8,128)(2,1)}, u32[]{:S(2)}, u32[]{:S(2)}) collective-permute-start(bf16[4,128,512]{2,1,0:T(8,128)(2,1)S(1)} %collective-permute-done.4.refs_5_), channel_id=1, source_target_pairs={{0,448},{1,57},{8,456},{9,1},{16,464},{17,9},{24,472},{25,17},{32,... | collective-permute-start | bytes 1572872 | tf_op jit(solution)/shard_map/ppermute | solution.py:201
  57.3 1.9 collective-permute-start.8
  59.3 4.6 %collective-permute-start.12 = (bf16[4,128,512]{2,1,0:T(8,128)(2,1)}, bf16[4,128,512]{2,1,0:T(8,128)(2,1)}, u32[]{:S(2)}, u32[]{:S(2)}) collective-permute-start(bf16[4,128,512]{2,1,0:T(8,128)(2,1)} %collective-permute-done.11.refs_10_), channel_id=1, source_target_pairs={{0,448},{1,57},{8,456},{9,1},{16,464},{17,9},{24,472},{25,17},{32,... | collective-permute-start | bytes 1572872 | tf_op jit(solution)/shard_map/ppermute | solution.py:201
  63.9 1.9 collective-permute-start.2
  66.5 4.6 %collective-permute-start.6 = (bf16[4,128,512]{2,1,0:T(8,128)(2,1)}, bf16[4,128,512]{2,1,0:T(8,128)(2,1)S(1)}, u32[]{:S(2)}, u32[]{:S(2)}) collective-permute-start(bf16[4,128,512]{2,1,0:T(8,128)(2,1)} %collective-permute-done.5.refs_4_), channel_id=1, source_target_pairs={{0,448},{1,57},{8,456},{9,1},{16,464},{17,9},{24,472},{25,17},{32,... | collective-permute-start | bytes 1572872 | tf_op jit(solution)/shard_map/ppermute | solution.py:201
  71.0 1.9 collective-permute-start.9
  73.0 4.6 %collective-permute-start.13 = (bf16[4,128,512]{2,1,0:T(8,128)(2,1)}, bf16[4,128,512]{2,1,0:T(8,128)(2,1)S(1)}, u32[]{:S(2)}, u32[]{:S(2)}) collective-permute-start(bf16[4,128,512]{2,1,0:T(8,128)(2,1)} %collective-permute-done.12.refs_9_), channel_id=1, source_target_pairs={{0,448},{1,57},{8,456},{9,1},{16,464},{17,9},{24,472},{25,17},{32,... | collective-permute-start | bytes 1572872 | tf_op jit(solution)/shard_map/ppermute | solution.py:201
  77.6 1.9 collective-permute-start.3
  79.6 4.5 %shard_map.77.refs_4_ = f32[8,128,512]{2,1,0:T(8,128)S(1)} custom-call(s32[73]{0:T(128)S(1)} %pad_add_fusion.meta_ref, bf16[24,128,128]{2,1,0:T(8,128)(2,1)S(1)} %bitcast.39, bf16[4,128,512]{2,1,0:T(8,128)(2,1)S(1)} %get-tuple-element.11.refs_0_, bf16[4,128,512]{2,1,0:T(8,128)(2,1)S(1)} %collective-permute-done.refs_1_, ...), custom_call_target="tpu_custom_call" | custom-call | tf_op jit(solution)/shard_map/pallas_call | solution.py:271
  84.2 5.0 %collective-permute-done.3.refs_0_ = bf16[4,128,512]{2,1,0:T(8,128)(2,1)S(1)} collective-permute-done((bf16[4,128,512]{2,1,0:T(8,128)(2,1)}, bf16[4,128,512]{2,1,0:T(8,128)(2,1)S(1)}, u32[]{:S(2)}, u32[]{:S(2)}) %collective-permute-start.3) | collective-permute-done | bytes 524320 | tf_op jit(solution)/shard_map/ppermute | solution.py:199
  89.2 0.9 shard_map.79
  90.1 7.0 %collective-permute-start.14 = (f32[4,128,512]{2,1,0:T(8,128)S(1)}, f32[4,128,512]{2,1,0:T(8,128)S(1)}, u32[]{:S(2)}, u32[]{:S(2)}) collective-permute-start(f32[4,128,512]{2,1,0:T(8,128)S(1)} %shard_map.79), channel_id=1, source_target_pairs={{0,1},{1,0},{2,3},{3,2},{4,5},{5,4},{6,7},{7,6},{8,9},{9,8},{10,11... | collective-permute-start | bytes 3145736 | tf_op jit(solution)/shard_map/ppermute | solution.py:281
  97.1 1.1 shard_map.78
  98.2 1.1 collective-permute-done.14
  99.3 1.2 add.52
  100.5 3.5 %all-to-all-start.1 = ((f32[4,128,512]{2,1,0:T(8,128)}), f32[4,128,512]{2,1,0:T(8,128)S(1)}, u32[]{:S(2)}, u32[]{:S(2)}) async-start(f32[4,128,512]{2,1,0:T(8,128)} %add.52), calls=%async_computation.1 | async-start | bytes 2097152 | tf_op jit(solution)/shard_map/all_to_all | solution.py:283
  104.2 14.6 %all-to-all-done.1.parts_ref = f32[4,128,512]{2,1,0:T(8,128)S(1)} async-done(((f32[4,128,512]{2,1,0:T(8,128)}), f32[4,128,512]{2,1,0:T(8,128)S(1)}, u32[]{:S(2)}, u32[]{:S(2)}) %all-to-all-start.1) | async-done | bytes 1048608 | tf_op jit(solution)/shard_map/all_to_all | solution.py:283
  118.8 0.8 shard_map.80
  119.6 3.1 %all-gather = f32[10,128,128]{2,1,0:T(8,128)S(1)} all-gather(f32[5,128,128]{2,1,0:T(8,128)S(1)} %get-tuple-element.6), channel_id=2, replica_groups=mesh['y'=8,'z'=8,'x'=4,'k'=2] {'k'}, dimensions={0}, use_global_device_ids=true | all-gather | bytes 983040 | tf_op jit(solution)/shard_map/all_gather | solution.py:292
  123.3 25.1 %all_to_all.32 = f32[256,1,320]{2,1,0:T(1,128)S(1)} all-to-all(f32[256,1,320]{2,1,0:T(1,128)S(1)} %all_to_all.25), channel_id=1, replica_groups={{0,8,16,24,32,40,48,56,64,72,80,88,96,104,112,120,128,136,144,152,160,1..., dimensions={0} | all-to-all | bytes 655360 | tf_op jit(solution)/shard_map/all_to_all | solution.py:239
  148.8 21.2 %all_to_all.33 = f32[64,1,320]{2,1,0:T(1,128)S(1)} all-to-all(f32[64,1,320]{2,1,0:T(1,128)S(1)} %broadcast_in_dim.9), channel_id=1, replica_groups={{0,8,16,24,32,40,48,56,64,72,80,88,96,104,112,120,128,136,144,152,160,1..., dimensions={0} | all-to-all | bytes 163840 | tf_op jit(solution)/shard_map/all_to_all | solution.py:239
  170.4 7.8 %all_to_all.34 = f32[4,160,128]{2,1,0:T(8,128)S(1)} all-to-all(f32[4,160,128]{2,1,0:T(8,128)S(1)} %broadcast_in_dim.11), channel_id=1, replica_groups={{0,2,4,6},{8,10,12,14},{16,18,20,22},{24,26,28,30},{32,34,36,38},{40,42..., dimensions={0} | all-to-all | bytes 655360 | tf_op jit(solution)/shard_map/all_to_all | solution.py:239
  178.2 2.5 %all_gather.11.gram_ref = f32[10,128,128]{2,1,0:T(8,128)S(1)} all-gather(f32[5,128,128]{2,1,0:T(8,128)S(1)} %bitcast.43), channel_id=1, replica_groups=mesh['y'=8,'z'=8,'x'=4,'k'=2] {'k'}, dimensions={0}, use_global_device_ids=true | all-gather | bytes 983040 | tf_op jit(solution)/shard_map/all_gather | solution.py:294
  180.7 15.0 %shard_map.81 = (f32[128,512]{1,0:T(8,128)}, f32[512,512]{1,0:T(8,128)}) custom-call(f32[10,128,128]{2,1,0:T(8,128)S(1)} %all_gather.11.gram_ref, f32[128,512]{1,0:T(8,128)S(1)} %get-tuple-element.7.applied_ref), custom_call_target="tpu_custom_call" | custom-call | tf_op jit(solution)/shard_map/pallas_call | solution.py:296
  (35 shorter events, 1.6 us)
Async XLA Ops:
  1.6 77.9 %copy-start.2 = (s32[1,1,24]{2,1,0:T(1,128)S(1)}, s32[1,1,24]{2,1,0:T(1,128)}, u32[]{:S(2)}) copy-start(s32[1,1,24]{2,1,0:T(1,128)} %param.10) | copy-start | bytes 292
  1.6 77.9 %copy-start.4 = (s32[1,1,24]{2,1,0:T(1,128)S(1)}, s32[1,1,24]{2,1,0:T(1,128)}, u32[]{:S(2)}) copy-start(s32[1,1,24]{2,1,0:T(1,128)} %param.9) | copy-start | bytes 292
  1.6 78.0 %copy-start = (bf16[1,1,24,128,128]{4,3,2,1,0:T(8,128)(2,1)S(1)}, bf16[1,1,24,128,128]{4,3,2,1,0:T(8,128)(2,1)}, u32[]{:S(2)}) copy-start(bf16[1,1,24,128,128]{4,3,2,1,0:T(8,128)(2,1)} %param.8) | copy-start | bytes 2359300
  27.1 19.1 %collective-permute-start.10 = (bf16[4,128,512]{2,1,0:T(8,128)(2,1)S(1)}, bf16[4,128,512]{2,1,0:T(8,128)(2,1)S(1)}, u32[]{:S(2)}, u32[]{:S(2)}) collective-permute-start(bf16[4,128,512]{2,1,0:T(8,128)(2,1)S(1)} %get-tuple-element.10.refs_6_), channel_id=1, source_target_pairs={{0,448},{1,57},{8,456},{9,1},{16,464},{17,9},{24,472},{25,17},{32,... | collective-permute-start | bytes 1572872 | tf_op jit(solution)/shard_map/ppermute | solution.py:201
  37.7 13.0 %collective-permute-start = (bf16[4,128,512]{2,1,0:T(8,128)(2,1)S(1)}, bf16[4,128,512]{2,1,0:T(8,128)(2,1)S(1)}, u32[]{:S(2)}, u32[]{:S(2)}) collective-permute-start(bf16[4,128,512]{2,1,0:T(8,128)(2,1)S(1)} %get-tuple-element.11.refs_0_), channel_id=1, source_target_pairs={{0,64},{1,9},{8,72},{9,17},{16,80},{17,25},{24,88},{25,33},{32,96}... | collective-permute-start | bytes 1572872 | tf_op jit(solution)/shard_map/ppermute | solution.py:199
  39.7 13.0 %collective-permute-start.4 = (bf16[4,128,512]{2,1,0:T(8,128)(2,1)S(1)}, bf16[4,128,512]{2,1,0:T(8,128)(2,1)S(1)}, u32[]{:S(2)}, u32[]{:S(2)}) collective-permute-start(bf16[4,128,512]{2,1,0:T(8,128)(2,1)S(1)} %get-tuple-element.11.refs_0_), channel_id=1, source_target_pairs={{0,448},{1,57},{8,456},{9,1},{16,464},{17,9},{24,472},{25,17},{32,... | collective-permute-start | bytes 1572872 | tf_op jit(solution)/shard_map/ppermute | solution.py:201
  44.3 13.1 %collective-permute-start.7 = (bf16[4,128,512]{2,1,0:T(8,128)(2,1)S(1)}, bf16[4,128,512]{2,1,0:T(8,128)(2,1)}, u32[]{:S(2)}, u32[]{:S(2)}) collective-permute-start(bf16[4,128,512]{2,1,0:T(8,128)(2,1)S(1)} %get-tuple-element.10.refs_6_), channel_id=1, source_target_pairs={{0,64},{1,9},{8,72},{9,17},{16,80},{17,25},{24,88},{25,33},{32,96}... | collective-permute-start | bytes 1572872 | tf_op jit(solution)/shard_map/ppermute | solution.py:199
  46.2 13.1 %collective-permute-start.11 = (bf16[4,128,512]{2,1,0:T(8,128)(2,1)S(1)}, bf16[4,128,512]{2,1,0:T(8,128)(2,1)}, u32[]{:S(2)}, u32[]{:S(2)}) collective-permute-start(bf16[4,128,512]{2,1,0:T(8,128)(2,1)S(1)} %collective-permute-done.10.refs_11_), channel_id=1, source_target_pairs={{0,448},{1,57},{8,456},{9,1},{16,464},{17,9},{24,472},{25,17},{32,... | collective-permute-start | bytes 1572872 | tf_op jit(solution)/shard_map/ppermute | solution.py:201
  50.8 13.1 %collective-permute-start.1 = (bf16[4,128,512]{2,1,0:T(8,128)(2,1)S(1)}, bf16[4,128,512]{2,1,0:T(8,128)(2,1)}, u32[]{:S(2)}, u32[]{:S(2)}) collective-permute-start(bf16[4,128,512]{2,1,0:T(8,128)(2,1)S(1)} %collective-permute-done.refs_1_), channel_id=1, source_target_pairs={{0,64},{1,9},{8,72},{9,17},{16,80},{17,25},{24,88},{25,33},{32,96}... | collective-permute-start | bytes 1572872 | tf_op jit(solution)/shard_map/ppermute | solution.py:199
  52.7 13.7 %collective-permute-start.5 = (bf16[4,128,512]{2,1,0:T(8,128)(2,1)S(1)}, bf16[4,128,512]{2,1,0:T(8,128)(2,1)}, u32[]{:S(2)}, u32[]{:S(2)}) collective-permute-start(bf16[4,128,512]{2,1,0:T(8,128)(2,1)S(1)} %collective-permute-done.4.refs_5_), channel_id=1, source_target_pairs={{0,448},{1,57},{8,456},{9,1},{16,464},{17,9},{24,472},{25,17},{32,... | collective-permute-start | bytes 1572872 | tf_op jit(solution)/shard_map/ppermute | solution.py:201
  57.3 13.7 %collective-permute-start.8 = (bf16[4,128,512]{2,1,0:T(8,128)(2,1)}, bf16[4,128,512]{2,1,0:T(8,128)(2,1)}, u32[]{:S(2)}, u32[]{:S(2)}) collective-permute-start(bf16[4,128,512]{2,1,0:T(8,128)(2,1)} %collective-permute-done.7.refs_7_), channel_id=1, source_target_pairs={{0,64},{1,9},{8,72},{9,17},{16,80},{17,25},{24,88},{25,33},{32,96}... | collective-permute-start | bytes 1572872 | tf_op jit(solution)/shard_map/ppermute | solution.py:199
  59.3 13.7 %collective-permute-start.12 = (bf16[4,128,512]{2,1,0:T(8,128)(2,1)}, bf16[4,128,512]{2,1,0:T(8,128)(2,1)}, u32[]{:S(2)}, u32[]{:S(2)}) collective-permute-start(bf16[4,128,512]{2,1,0:T(8,128)(2,1)} %collective-permute-done.11.refs_10_), channel_id=1, source_target_pairs={{0,448},{1,57},{8,456},{9,1},{16,464},{17,9},{24,472},{25,17},{32,... | collective-permute-start | bytes 1572872 | tf_op jit(solution)/shard_map/ppermute | solution.py:201
  63.9 13.7 %collective-permute-start.2 = (bf16[4,128,512]{2,1,0:T(8,128)(2,1)}, bf16[4,128,512]{2,1,0:T(8,128)(2,1)}, u32[]{:S(2)}, u32[]{:S(2)}) collective-permute-start(bf16[4,128,512]{2,1,0:T(8,128)(2,1)} %collective-permute-done.1.refs_2_), channel_id=1, source_target_pairs={{0,64},{1,9},{8,72},{9,17},{16,80},{17,25},{24,88},{25,33},{32,96}... | collective-permute-start | bytes 1572872 | tf_op jit(solution)/shard_map/ppermute | solution.py:199
  66.5 17.7 %collective-permute-start.6 = (bf16[4,128,512]{2,1,0:T(8,128)(2,1)}, bf16[4,128,512]{2,1,0:T(8,128)(2,1)S(1)}, u32[]{:S(2)}, u32[]{:S(2)}) collective-permute-start(bf16[4,128,512]{2,1,0:T(8,128)(2,1)} %collective-permute-done.5.refs_4_), channel_id=1, source_target_pairs={{0,448},{1,57},{8,456},{9,1},{16,464},{17,9},{24,472},{25,17},{32,... | collective-permute-start | bytes 1572872 | tf_op jit(solution)/shard_map/ppermute | solution.py:201
  71.0 13.1 %collective-permute-start.9 = (bf16[4,128,512]{2,1,0:T(8,128)(2,1)}, bf16[4,128,512]{2,1,0:T(8,128)(2,1)S(1)}, u32[]{:S(2)}, u32[]{:S(2)}) collective-permute-start(bf16[4,128,512]{2,1,0:T(8,128)(2,1)} %collective-permute-done.8.refs_8_), channel_id=1, source_target_pairs={{0,64},{1,9},{8,72},{9,17},{16,80},{17,25},{24,88},{25,33},{32,96}... | collective-permute-start | bytes 1572872 | tf_op jit(solution)/shard_map/ppermute | solution.py:199
  73.0 11.2 %collective-permute-start.13 = (bf16[4,128,512]{2,1,0:T(8,128)(2,1)}, bf16[4,128,512]{2,1,0:T(8,128)(2,1)S(1)}, u32[]{:S(2)}, u32[]{:S(2)}) collective-permute-start(bf16[4,128,512]{2,1,0:T(8,128)(2,1)} %collective-permute-done.12.refs_9_), channel_id=1, source_target_pairs={{0,448},{1,57},{8,456},{9,1},{16,464},{17,9},{24,472},{25,17},{32,... | collective-permute-start | bytes 1572872 | tf_op jit(solution)/shard_map/ppermute | solution.py:201
  77.6 11.6 %collective-permute-start.3 = (bf16[4,128,512]{2,1,0:T(8,128)(2,1)}, bf16[4,128,512]{2,1,0:T(8,128)(2,1)S(1)}, u32[]{:S(2)}, u32[]{:S(2)}) collective-permute-start(bf16[4,128,512]{2,1,0:T(8,128)(2,1)} %collective-permute-done.2.refs_3_), channel_id=1, source_target_pairs={{0,64},{1,9},{8,72},{9,17},{16,80},{17,25},{24,88},{25,33},{32,96}... | collective-permute-start | bytes 1572872 | tf_op jit(solution)/shard_map/ppermute | solution.py:199
  90.1 9.3 %collective-permute-start.14 = (f32[4,128,512]{2,1,0:T(8,128)S(1)}, f32[4,128,512]{2,1,0:T(8,128)S(1)}, u32[]{:S(2)}, u32[]{:S(2)}) collective-permute-start(f32[4,128,512]{2,1,0:T(8,128)S(1)} %shard_map.79), channel_id=1, source_target_pairs={{0,1},{1,0},{2,3},{3,2},{4,5},{5,4},{6,7},{7,6},{8,9},{9,8},{10,11... | collective-permute-start | bytes 3145736 | tf_op jit(solution)/shard_map/ppermute | solution.py:281
  98.2 5.9 %copy-start.1 = (bf16[128,512]{1,0:T(8,128)(2,1)S(1)}, bf16[128,512]{1,0:T(8,128)(2,1)}, u32[]{:S(2)}) copy-start(bf16[128,512]{1,0:T(8,128)(2,1)} %param.6) | copy-start | bytes 393220
  98.2 5.9 %copy-start.3 = (f32[128]{0:T(128)S(1)}, f32[128]{0:T(128)}, u32[]{:S(2)}) copy-start(f32[128]{0:T(128)} %param.7) | copy-start | bytes 1540
  100.5 18.3 %all-to-all-start.1 = ((f32[4,128,512]{2,1,0:T(8,128)}), f32[4,128,512]{2,1,0:T(8,128)S(1)}, u32[]{:S(2)}, u32[]{:S(2)}) async-start(f32[4,128,512]{2,1,0:T(8,128)} %add.52), calls=%async_computation.1 | async-start | bytes 2097152 | tf_op jit(solution)/shard_map/all_to_all | solution.py:283

commit v10 on v8

--- a/solution.py
+++ b/solution.py
@@ -288,7 +288,8 @@
         [jax.ShapeDtypeStruct((own_rows, kstates), f32), half, half],
         [sm, vm, vm],
     )(k.astype(jnp.int32).reshape(1), parts, local)
-    own = sum_halves(own + lax.ppermute(other, "k", [(0, 1), (1, 0)]))
+    others = lax.all_gather(other, "k", axis=0)
+    own = sum_halves(own + lax.dynamic_index_in_dim(others, 1 - k, 0, keepdims=False))
     gram = lax.all_gather(own, "k", axis=0, tiled=True)
 
     states, upper = call(

time: 197 us -> 195 us (0.990)
  waiting for transfers between devices: 22.8 us -> 18.3 us
  Pallas kernels: 21.2 us -> 25.3 us
  starting transfers between devices: 65.4 us -> 61.9 us
  blocking collectives: 81.7 us -> 83.8 us
    pallas_call x3, Pallas kernels: 5.39 us -> 9.47 us  [products(): call(functools.partial(tile_products, ids, first_place, bool(base)), [jax...]
    ppermute x1 -> x0, starting transfers between devices: 3.42 us -> none  [per_device(): own = sum_halves(own + lax.ppermute(other, 'k', [(0, 1), (1, 0)]))]
    all_gather x0 -> x1, blocking collectives: none -> 3.42 us  [per_device(): others = lax.all_gather(other, 'k', axis=0)]
    ppermute x7, waiting for transfers between devices: 5.25 us -> 2.9 us  [gather_states(): above[at].append(lax.ppermute(above[at][-1], axes, up))]
  transfers between devices with their start and end apart: 17 -> 16, of which waited for: 5 -> 3; matrix products, arithmetic and copies ran while one was open for 0% -> 0% of each run, Pallas kernels for 2% -> 4%
where the time goes in v10:
time: 195 us; the launch traced here: 194 us
  blocking collectives  83.8 us (43%)
  starting transfers between devices  61.9 us (32%)
  Pallas kernels  25.3 us (13%)
  waiting for transfers between devices  18.3 us (9%)
    all_to_all x4, blocking collectives, exchange(): lax.all_to_all(pieces, axes, 0, 0, axis_index_groups=groups, tiled=True)  52.4 us
    ppermute x7, starting transfers between devices, gather_states(): below[at].append(lax.ppermute(below[at][-1], axes, down))  38.1 us
    all_to_all x1, blocking collectives, gather_states(): lax.all_to_all(copies, axes, 0, 0, axis_index_groups=line_places(*sizes),...  25.3 us
    pallas_call x1, Pallas kernels, per_device(): call(factor_and_solve, [jax.ShapeDtypeStruct((own_rows, kstates), f32), j...  15 us
    all_to_all x1, waiting for transfers between devices, per_device(): parts = lax.all_to_all(keep + other, 'x', 0, 0, tiled=True)  14.4 us
    ppermute x7, starting transfers between devices, gather_states(): above[at].append(lax.ppermute(above[at][-1], axes, up))  13.4 us
    pallas_call x3, Pallas kernels, products(): call(functools.partial(tile_products, ids, first_place, bool(base)), [jax...  9.47 us
    ppermute x1, starting transfers between devices, per_device(): other = lax.ppermute(send, 'k', [(0, 1), (1, 0)])  5.36 us
  transfers between devices with their start and end apart: 16, of which 3 were waited for; matrix products, arithmetic and copies ran while one was open for 0% of the time, Pallas kernels for 4%

profile of v10, /device:TPU:1, one launch (start us, length us, event | category | flops | bytes accessed | tf_op | source)
XLA Modules:
  0.0 194.1 jit_solution(15547129621804817026)
XLA Ops:
  0.6 1.0 broadcast_in_dim.8
  1.7 25.3 %all_to_all.35 = bf16[8,128,512]{2,1,0:T(8,128)(2,1)S(1)} all-to-all(bf16[8,128,512]{2,1,0:T(8,128)(2,1)S(1)} %broadcast_in_dim.8), channel_id=1, replica_groups={{0,8,16,24,32,40,48,56},{1,65,129,193,257,321,385,449},{64,72,80,88,96,..., dimensions={0} | all-to-all | bytes 2097152 | tf_op jit(solution)/shard_map/all_to_all | solution.py:191
  27.1 10.7 %collective-permute-start.10 = (bf16[4,128,512]{2,1,0:T(8,128)(2,1)S(1)}, bf16[4,128,512]{2,1,0:T(8,128)(2,1)S(1)}, u32[]{:S(2)}, u32[]{:S(2)}) collective-permute-start(bf16[4,128,512]{2,1,0:T(8,128)(2,1)S(1)} %get-tuple-element.10.refs_6_), channel_id=1, source_target_pairs={{0,448},{1,57},{8,456},{9,1},{16,464},{17,9},{24,472},{25,17},{32,... | collective-permute-start | bytes 1572872 | tf_op jit(solution)/shard_map/ppermute | solution.py:201
  37.7 1.9 collective-permute-start
  39.7 4.6 %collective-permute-start.4 = (bf16[4,128,512]{2,1,0:T(8,128)(2,1)S(1)}, bf16[4,128,512]{2,1,0:T(8,128)(2,1)S(1)}, u32[]{:S(2)}, u32[]{:S(2)}) collective-permute-start(bf16[4,128,512]{2,1,0:T(8,128)(2,1)S(1)} %get-tuple-element.11.refs_0_), channel_id=1, source_target_pairs={{0,448},{1,57},{8,456},{9,1},{16,464},{17,9},{24,472},{25,17},{32,... | collective-permute-start | bytes 1572872 | tf_op jit(solution)/shard_map/ppermute | solution.py:201
  44.3 1.9 collective-permute-start.7
  46.2 4.6 %collective-permute-start.11 = (bf16[4,128,512]{2,1,0:T(8,128)(2,1)S(1)}, bf16[4,128,512]{2,1,0:T(8,128)(2,1)}, u32[]{:S(2)}, u32[]{:S(2)}) collective-permute-start(bf16[4,128,512]{2,1,0:T(8,128)(2,1)S(1)} %collective-permute-done.10.refs_11_), channel_id=1, source_target_pairs={{0,448},{1,57},{8,456},{9,1},{16,464},{17,9},{24,472},{25,17},{32,... | collective-permute-start | bytes 1572872 | tf_op jit(solution)/shard_map/ppermute | solution.py:201
  50.8 1.9 collective-permute-start.1
  52.7 4.6 %collective-permute-start.5 = (bf16[4,128,512]{2,1,0:T(8,128)(2,1)S(1)}, bf16[4,128,512]{2,1,0:T(8,128)(2,1)}, u32[]{:S(2)}, u32[]{:S(2)}) collective-permute-start(bf16[4,128,512]{2,1,0:T(8,128)(2,1)S(1)} %collective-permute-done.4.refs_5_), channel_id=1, source_target_pairs={{0,448},{1,57},{8,456},{9,1},{16,464},{17,9},{24,472},{25,17},{32,... | collective-permute-start | bytes 1572872 | tf_op jit(solution)/shard_map/ppermute | solution.py:201
  57.3 1.9 collective-permute-start.8
  59.3 4.6 %collective-permute-start.12 = (bf16[4,128,512]{2,1,0:T(8,128)(2,1)}, bf16[4,128,512]{2,1,0:T(8,128)(2,1)}, u32[]{:S(2)}, u32[]{:S(2)}) collective-permute-start(bf16[4,128,512]{2,1,0:T(8,128)(2,1)} %collective-permute-done.11.refs_10_), channel_id=1, source_target_pairs={{0,448},{1,57},{8,456},{9,1},{16,464},{17,9},{24,472},{25,17},{32,... | collective-permute-start | bytes 1572872 | tf_op jit(solution)/shard_map/ppermute | solution.py:201
  63.9 1.9 collective-permute-start.2
  66.5 4.6 %collective-permute-start.6 = (bf16[4,128,512]{2,1,0:T(8,128)(2,1)}, bf16[4,128,512]{2,1,0:T(8,128)(2,1)S(1)}, u32[]{:S(2)}, u32[]{:S(2)}) collective-permute-start(bf16[4,128,512]{2,1,0:T(8,128)(2,1)} %collective-permute-done.5.refs_4_), channel_id=1, source_target_pairs={{0,448},{1,57},{8,456},{9,1},{16,464},{17,9},{24,472},{25,17},{32,... | collective-permute-start | bytes 1572872 | tf_op jit(solution)/shard_map/ppermute | solution.py:201
  71.0 1.9 collective-permute-start.9
  73.0 4.6 %collective-permute-start.13 = (bf16[4,128,512]{2,1,0:T(8,128)(2,1)}, bf16[4,128,512]{2,1,0:T(8,128)(2,1)S(1)}, u32[]{:S(2)}, u32[]{:S(2)}) collective-permute-start(bf16[4,128,512]{2,1,0:T(8,128)(2,1)} %collective-permute-done.12.refs_9_), channel_id=1, source_target_pairs={{0,448},{1,57},{8,456},{9,1},{16,464},{17,9},{24,472},{25,17},{32,... | collective-permute-start | bytes 1572872 | tf_op jit(solution)/shard_map/ppermute | solution.py:201
  77.6 1.9 collective-permute-start.3
  79.6 6.6 %shard_map.77.refs_4_ = f32[8,128,512]{2,1,0:T(8,128)S(1)} custom-call(s32[73]{0:T(128)S(1)} %pad_add_fusion.meta_ref, bf16[24,128,128]{2,1,0:T(8,128)(2,1)S(1)} %bitcast.40, bf16[4,128,512]{2,1,0:T(8,128)(2,1)S(1)} %get-tuple-element.11.refs_0_, bf16[4,128,512]{2,1,0:T(8,128)(2,1)S(1)} %collective-permute-done.refs_1_, ...), custom_call_target="tpu_custom_call" | custom-call | tf_op jit(solution)/shard_map/pallas_call | solution.py:270
  86.3 2.9 %collective-permute-done.3.refs_0_ = bf16[4,128,512]{2,1,0:T(8,128)(2,1)S(1)} collective-permute-done((bf16[4,128,512]{2,1,0:T(8,128)(2,1)}, bf16[4,128,512]{2,1,0:T(8,128)(2,1)S(1)}, u32[]{:S(2)}, u32[]{:S(2)}) %collective-permute-start.3) | collective-permute-done | bytes 524320 | tf_op jit(solution)/shard_map/ppermute | solution.py:199
  89.2 1.5 shard_map.79
  90.7 5.4 %collective-permute-start.14 = (f32[4,128,512]{2,1,0:T(8,128)S(1)}, f32[4,128,512]{2,1,0:T(8,128)S(1)}, u32[]{:S(2)}, u32[]{:S(2)}) collective-permute-start(f32[4,128,512]{2,1,0:T(8,128)S(1)} %shard_map.79), channel_id=1, source_target_pairs={{0,1},{1,0},{2,3},{3,2},{4,5},{5,4},{6,7},{7,6},{8,9},{9,8},{10,11... | collective-permute-start | bytes 3145736 | tf_op jit(solution)/shard_map/ppermute | solution.py:280
  96.1 1.3 shard_map.78
  97.5 0.9 collective-permute-done.14
  98.4 1.2 add.52
  99.6 5.0 %all-to-all-start.1 = ((f32[4,128,512]{2,1,0:T(8,128)}), f32[4,128,512]{2,1,0:T(8,128)S(1)}, u32[]{:S(2)}, u32[]{:S(2)}) async-start(f32[4,128,512]{2,1,0:T(8,128)} %add.52), calls=%async_computation.1 | async-start | bytes 2097152 | tf_op jit(solution)/shard_map/all_to_all | solution.py:282
  104.6 14.4 %all-to-all-done.1.parts_ref = f32[4,128,512]{2,1,0:T(8,128)S(1)} async-done(((f32[4,128,512]{2,1,0:T(8,128)}), f32[4,128,512]{2,1,0:T(8,128)S(1)}, u32[]{:S(2)}, u32[]{:S(2)}) %all-to-all-start.1) | async-done | bytes 1048608 | tf_op jit(solution)/shard_map/all_to_all | solution.py:282
  119.8 3.4 %all-gather = f32[10,128,128]{2,1,0:T(8,128)S(1)} all-gather(f32[5,128,128]{2,1,0:T(8,128)S(1)} %get-tuple-element.6), channel_id=2, replica_groups=mesh['y'=8,'z'=8,'x'=4,'k'=2] {'k'}, dimensions={0}, use_global_device_ids=true | all-gather | bytes 983040 | tf_op jit(solution)/shard_map/all_gather | solution.py:291
  123.3 7.8 %all_to_all.36 = f32[4,160,128]{2,1,0:T(8,128)S(1)} all-to-all(f32[4,160,128]{2,1,0:T(8,128)S(1)} %bitcast.44), channel_id=1, replica_groups={{0,2,4,6},{8,10,12,14},{16,18,20,22},{24,26,28,30},{32,34,36,38},{40,42..., dimensions={0} | all-to-all | bytes 655360 | tf_op jit(solution)/shard_map/all_to_all | solution.py:239
  131.2 18.6 %all_to_all.37 = f32[64,1,320]{2,1,0:T(1,128)S(1)} all-to-all(f32[64,1,320]{2,1,0:T(1,128)S(1)} %all_to_all.25), channel_id=1, replica_groups={{0,8,16,24,32,40,48,56,64,72,80,88,96,104,112,120,128,136,144,152,160,1..., dimensions={0} | all-to-all | bytes 163840 | tf_op jit(solution)/shard_map/all_to_all | solution.py:239
  150.0 18.3 %all_to_all.38 = f32[64,1,320]{2,1,0:T(1,128)S(1)} all-to-all(f32[64,1,320]{2,1,0:T(1,128)S(1)} %broadcast_in_dim.9), channel_id=1, replica_groups={{0,8,16,24,32,40,48,56,64,72,80,88,96,104,112,120,128,136,144,152,160,1..., dimensions={0} | all-to-all | bytes 163840 | tf_op jit(solution)/shard_map/all_to_all | solution.py:239
  168.7 7.8 %all_to_all.39 = f32[4,160,128]{2,1,0:T(8,128)S(1)} all-to-all(f32[4,160,128]{2,1,0:T(8,128)S(1)} %broadcast_in_dim.11), channel_id=1, replica_groups={{0,2,4,6},{8,10,12,14},{16,18,20,22},{24,26,28,30},{32,34,36,38},{40,42..., dimensions={0} | all-to-all | bytes 655360 | tf_op jit(solution)/shard_map/all_to_all | solution.py:239
  176.4 2.6 %all_gather.11.gram_ref = f32[10,128,128]{2,1,0:T(8,128)S(1)} all-gather(f32[5,128,128]{2,1,0:T(8,128)S(1)} %bitcast.45), channel_id=1, replica_groups=mesh['y'=8,'z'=8,'x'=4,'k'=2] {'k'}, dimensions={0}, use_global_device_ids=true | all-gather | bytes 983040 | tf_op jit(solution)/shard_map/all_gather | solution.py:293
  179.0 15.0 %shard_map.81 = (f32[128,512]{1,0:T(8,128)}, f32[512,512]{1,0:T(8,128)}) custom-call(f32[10,128,128]{2,1,0:T(8,128)S(1)} %all_gather.11.gram_ref, f32[128,512]{1,0:T(8,128)S(1)} %get-tuple-element.7.applied_ref), custom_call_target="tpu_custom_call" | custom-call | tf_op jit(solution)/shard_map/pallas_call | solution.py:295
  (37 shorter events, 1.8 us)
Async XLA Ops:
  1.6 77.9 %copy-start.2 = (s32[1,1,24]{2,1,0:T(1,128)S(1)}, s32[1,1,24]{2,1,0:T(1,128)}, u32[]{:S(2)}) copy-start(s32[1,1,24]{2,1,0:T(1,128)} %param.10) | copy-start | bytes 292
  1.6 77.9 %copy-start.4 = (s32[1,1,24]{2,1,0:T(1,128)S(1)}, s32[1,1,24]{2,1,0:T(1,128)}, u32[]{:S(2)}) copy-start(s32[1,1,24]{2,1,0:T(1,128)} %param.9) | copy-start | bytes 292
  1.6 78.0 %copy-start = (bf16[1,1,24,128,128]{4,3,2,1,0:T(8,128)(2,1)S(1)}, bf16[1,1,24,128,128]{4,3,2,1,0:T(8,128)(2,1)}, u32[]{:S(2)}) copy-start(bf16[1,1,24,128,128]{4,3,2,1,0:T(8,128)(2,1)} %param.8) | copy-start | bytes 2359300
  27.1 19.1 %collective-permute-start.10 = (bf16[4,128,512]{2,1,0:T(8,128)(2,1)S(1)}, bf16[4,128,512]{2,1,0:T(8,128)(2,1)S(1)}, u32[]{:S(2)}, u32[]{:S(2)}) collective-permute-start(bf16[4,128,512]{2,1,0:T(8,128)(2,1)S(1)} %get-tuple-element.10.refs_6_), channel_id=1, source_target_pairs={{0,448},{1,57},{8,456},{9,1},{16,464},{17,9},{24,472},{25,17},{32,... | collective-permute-start | bytes 1572872 | tf_op jit(solution)/shard_map/ppermute | solution.py:201
  37.7 13.0 %collective-permute-start = (bf16[4,128,512]{2,1,0:T(8,128)(2,1)S(1)}, bf16[4,128,512]{2,1,0:T(8,128)(2,1)S(1)}, u32[]{:S(2)}, u32[]{:S(2)}) collective-permute-start(bf16[4,128,512]{2,1,0:T(8,128)(2,1)S(1)} %get-tuple-element.11.refs_0_), channel_id=1, source_target_pairs={{0,64},{1,9},{8,72},{9,17},{16,80},{17,25},{24,88},{25,33},{32,96}... | collective-permute-start | bytes 1572872 | tf_op jit(solution)/shard_map/ppermute | solution.py:199
  39.7 13.0 %collective-permute-start.4 = (bf16[4,128,512]{2,1,0:T(8,128)(2,1)S(1)}, bf16[4,128,512]{2,1,0:T(8,128)(2,1)S(1)}, u32[]{:S(2)}, u32[]{:S(2)}) collective-permute-start(bf16[4,128,512]{2,1,0:T(8,128)(2,1)S(1)} %get-tuple-element.11.refs_0_), channel_id=1, source_target_pairs={{0,448},{1,57},{8,456},{9,1},{16,464},{17,9},{24,472},{25,17},{32,... | collective-permute-start | bytes 1572872 | tf_op jit(solution)/shard_map/ppermute | solution.py:201
  44.3 13.1 %collective-permute-start.7 = (bf16[4,128,512]{2,1,0:T(8,128)(2,1)S(1)}, bf16[4,128,512]{2,1,0:T(8,128)(2,1)}, u32[]{:S(2)}, u32[]{:S(2)}) collective-permute-start(bf16[4,128,512]{2,1,0:T(8,128)(2,1)S(1)} %get-tuple-element.10.refs_6_), channel_id=1, source_target_pairs={{0,64},{1,9},{8,72},{9,17},{16,80},{17,25},{24,88},{25,33},{32,96}... | collective-permute-start | bytes 1572872 | tf_op jit(solution)/shard_map/ppermute | solution.py:199
  46.2 13.1 %collective-permute-start.11 = (bf16[4,128,512]{2,1,0:T(8,128)(2,1)S(1)}, bf16[4,128,512]{2,1,0:T(8,128)(2,1)}, u32[]{:S(2)}, u32[]{:S(2)}) collective-permute-start(bf16[4,128,512]{2,1,0:T(8,128)(2,1)S(1)} %collective-permute-done.10.refs_11_), channel_id=1, source_target_pairs={{0,448},{1,57},{8,456},{9,1},{16,464},{17,9},{24,472},{25,17},{32,... | collective-permute-start | bytes 1572872 | tf_op jit(solution)/shard_map/ppermute | solution.py:201
  50.8 13.1 %collective-permute-start.1 = (bf16[4,128,512]{2,1,0:T(8,128)(2,1)S(1)}, bf16[4,128,512]{2,1,0:T(8,128)(2,1)}, u32[]{:S(2)}, u32[]{:S(2)}) collective-permute-start(bf16[4,128,512]{2,1,0:T(8,128)(2,1)S(1)} %collective-permute-done.refs_1_), channel_id=1, source_target_pairs={{0,64},{1,9},{8,72},{9,17},{16,80},{17,25},{24,88},{25,33},{32,96}... | collective-permute-start | bytes 1572872 | tf_op jit(solution)/shard_map/ppermute | solution.py:199
  52.7 13.7 %collective-permute-start.5 = (bf16[4,128,512]{2,1,0:T(8,128)(2,1)S(1)}, bf16[4,128,512]{2,1,0:T(8,128)(2,1)}, u32[]{:S(2)}, u32[]{:S(2)}) collective-permute-start(bf16[4,128,512]{2,1,0:T(8,128)(2,1)S(1)} %collective-permute-done.4.refs_5_), channel_id=1, source_target_pairs={{0,448},{1,57},{8,456},{9,1},{16,464},{17,9},{24,472},{25,17},{32,... | collective-permute-start | bytes 1572872 | tf_op jit(solution)/shard_map/ppermute | solution.py:201
  57.3 13.7 %collective-permute-start.8 = (bf16[4,128,512]{2,1,0:T(8,128)(2,1)}, bf16[4,128,512]{2,1,0:T(8,128)(2,1)}, u32[]{:S(2)}, u32[]{:S(2)}) collective-permute-start(bf16[4,128,512]{2,1,0:T(8,128)(2,1)} %collective-permute-done.7.refs_7_), channel_id=1, source_target_pairs={{0,64},{1,9},{8,72},{9,17},{16,80},{17,25},{24,88},{25,33},{32,96}... | collective-permute-start | bytes 1572872 | tf_op jit(solution)/shard_map/ppermute | solution.py:199
  59.3 13.7 %collective-permute-start.12 = (bf16[4,128,512]{2,1,0:T(8,128)(2,1)}, bf16[4,128,512]{2,1,0:T(8,128)(2,1)}, u32[]{:S(2)}, u32[]{:S(2)}) collective-permute-start(bf16[4,128,512]{2,1,0:T(8,128)(2,1)} %collective-permute-done.11.refs_10_), channel_id=1, source_target_pairs={{0,448},{1,57},{8,456},{9,1},{16,464},{17,9},{24,472},{25,17},{32,... | collective-permute-start | bytes 1572872 | tf_op jit(solution)/shard_map/ppermute | solution.py:201
  63.9 13.7 %collective-permute-start.2 = (bf16[4,128,512]{2,1,0:T(8,128)(2,1)}, bf16[4,128,512]{2,1,0:T(8,128)(2,1)}, u32[]{:S(2)}, u32[]{:S(2)}) collective-permute-start(bf16[4,128,512]{2,1,0:T(8,128)(2,1)} %collective-permute-done.1.refs_2_), channel_id=1, source_target_pairs={{0,64},{1,9},{8,72},{9,17},{16,80},{17,25},{24,88},{25,33},{32,96}... | collective-permute-start | bytes 1572872 | tf_op jit(solution)/shard_map/ppermute | solution.py:199
  66.5 19.8 %collective-permute-start.6 = (bf16[4,128,512]{2,1,0:T(8,128)(2,1)}, bf16[4,128,512]{2,1,0:T(8,128)(2,1)S(1)}, u32[]{:S(2)}, u32[]{:S(2)}) collective-permute-start(bf16[4,128,512]{2,1,0:T(8,128)(2,1)} %collective-permute-done.5.refs_4_), channel_id=1, source_target_pairs={{0,448},{1,57},{8,456},{9,1},{16,464},{17,9},{24,472},{25,17},{32,... | collective-permute-start | bytes 1572872 | tf_op jit(solution)/shard_map/ppermute | solution.py:201
  71.0 15.3 %collective-permute-start.9 = (bf16[4,128,512]{2,1,0:T(8,128)(2,1)}, bf16[4,128,512]{2,1,0:T(8,128)(2,1)S(1)}, u32[]{:S(2)}, u32[]{:S(2)}) collective-permute-start(bf16[4,128,512]{2,1,0:T(8,128)(2,1)} %collective-permute-done.8.refs_8_), channel_id=1, source_target_pairs={{0,64},{1,9},{8,72},{9,17},{16,80},{17,25},{24,88},{25,33},{32,96}... | collective-permute-start | bytes 1572872 | tf_op jit(solution)/shard_map/ppermute | solution.py:199
  73.0 13.3 %collective-permute-start.13 = (bf16[4,128,512]{2,1,0:T(8,128)(2,1)}, bf16[4,128,512]{2,1,0:T(8,128)(2,1)S(1)}, u32[]{:S(2)}, u32[]{:S(2)}) collective-permute-start(bf16[4,128,512]{2,1,0:T(8,128)(2,1)} %collective-permute-done.12.refs_9_), channel_id=1, source_target_pairs={{0,448},{1,57},{8,456},{9,1},{16,464},{17,9},{24,472},{25,17},{32,... | collective-permute-start | bytes 1572872 | tf_op jit(solution)/shard_map/ppermute | solution.py:201
  77.6 11.6 %collective-permute-start.3 = (bf16[4,128,512]{2,1,0:T(8,128)(2,1)}, bf16[4,128,512]{2,1,0:T(8,128)(2,1)S(1)}, u32[]{:S(2)}, u32[]{:S(2)}) collective-permute-start(bf16[4,128,512]{2,1,0:T(8,128)(2,1)} %collective-permute-done.2.refs_3_), channel_id=1, source_target_pairs={{0,64},{1,9},{8,72},{9,17},{16,80},{17,25},{24,88},{25,33},{32,96}... | collective-permute-start | bytes 1572872 | tf_op jit(solution)/shard_map/ppermute | solution.py:199
  90.7 7.6 %collective-permute-start.14 = (f32[4,128,512]{2,1,0:T(8,128)S(1)}, f32[4,128,512]{2,1,0:T(8,128)S(1)}, u32[]{:S(2)}, u32[]{:S(2)}) collective-permute-start(f32[4,128,512]{2,1,0:T(8,128)S(1)} %shard_map.79), channel_id=1, source_target_pairs={{0,1},{1,0},{2,3},{3,2},{4,5},{5,4},{6,7},{7,6},{8,9},{9,8},{10,11... | collective-permute-start | bytes 3145736 | tf_op jit(solution)/shard_map/ppermute | solution.py:280
  97.4 7.1 %copy-start.1 = (bf16[128,512]{1,0:T(8,128)(2,1)S(1)}, bf16[128,512]{1,0:T(8,128)(2,1)}, u32[]{:S(2)}) copy-start(bf16[128,512]{1,0:T(8,128)(2,1)} %param.6) | copy-start | bytes 393220
  97.4 7.1 %copy-start.3 = (f32[128]{0:T(128)S(1)}, f32[128]{0:T(128)}, u32[]{:S(2)}) copy-start(f32[128]{0:T(128)} %param.7) | copy-start | bytes 1540
  99.6 19.5 %all-to-all-start.1 = ((f32[4,128,512]{2,1,0:T(8,128)}), f32[4,128,512]{2,1,0:T(8,128)S(1)}, u32[]{:S(2)}, u32[]{:S(2)}) async-start(f32[4,128,512]{2,1,0:T(8,128)} %add.52), calls=%async_computation.1 | async-start | bytes 2097152 | tf_op jit(solution)/shard_map/all_to_all | solution.py:282
